TPU v7x, 32 devices: a whole 2x2x4 slice. The times are simulated.
32 devices in a mesh: ctx: 4 (over z), fsdp: 8 (over y, x, core).
Axes of the slice: x: 2, y: 2, z: 4, core: 2. Of those that a mesh axis runs over, the one named last changes fastest.
Arguments:
- tokens: bfloat16 [8, 1024, 2048], P('fsdp', 'ctx'), may hold values from -6 to 6
- segments: int32 [8, 1024], P('fsdp'), may hold values from 0 to 1, as said below
- query_weight: bfloat16 [2048, 2048], P('fsdp'), may hold values from -0.125 to 0.125
- pair_weight: bfloat16 [2048, 256], P('fsdp'), may hold values from -0.125 to 0.125
- out_weight: bfloat16 [2048, 2048], P('fsdp'), may hold values from -2 to 2
- query_bias: bfloat16 [2048], P('fsdp'), may hold values from -1.5 to 1.5
- value_bias: bfloat16 [128], P('fsdp'), may hold values from -1.5 to 1.5
- out_bias: bfloat16 [2048], P('fsdp'), may hold values from -1.5 to 1.5
- norm1_gain: bfloat16 [2048], P('fsdp'), may hold values from 0.25 to 1.75
- norm1_bias: bfloat16 [2048], P('fsdp'), may hold values from -1.5 to 1.5
- fc_weight: bfloat16 [2048, 8192], P('fsdp'), may hold values from -0.125 to 0.125
- proj_weight: bfloat16 [8192, 2048], P('fsdp'), may hold values from -0.125 to 0.125
- fc_bias: bfloat16 [8192], P('fsdp'), may hold values from -1.5 to 1.5
- proj_bias: bfloat16 [2048], P('fsdp'), may hold values from -1.5 to 1.5
- norm2_gain: bfloat16 [2048], P('fsdp'), may hold values from 0.25 to 1.75
- norm2_bias: bfloat16 [2048], P('fsdp'), may hold values from -1.5 to 1.5
- cotangent: bfloat16 [8, 1024, 2048], P('fsdp', 'ctx'), may hold values from -6 to 6
Outputs:
- output: bfloat16 [8, 1024, 2048], P('fsdp', 'ctx')
- grad_tokens: bfloat16 [8, 1024, 2048], P('fsdp', 'ctx')
- grad_query_weight: float32 [2048, 2048], P('fsdp')
- grad_pair_weight: float32 [2048, 256], P('fsdp')
- grad_out_weight: float32 [2048, 2048], P('fsdp')
- grad_query_bias: float32 [2048], P('fsdp')
- grad_value_bias: float32 [128], P('fsdp')
- grad_out_bias: float32 [2048], P('fsdp')
- grad_norm1_gain: float32 [2048], P('fsdp')
- grad_norm1_bias: float32 [2048], P('fsdp')
- grad_fc_weight: float32 [2048, 8192], P('fsdp')
- grad_proj_weight: float32 [8192, 2048], P('fsdp')
- grad_fc_bias: float32 [8192], P('fsdp')
- grad_proj_bias: float32 [2048], P('fsdp')
- grad_norm2_gain: float32 [2048], P('fsdp')
- grad_norm2_bias: float32 [2048], P('fsdp')
Inputs may be any that keep to these rules, and one draw needn't show every extreme that they name: `segments`: each row holds two documents numbered 0 and 1 in order of position; the first or the last of them has 1 to 255 tokens, which one is drawn per row.
All inputs are finite; a program needn't handle non-finite values.
Results may differ from a plain program's by a relative error of at most 0.019.
Values may be sent and summed in bfloat16 or wider, within the bound.
No kernel may reach another device: no remote copies, remote signals or barrier semaphores. Data moves between devices by JAX's collectives and lax.ppermute only.
A program may use at most 512 MiB of HBM per device.

v0:
```python
import math

import jax
import jax.numpy as jnp
from jax import lax
from jax.sharding import PartitionSpec as P

H = 16
HD = 128
WINDOW = 1024


EPSILON = 1e-05
NEGATIVE = -1e30


def from_behind(array, axis, by):
    peers = lax.axis_size(axis)
    pairs = [(i, i + by) for i in range(peers) if 0 <= i + by < peers]
    return lax.ppermute(array, axis, pairs)


def shifted(array, axis, by):
    peers = lax.axis_size(axis)
    return lax.ppermute(array, axis, [(i, (i + by) % peers) for i in range(peers)])


def normalize(values_in):
    center = values_in - jnp.mean(values_in, axis=-1, keepdims=True)
    spread = jnp.mean(center * center, axis=-1, keepdims=True)
    return center * lax.rsqrt(spread + EPSILON)


def gelu_tanh(values_in):
    return jax.nn.gelu(values_in, approximate=True)


def product(left_side, right_side):
    return jnp.dot(left_side, right_side, preferred_element_type=jnp.float32)


def product_tn(left_side, right_side):
    return lax.dot_general(
        left_side, right_side, (((0,), (0,)), ((), ())), preferred_element_type=jnp.float32
    )


def product_nt(left_side, right_side):
    return lax.dot_general(
        left_side, right_side, (((1,), (1,)), ((), ())), preferred_element_type=jnp.float32
    )


def norm_pullback(values_in, gain_vec, grad_in):

    def scaled(inner_rows, inner_gain):
        return normalize(inner_rows) * inner_gain

    unused_out, pull_fn = jax.vjp(scaled, values_in, gain_vec)
    grad_values, grad_gain = pull_fn(grad_in)
    return (grad_values, grad_gain, jnp.sum(grad_in, axis=0))


def window_mask(seg_row, query_first, key_first, tok_count, source_ok):
    query_pos = query_first + jnp.arange(tok_count, dtype=jnp.int32)
    key_pos = key_first + jnp.arange(tok_count, dtype=jnp.int32)
    query_seg = lax.dynamic_slice_in_dim(seg_row, query_first, tok_count, 0)
    key_seg = lax.dynamic_slice_in_dim(seg_row, key_first, tok_count, 0)
    allowed = (query_seg[:, None] == key_seg[None, :]) & (key_pos[None, :] <= query_pos[:, None])
    return allowed & (query_pos[:, None] - key_pos[None, :] < WINDOW) & source_ok


def block_scores(queries, current, allowed):
    scaling = 1.0 / math.sqrt(HD)
    scores = scaling * jnp.einsum(
        "thd,kd->thk", queries, current[:, :HD], preferred_element_type=jnp.float32
    )
    return jnp.where(allowed[:, None, :], scores, NEGATIVE)


def absorb(carry_state, queries, current, allowed):
    running_max, running_sum, accumulated = carry_state
    scores = block_scores(queries, current, allowed)
    new_max = jnp.maximum(running_max, jnp.max(scores, axis=-1))
    weights = jnp.where(allowed[:, None, :], jnp.exp(scores - new_max[:, :, None]), 0.0)
    factor = jnp.exp(running_max - new_max)
    running_sum = running_sum * factor + jnp.sum(weights, axis=-1)
    accumulated = accumulated * factor[:, :, None] + jnp.einsum(
        "thk,kd->thd",
        weights.astype(jnp.bfloat16),
        current[:, HD:],
        preferred_element_type=jnp.float32,
    )
    return (new_max, running_sum, accumulated)


def block_pullback(queries, current, allowed, log_total, grad_attended, delta_rows):
    scores = block_scores(queries, current, allowed)
    probabilities = jnp.where(allowed[:, None, :], jnp.exp(scores - log_total[:, :, None]), 0.0)
    grad_probs = jnp.einsum(
        "thd,kd->thk", grad_attended, current[:, HD:], preferred_element_type=jnp.float32
    )
    grad_scores = (probabilities * (grad_probs - delta_rows[:, :, None])).astype(jnp.bfloat16)
    query_part = jnp.einsum(
        "thk,kd->thd", grad_scores, current[:, :HD], preferred_element_type=jnp.float32
    )
    key_part = jnp.einsum("thk,thd->kd", grad_scores, queries, preferred_element_type=jnp.float32)
    value_part = jnp.einsum(
        "thk,thd->kd",
        probabilities.astype(jnp.bfloat16),
        grad_attended,
        preferred_element_type=jnp.float32,
    )
    return (query_part, jnp.concatenate([key_part, value_part], axis=1))


def per_device(
    tokens,
    segments,
    query_weight,
    pair_weight,
    out_weight,
    query_bias,
    value_bias,
    out_bias,
    norm1_gain,
    norm1_bias,
    fc_weight,
    proj_weight,
    fc_bias,
    proj_bias,
    norm2_gain,
    norm2_bias,
    cotangent,
):
    tok_count = tokens.shape[1]
    width = tokens.shape[2]
    ctx_count = lax.axis_size("ctx")
    ctx_index = lax.axis_index("ctx")
    seg_row = segments[0]
    tok_rows = tokens[0].astype(jnp.float32)
    query_first = ctx_index * tok_count
    scaling = 1.0 / math.sqrt(HD)
    cycle_depth = ctx_count - 1
    attn_full = (
        lax.all_gather(query_weight, "fsdp", axis=0, tiled=True),
        lax.all_gather(pair_weight, "fsdp", axis=0, tiled=True),
        lax.all_gather(out_weight, "fsdp", axis=0, tiled=True),
        lax.all_gather(query_bias, "fsdp", axis=0, tiled=True),
        lax.all_gather(value_bias, "fsdp", axis=0, tiled=True),
        lax.all_gather(out_bias, "fsdp", axis=0, tiled=True),
        lax.all_gather(norm1_gain, "fsdp", axis=0, tiled=True),
        lax.all_gather(norm1_bias, "fsdp", axis=0, tiled=True),
    )
    (
        query_all,
        pair_all,
        out_all,
        query_bias_all,
        value_bias_all,
        out_bias_all,
        gain1_all,
        bias1_all,
    ) = attn_full
    normed_in = (
        normalize(tok_rows) * gain1_all.astype(jnp.float32) + bias1_all.astype(jnp.float32)
    ).astype(jnp.bfloat16)
    queries = (product(normed_in, query_all) + query_bias_all.astype(jnp.float32)).astype(
        jnp.bfloat16
    )
    queries = queries.reshape(tok_count, H, HD)
    pair_bias = jnp.concatenate([jnp.zeros((HD,), jnp.float32), value_bias_all.astype(jnp.float32)])
    key_pair = (product(normed_in, pair_all) + pair_bias).astype(jnp.bfloat16)
    moving = key_pair
    kept_pairs = []
    carry_state = (
        jnp.full((tok_count, H), NEGATIVE, jnp.float32),
        jnp.zeros((tok_count, H), jnp.float32),
        jnp.zeros((tok_count, H, HD), jnp.float32),
    )
    for cycle_step in range(cycle_depth + 1):
        source = ctx_index - cycle_step
        key_first = jnp.maximum(source, 0) * tok_count
        if cycle_step > 0:
            moving = from_behind(moving, "ctx", 1)
        kept_pairs.append(moving)
        allowed = window_mask(seg_row, query_first, key_first, tok_count, source >= 0)
        carry_state = absorb(carry_state, queries, moving, allowed)
    running_max, running_sum, accumulated = carry_state
    attended = accumulated / running_sum[:, :, None]
    log_total = running_max + jnp.log(running_sum)
    attended_low = attended.reshape(tok_count, width).astype(jnp.bfloat16)
    middle = tok_rows + (product(attended_low, out_all) + out_bias_all.astype(jnp.float32))
    mlp_full = (
        lax.all_gather(fc_weight, "fsdp", axis=0, tiled=True),
        lax.all_gather(proj_weight, "fsdp", axis=0, tiled=True),
        lax.all_gather(fc_bias, "fsdp", axis=0, tiled=True),
        lax.all_gather(proj_bias, "fsdp", axis=0, tiled=True),
        lax.all_gather(norm2_gain, "fsdp", axis=0, tiled=True),
        lax.all_gather(norm2_bias, "fsdp", axis=0, tiled=True),
    )
    fc_all, proj_all, fc_bias_all, proj_bias_all, gain2_all, bias2_all = mlp_full
    normed_mid = (
        normalize(middle) * gain2_all.astype(jnp.float32) + bias2_all.astype(jnp.float32)
    ).astype(jnp.bfloat16)
    hidden_pre = product(normed_mid, fc_all) + fc_bias_all.astype(jnp.float32)
    hidden_act, gelu_pull = jax.vjp(gelu_tanh, hidden_pre)
    hidden_low = hidden_act.astype(jnp.bfloat16)
    output = (middle + (product(hidden_low, proj_all) + proj_bias_all.astype(jnp.float32))).astype(
        jnp.bfloat16
    )
    fc_back, proj_back, gain2_back = (
        lax.all_gather(fc_weight, "fsdp", axis=0, tiled=True),
        lax.all_gather(proj_weight, "fsdp", axis=0, tiled=True),
        lax.all_gather(norm2_gain, "fsdp", axis=0, tiled=True),
    )
    out_grad = cotangent[0]
    grad_act = product_nt(out_grad, proj_back)
    grad_pre = gelu_pull(grad_act)[0].astype(jnp.bfloat16)
    grad_normed_mid = product_nt(grad_pre, fc_back)
    grad_middle_ln, grad_gain2, grad_bias2 = norm_pullback(
        middle, gain2_back.astype(jnp.float32), grad_normed_mid
    )
    grad_middle = out_grad.astype(jnp.float32) + grad_middle_ln
    grad_mid_low = grad_middle.astype(jnp.bfloat16)
    query_back, pair_back, out_back, gain1_back = (
        lax.all_gather(query_weight, "fsdp", axis=0, tiled=True),
        lax.all_gather(pair_weight, "fsdp", axis=0, tiled=True),
        lax.all_gather(out_weight, "fsdp", axis=0, tiled=True),
        lax.all_gather(norm1_gain, "fsdp", axis=0, tiled=True),
    )
    grad_attended = (
        product_nt(grad_mid_low, out_back).astype(jnp.bfloat16).reshape(tok_count, H, HD)
    )
    delta_rows = jnp.sum(grad_attended.astype(jnp.float32) * attended, axis=-1)
    grad_queries = jnp.zeros((tok_count, H, HD), jnp.float32)
    carried = jnp.zeros((tok_count, 2 * HD), jnp.float32)
    for cycle_step in range(cycle_depth + 1):
        source = ctx_index - cycle_step
        key_first = jnp.maximum(source, 0) * tok_count
        allowed = window_mask(seg_row, query_first, key_first, tok_count, source >= 0)
        query_part, pair_part = block_pullback(
            queries, kept_pairs[cycle_step], allowed, log_total, grad_attended, delta_rows
        )
        grad_queries = grad_queries + query_part
        if cycle_step > 0:
            carried = shifted(carried.astype(jnp.bfloat16), "ctx", 1).astype(carried.dtype)
        carried = carried + pair_part
    grad_pair_sum = shifted(carried.astype(jnp.bfloat16), "ctx", -cycle_depth).astype(carried.dtype)
    pair_scaling = jnp.concatenate(
        [jnp.full((HD,), scaling, jnp.float32), jnp.ones((HD,), jnp.float32)]
    )
    grad_pair_low = (grad_pair_sum * pair_scaling).astype(jnp.bfloat16)
    grad_query_low = (scaling * grad_queries).reshape(tok_count, width).astype(jnp.bfloat16)
    grad_normed_in = product_nt(grad_query_low, query_back) + product_nt(grad_pair_low, pair_back)
    grad_tok_ln, grad_gain1, grad_bias1 = norm_pullback(
        tok_rows, gain1_back.astype(jnp.float32), grad_normed_in
    )
    grad_tokens = (grad_middle + grad_tok_ln).astype(jnp.bfloat16)
    query_term = product_tn(normed_in, grad_query_low)
    pair_term = product_tn(normed_in, grad_pair_low)
    out_term = product_tn(attended_low, grad_mid_low)
    shares = (
        lax.psum_scatter(
            query_term.astype(jnp.bfloat16), "fsdp", scatter_dimension=0, tiled=True
        ).astype(jnp.float32),
        lax.psum_scatter(
            pair_term.astype(jnp.bfloat16), "fsdp", scatter_dimension=0, tiled=True
        ).astype(jnp.float32),
        lax.psum_scatter(
            out_term.astype(jnp.bfloat16), "fsdp", scatter_dimension=0, tiled=True
        ).astype(jnp.float32),
        lax.psum_scatter(
            jnp.sum(grad_query_low.astype(jnp.float32), axis=0).astype(jnp.bfloat16),
            "fsdp",
            scatter_dimension=0,
            tiled=True,
        ).astype(jnp.float32),
        lax.psum_scatter(
            jnp.sum(grad_pair_low[:, HD:].astype(jnp.float32), axis=0).astype(jnp.bfloat16),
            "fsdp",
            scatter_dimension=0,
            tiled=True,
        ).astype(jnp.float32),
        lax.psum_scatter(
            jnp.sum(grad_mid_low.astype(jnp.float32), axis=0).astype(jnp.bfloat16),
            "fsdp",
            scatter_dimension=0,
            tiled=True,
        ).astype(jnp.float32),
        lax.psum_scatter(
            grad_gain1.astype(jnp.bfloat16), "fsdp", scatter_dimension=0, tiled=True
        ).astype(jnp.float32),
        lax.psum_scatter(
            grad_bias1.astype(jnp.bfloat16), "fsdp", scatter_dimension=0, tiled=True
        ).astype(jnp.float32),
        lax.psum_scatter(
            jnp.sum(grad_pre.astype(jnp.float32), axis=0).astype(jnp.bfloat16),
            "fsdp",
            scatter_dimension=0,
            tiled=True,
        ).astype(jnp.float32),
        lax.psum_scatter(
            jnp.sum(out_grad.astype(jnp.float32), axis=0).astype(jnp.bfloat16),
            "fsdp",
            scatter_dimension=0,
            tiled=True,
        ).astype(jnp.float32),
        lax.psum_scatter(
            grad_gain2.astype(jnp.bfloat16), "fsdp", scatter_dimension=0, tiled=True
        ).astype(jnp.float32),
        lax.psum_scatter(
            grad_bias2.astype(jnp.bfloat16), "fsdp", scatter_dimension=0, tiled=True
        ).astype(jnp.float32),
    )
    fc_share = lax.psum_scatter(
        product_tn(normed_mid, grad_pre).astype(jnp.bfloat16),
        "fsdp",
        scatter_dimension=0,
        tiled=True,
    )
    proj_share = lax.psum_scatter(
        product_tn(hidden_low, out_grad).astype(jnp.bfloat16),
        "fsdp",
        scatter_dimension=0,
        tiled=True,
    )
    totals = (
        lax.psum(shares[0].astype(jnp.bfloat16), "ctx").astype(jnp.float32),
        lax.psum(shares[1].astype(jnp.bfloat16), "ctx").astype(jnp.float32),
        lax.psum(shares[2].astype(jnp.bfloat16), "ctx").astype(jnp.float32),
        lax.psum(shares[3].astype(jnp.bfloat16), "ctx").astype(jnp.float32),
        lax.psum(shares[4].astype(jnp.bfloat16), "ctx").astype(jnp.float32),
        lax.psum(shares[5].astype(jnp.bfloat16), "ctx").astype(jnp.float32),
        lax.psum(shares[6].astype(jnp.bfloat16), "ctx").astype(jnp.float32),
        lax.psum(shares[7].astype(jnp.bfloat16), "ctx").astype(jnp.float32),
        lax.psum(fc_share, "ctx").astype(jnp.float32),
        lax.psum(proj_share, "ctx").astype(jnp.float32),
        lax.psum(shares[8].astype(jnp.bfloat16), "ctx").astype(jnp.float32),
        lax.psum(shares[9].astype(jnp.bfloat16), "ctx").astype(jnp.float32),
        lax.psum(shares[10].astype(jnp.bfloat16), "ctx").astype(jnp.float32),
        lax.psum(shares[11].astype(jnp.bfloat16), "ctx").astype(jnp.float32),
    )
    return (
        output[None],
        grad_tokens[None],
        totals[0],
        totals[1],
        totals[2],
        totals[3],
        totals[4],
        totals[5],
        totals[6],
        totals[7],
        totals[8],
        totals[9],
        totals[10],
        totals[11],
        totals[12],
        totals[13],
    )


def solution(mesh):
    return jax.shard_map(
        per_device,
        mesh=mesh,
        in_specs=(
            P("fsdp", "ctx", None),
            P("fsdp", None),
            P("fsdp", None),
            P("fsdp", None),
            P("fsdp", None),
            P("fsdp"),
            P("fsdp"),
            P("fsdp"),
            P("fsdp"),
            P("fsdp"),
            P("fsdp", None),
            P("fsdp", None),
            P("fsdp"),
            P("fsdp"),
            P("fsdp"),
            P("fsdp"),
            P("fsdp", "ctx", None),
        ),
        out_specs=(
            P("fsdp", "ctx", None),
            P("fsdp", "ctx", None),
            P("fsdp", None),
            P("fsdp", None),
            P("fsdp", None),
            P("fsdp"),
            P("fsdp"),
            P("fsdp"),
            P("fsdp"),
            P("fsdp"),
            P("fsdp", None),
            P("fsdp", None),
            P("fsdp"),
            P("fsdp"),
            P("fsdp"),
            P("fsdp"),
        ),
        check_vma=False,
    )
```

profile of v0, /device:TPU:0, one launch (start us, length us, event | category | flops | bytes accessed | tf_op | source)
XLA Modules:
  0.0 1566.1 jit_solution(13520287328131510487)
XLA Ops:
  10.8 10.3 all-gather.1
  21.2 8.9 all-gather
  31.6 13.2 all-reduce.1
  51.0 7.9 all-gather.3
  59.0 8.9 all-gather.2
  67.9 7.9 all_gather.60
  75.8 8.9 all-gather.5
  84.8 7.9 all-gather.4
  104.6 5.8 fusion.26
  129.6 19.3 %all-gather.17.cloned.1.call-done = bf16[2048,2048]{1,0:T(8,128)(2,1)} async-done(((bf16[256,2048]{1,0:T(8,128)(2,1)}), bf16[2048,2048]{1,0:T(8,128)(2,1)}) %all-gather.17.cloned.1.call-update) | async-done | bytes 8388624 | tf_op jit(solution)/shard_map/all_gather | solution.py:148
  148.9 5.8 fusion.173
  156.4 155.0 %all-gather.19.cloned.1.call-done = bf16[2048,8192]{1,0:T(8,128)(2,1)} async-done(((bf16[256,8192]{1,0:T(8,128)(2,1)}), bf16[2048,8192]{1,0:T(8,128)(2,1)}) %all-gather.19.cloned.1.call-update) | async-done | bytes 33554448 | tf_op jit(solution)/shard_map/all_gather | solution.py:195
  311.5 21.5 %convolution_add_fusion = f32[256,8192]{1,0:T(8,128)} fusion(bf16[2048,8192]{1,0:T(8,128)(2,1)} %all-gather.19.cloned.1.call-done, f32[8192]{0:T(1024)S(1)} %convert_element_type.271, f32[256,2048]{1,0:T(8,128)} %copy-done.1, f32[2048]{0:T(1024)S(1)} %bitcast.221, f32[2048]{0:T(1024)S(1)} %bitcast.210, f32[256]{0:T(256)S(1)} %fusion.135, ...), kind=kOutput, calls=%fused_computation.4 | convolution fusion | flops 8594653184 | bytes 44091392 | tf_op jit(solution)/shard_map/dot_general | solution.py:39
  333.0 141.0 %all-gather.21.cloned.1.call-done = bf16[8192,2048]{1,0:T(8,128)(2,1)} async-done(((bf16[1024,2048]{1,0:T(8,128)(2,1)}), bf16[8192,2048]{1,0:T(8,128)(2,1)}) %all-gather.21.cloned.1.call-update) | async-done | bytes 33554448 | tf_op jit(solution)/shard_map/all_gather | solution.py:196
  474.0 21.9 %fusion.175 = (bf16[8192]{0:T(1024)(128)(2,1)}, bf16[256,8192]{1,0:T(8,128)(2,1)}) fusion(f32[256,8192]{1,0:T(8,128)} %convolution_add_fusion, bf16[8192,2048]{1,0:T(8,128)(2,1)} %all-gather.21.cloned.1.call-done, bf16[1,256,2048]{2,1,0:T(8,128)(2,1)S(1)} %copy-done.14), kind=kOutput, calls=%fused_computation.240 | convolution fusion | flops 8633966592 | bytes 47202304 | tf_op jit(solution)/shard_map/dot_general | solution.py:49
  495.9 18.0 %multiply_reduce_fusion = (bf16[2048]{0:T(1024)(128)(2,1)S(1)}, f32[256]{0:T(256)S(1)}, bf16[2048]{0:T(1024)(128)(2,1)S(1)}, f32[256,2048]{1,0:T(8,128)}) fusion(f32[256,2048]{1,0:T(8,128)} %copy-done.1, f32[256]{0:T(256)S(1)} %fusion.135, f32[256]{0:T(256)S(1)} %broadcast_multiply_fusion, f32[2048]{0:T(1024)S(1)} %bitcast.211, ...), kind=kOutput, calls=%fused_computation.83 | convolution fusion | flops 8594124800 | bytes 41962496 | tf_op jit(solution)/shard_map/dot_general | solution.py:49
  519.6 6.7 convolution_convert_fusion.5
  557.3 5.9 collective-permute-done.5
  578.3 5.9 convolution_convert_fusion.3
  585.8 5.6 convolution_convert_fusion.2
  592.9 16.3 %convolution_convert_fusion.1 = bf16[2048,8192]{1,0:T(8,128)(2,1)} fusion(bf16[256,8192]{1,0:T(8,128)(2,1)} %get-tuple-element.88, f32[256,2048]{1,0:T(8,128)S(1)} %copy-done.2, f32[2048]{0:T(1024)S(1)} %bitcast.222, f32[2048]{0:T(1024)S(1)} %bitcast.213, f32[256]{0:T(256)S(1)} %fusion.135, f32[256]{0:T(256)S(1)} %broadcast_multiply_fusion), kind=kOutput, calls=%fused_computation.1 | convolution fusion | flops 8609333248 | bytes 39864320 | tf_op jit(solution)/shard_map/dot_general | solution.py:43
  609.4 20.5 %convolution_convert_fusion = bf16[8192,2048]{1,0:T(8,128)(2,1)} fusion(bf16[1,256,2048]{2,1,0:T(8,128)(2,1)} %param.33, f32[256,8192]{1,0:T(8,128)} %convolution_add_fusion), kind=kOutput, calls=%fused_computation | convolution fusion | flops 8625586176 | bytes 42991616 | tf_op jit(solution)/shard_map/dot_general | solution.py:43
  630.0 51.0 %reduce-scatter.6.cloned.1.call-done = bf16[256,2048]{1,0:T(8,128)(2,1)} async-done(((bf16[2048,2048]{1,0:T(8,128)(2,1)}), bf16[256,2048]{1,0:T(8,128)(2,1)}) %reduce-scatter.6.cloned.1.call-update) | async-done | bytes 1048592 | tf_op jit(solution)/shard_map/reduce_scatter | solution.py:264
  681.0 75.1 %reduce-scatter.10.cloned.1.call-done = bf16[256,2048]{1,0:T(8,128)(2,1)} async-done(((bf16[2048,2048]{1,0:T(8,128)(2,1)}), bf16[256,2048]{1,0:T(8,128)(2,1)}) %reduce-scatter.10.cloned.1.call-update) | async-done | bytes 1048592 | tf_op jit(solution)/shard_map/reduce_scatter | solution.py:270
  756.1 208.8 %reduce-scatter.12.cloned.1.call-done = bf16[256,8192]{1,0:T(8,128)(2,1)} async-done(((bf16[2048,8192]{1,0:T(8,128)(2,1)}), bf16[256,8192]{1,0:T(8,128)(2,1)}) %reduce-scatter.12.cloned.1.call-update) | async-done | bytes 4194320 | tf_op jit(solution)/shard_map/reduce_scatter | solution.py:316
  965.0 209.1 %reduce-scatter.14.cloned.1.call-done = bf16[1024,2048]{1,0:T(8,128)(2,1)} async-done(((bf16[8192,2048]{1,0:T(8,128)(2,1)}), bf16[1024,2048]{1,0:T(8,128)(2,1)}) %reduce-scatter.14.cloned.1.call-update) | async-done | bytes 4194320 | tf_op jit(solution)/shard_map/reduce_scatter | solution.py:322
  1175.5 8.8 all-gather.6
  1186.3 7.4 fusion.176
  1193.7 19.6 %fusion.28 = bf16[1,256,2048]{2,1,0:T(8,128)(2,1)} fusion(f32[256,2048]{1,0:T(8,128)S(1)} %copy-done.2, bf16[8192,2048]{1,0:T(8,128)(2,1)} %all-gather.21.cloned.1.call-done, f32[2048]{0:T(1024)S(1)} %bitcast.230, f32[256,8192]{1,0:T(8,128)} %convolution_add_fusion), kind=kOutput, calls=%fused_computation.63 | convolution fusion | flops 8610381824 | bytes 45096960 | tf_op jit(solution)/shard_map/dot_general | solution.py:39
  1218.9 25.7 %all-reduce.11 = (bf16[2048]{0:T(1024)(128)(2,1)S(1)}, bf16[128]{0:T(256)(128)(2,1)S(1)}, bf16[2048]{0:T(1024)(128)(2,1)S(1)}, bf16[2048]{0:T(1024)(128)(2,1)S(1...) all-reduce(bf16[2048]{0:T(1024)(128)(2,1)S(1)} %bitcast.228, ...), channel_id=5, replica_groups=mesh['ctx'=4,'fsdp'=8] {'fsdp'}, use_global_device_ids=true, to_apply=%region_24.25.clone | all-reduce | flops 22656 | bytes 90624
  1245.2 13.0 all-reduce.12
  1267.1 276.1 %all-reduce.16.cloned.1.call-done = (bf16[256,2048]{1,0:T(8,128)(2,1)}, bf16[256,256]{1,0:T(8,128)(2,1)}, bf16[256,2048]{1,0:T(8,128)(2,1)}, bf16[256,8192]{1,0:T(8,128)(2,1)}, bf16[1024,2048]{1,0:T(8,128)(2,1)}) async-done(((bf16[256,2048]{1,0:T(8,128)(2,1)}, bf16[256,256]{1,0:T(8,128)(2,1)}, bf16[256,2048]{1,0:T(8,128)(2,1)}, bf16[256,8192]{1,0:T(8,128)(2,1)}, bf16[1024,2048]{1,0:T(8,128)(2,1)}), ...) | async-done | bytes 10616848 | tf_op jit(solution)/shard_map/psum | solution.py:329
  (245 shorter events, 130.4 us)
Async XLA Ops:
  7.2 38.3 %all-gather.15.cloned.1.call-start = ((), (), s32[]{:S(2)}) async-start(), calls=%async_computation.6 | async-start | bytes 1179648 | tf_op jit(solution)/shard_map/all_gather | solution.py:147
  7.9 96.7 %all-gather.13.cloned.1.call-start = ((), (), s32[]{:S(2)}) async-start(), calls=%async_computation.5 | async-start | bytes 9437184 | tf_op jit(solution)/shard_map/all_gather | solution.py:146
  8.7 140.2 %all-gather.17.cloned.1.call-start = ((), (), s32[]{:S(2)}) async-start(), calls=%async_computation.7 | async-start | bytes 9437184 | tf_op jit(solution)/shard_map/all_gather | solution.py:148
  9.4 20.6 %copy-start.42 = (u32[32]{0:T(128)S(1)}, u32[32]{0:T(128)}, u32[]{:S(2)}) copy-start(u32[32]{0:T(128)} %constant.82) | copy-start | bytes 388
  9.4 21.9 %copy-start.45 = (bf16[16]{0:T(256)(128)(2,1)S(1)}, bf16[16]{0:T(256)(128)(2,1)}, u32[]{:S(2)}) copy-start(bf16[16]{0:T(256)(128)(2,1)} %param.23) | copy-start | bytes 100
  9.4 35.4 %copy-start = (bf16[1,256,2048]{2,1,0:T(8,128)(2,1)S(1)}, bf16[1,256,2048]{2,1,0:T(8,128)(2,1)}, u32[]{:S(2)}) copy-start(bf16[1,256,2048]{2,1,0:T(8,128)(2,1)} %param.17) | copy-start | bytes 3145732
  9.5 302.0 %all-gather.19.cloned.1.call-start = ((), (), s32[]{:S(2)}) async-start(), calls=%async_computation.8 | async-start | bytes 37748736 | tf_op jit(solution)/shard_map/all_gather | solution.py:195
  10.0 464.0 %all-gather.21.cloned.1.call-start = ((), (), s32[]{:S(2)}) async-start(), calls=%async_computation.9 | async-start | bytes 37748736 | tf_op jit(solution)/shard_map/all_gather | solution.py:196
  10.6 40.4 %copy-start.46 = (bf16[256]{0:T(256)(128)(2,1)S(1)}, bf16[256]{0:T(256)(128)(2,1)}, u32[]{:S(2)}) copy-start(bf16[256]{0:T(256)(128)(2,1)} %param.24) | copy-start | bytes 1540
  10.6 48.3 %copy-start.47 = (bf16[256]{0:T(256)(128)(2,1)S(1)}, bf16[256]{0:T(256)(128)(2,1)}, u32[]{:S(2)}) copy-start(bf16[256]{0:T(256)(128)(2,1)} %param.22) | copy-start | bytes 1540
  10.6 57.3 %copy-start.41 = (bf16[1024]{0:T(1024)(128)(2,1)S(1)}, bf16[1024]{0:T(1024)(128)(2,1)}, u32[]{:S(2)}) copy-start(bf16[1024]{0:T(1024)(128)(2,1)} %param.29) | copy-start | bytes 6148
  10.6 65.2 %copy-start.48 = (bf16[256]{0:T(256)(128)(2,1)S(1)}, bf16[256]{0:T(256)(128)(2,1)}, u32[]{:S(2)}) copy-start(bf16[256]{0:T(256)(128)(2,1)} %param.32) | copy-start | bytes 1540
  10.7 74.1 %copy-start.49 = (bf16[256]{0:T(256)(128)(2,1)S(1)}, bf16[256]{0:T(256)(128)(2,1)}, u32[]{:S(2)}) copy-start(bf16[256]{0:T(256)(128)(2,1)} %param.31) | copy-start | bytes 1540
  10.7 82.0 %copy-start.39 = (s32[1,1024]{1,0:T(1,128)S(1)}, s32[1,1024]{1,0:T(1,128)}, u32[]{:S(2)}) copy-start(s32[1,1024]{1,0:T(1,128)} %param.18) | copy-start | bytes 12292
  10.7 619.3 %reduce-scatter.8.cloned.1.call-start = ((), (), s32[]{:S(2)}) async-start(), calls=%async_computation.11 | async-start | bytes 1179648 | tf_op jit(solution)/shard_map/reduce_scatter | solution.py:267
  47.4 57.2 %copy-start.33 = (bf16[256,256]{1,0:T(8,128)(2,1)}, bf16[256,256]{1,0:T(8,128)(2,1)S(1)}, u32[]{:S(2)}) copy-start(bf16[256,256]{1,0:T(8,128)(2,1)S(1)} %fusion.85) | copy-start | bytes 393220
  47.5 45.3 %collective-permute-start = (bf16[256,256]{1,0:T(8,128)(2,1)S(1)}, bf16[256,256]{1,0:T(8,128)(2,1)S(1)}, u32[]{:S(2)}, u32[]{:S(2)}) collective-permute-start(bf16[256,256]{1,0:T(8,128)(2,1)S(1)} %fusion.85), channel_id=1, source_target_pairs={{0,8},{8,16},{16,24},{1,9},{9,17},{17,25},{2,10},{10,18},{18,26},{... | collective-permute-start | bytes 393224 | tf_op jit(solution)/shard_map/ppermute | solution.py:20
  92.8 6.7 collective-permute-start.1
  99.5 15.7 collective-permute-start.2
  129.6 25.2 %copy-start.22 = (bf16[256,16,128]{0,2,1:T(8,128)(2,1)}, bf16[256,16,128]{0,2,1:T(8,128)(2,1)S(1)}, u32[]{:S(2)}) copy-start(bf16[256,16,128]{0,2,1:T(8,128)(2,1)S(1)} %get-tuple-element.79) | copy-start | bytes 3145732
  311.5 162.6 %copy-start.14 = (bf16[1,256,2048]{2,1,0:T(8,128)(2,1)S(1)}, bf16[1,256,2048]{2,1,0:T(8,128)(2,1)}, u32[]{:S(2)}) copy-start(bf16[1,256,2048]{2,1,0:T(8,128)(2,1)} %param.33) | copy-start | bytes 3145732
  540.1 9.0 collective-permute-start.3
  549.2 7.2 collective-permute-start.4
  551.5 19.0 %copy-start.40 = (f32[256]{0:T(256)S(1)}, f32[256]{0:T(256)}, u32[]{:S(2)}) copy-start(f32[256]{0:T(256)} %constant.74.clone.1) | copy-start | bytes 3076
  556.4 6.8 collective-permute-start.5
  563.3 7.2 collective-permute-start.6
  572.3 108.7 %reduce-scatter.6.cloned.1.call-start = ((), (), s32[]{:S(2)}) async-start(), calls=%async_computation.10 | async-start | bytes 9437184 | tf_op jit(solution)/shard_map/reduce_scatter | solution.py:264
  584.2 171.9 %reduce-scatter.10.cloned.1.call-start = ((), (), s32[]{:S(2)}) async-start(), calls=%async_computation.12 | async-start | bytes 9437184 | tf_op jit(solution)/shard_map/reduce_scatter | solution.py:270
  591.3 373.6 %reduce-scatter.12.cloned.1.call-start = ((), (), s32[]{:S(2)}) async-start(), calls=%async_computation.13 | async-start | bytes 37748736 | tf_op jit(solution)/shard_map/reduce_scatter | solution.py:316
  609.2 564.9 %reduce-scatter.14.cloned.1.call-start = ((), (), s32[]{:S(2)}) async-start(), calls=%async_computation.14 | async-start | bytes 37748736 | tf_op jit(solution)/shard_map/reduce_scatter | solution.py:322
  629.9 913.2 %all-reduce.16.cloned.1.call-start = ((), (), s32[]{:S(2)}) async-start(), calls=%async_computation.15 | async-start | bytes 21233664 | tf_op jit(solution)/shard_map/psum | solution.py:329
  1213.6 49.7 %copy-start.4 = (f32[256,2048]{1,0:T(8,128)S(1)}, f32[256,2048]{1,0:T(8,128)}, u32[]{:S(2)}) copy-start(f32[256,2048]{1,0:T(8,128)} %copy-done.3) | copy-start | bytes 6291460
  (37 other events, 163.4 us)
Sparse Core Ops, SparseCore 0:
  9.9 26.1 all-gather.14
  38.0 54.5 all-gather.12
  94.5 54.3 all-gather.16
  150.6 160.7 all-gather.18
  313.2 160.7 all-gather.20
  572.4 33.2 reduce-scatter.7
  609.7 71.2 reduce-scatter.5
  684.8 71.2 reduce-scatter.9
  759.7 205.2 reduce-scatter.11
  968.8 205.2 reduce-scatter.13
  1177.2 365.8 all-reduce.15
where the time goes:
time: 1580 us; the launch traced here: 1570 us
  waiting for transfers between devices  1160 us (73%)
  matrix products  200 us (13%)
  blocking collectives  121 us (8%)
  other arithmetic  37.6 us (2%)
  between operations  17.8 us (1%)
  starting transfers between devices  17 us (1%)
  local copies, waits for them, and re-layouts  16.2 us (1%)
    psum x1, waiting for transfers between devices, per_device(): lax.psum(shares[0].astype(jnp.bfloat16), 'ctx').astype(jnp.float32)  276 us
    reduce_scatter x1, waiting for transfers between devices, per_device(): lax.psum_scatter(product_tn(hidden_low, out_grad).astype(jnp.bfloat16), '...  209 us
    reduce_scatter x1, waiting for transfers between devices, per_device(): lax.psum_scatter(product_tn(normed_mid, grad_pre).astype(jnp.bfloat16), '...  209 us
    all_gather x1, waiting for transfers between devices, per_device(): lax.all_gather(fc_weight, 'fsdp', axis=0, tiled=True)  155 us
    all_gather x1, waiting for transfers between devices, per_device(): lax.all_gather(proj_weight, 'fsdp', axis=0, tiled=True)  141 us
    reduce_scatter x1, waiting for transfers between devices, per_device(): lax.psum_scatter(out_term.astype(jnp.bfloat16), 'fsdp', scatter_dimension...  75.1 us
    dot_general x5, matrix products, product_nt(): lax.dot_general(left_side, right_side, (((1,), (1,)), ((), ())), preferre...  57 us
    dot_general x5, matrix products, product(): return jnp.dot(left_side, right_side, preferred_element_type=jnp.float32)  54.7 us
  transfers between devices with their start and end apart: 18, of which 12 were waited for; matrix products, arithmetic and copies ran while one was open for 10% of the time, Pallas kernels for 0%

commit v1 on v0

v1 whole, which is shorter than its diff:
```python
import math

import jax
import jax.numpy as jnp
from jax import lax
from jax.experimental import pallas as pl
from jax.experimental.pallas import tpu as pltpu
from jax.sharding import PartitionSpec as P

H = 16
HD = 128
WINDOW = 1024
EPSILON = 1e-05
NEGATIVE = -1e30
SCALING = 1.0 / math.sqrt(HD)
LOG2E = math.log2(math.e)
LOW = jnp.bfloat16
FULL = jnp.float32


def tie(value, *after):
    return lax.optimization_barrier((value, after))[0]


def product(left_side, right_side):
    return jnp.dot(left_side, right_side, preferred_element_type=FULL)


def product_tn(left_side, right_side):
    return lax.dot_general(
        left_side, right_side, (((0,), (0,)), ((), ())), preferred_element_type=FULL
    )


def product_nt(left_side, right_side):
    return lax.dot_general(
        left_side, right_side, (((1,), (1,)), ((), ())), preferred_element_type=FULL
    )


QUICK = pl.CostEstimate(flops=0, bytes_accessed=0, transcendentals=0)
ROOMY = pltpu.CompilerParams(vmem_limit_bytes=56 * 2**20)


def matmul(left_side, right_side, kind, step_rows=512, step_cols=2048, first=0, count=None):
    rows = count or (left_side.shape[1] if kind == "tn" else left_side.shape[0])
    depth = left_side.shape[0] if kind == "tn" else left_side.shape[1]
    cols = right_side.shape[0] if kind == "nt" else right_side.shape[1]
    step_rows, step_cols = math.gcd(step_rows, rows), math.gcd(step_cols, cols)
    inner = {"nn": product, "nt": product_nt, "tn": product_tn}[kind]
    at = first // step_rows

    def body(left_ref, right_ref, out_ref):
        out_ref[...] = inner(left_ref[...], right_ref[...]).astype(LOW)

    left_spec = (
        pl.BlockSpec((depth, step_rows), lambda j, i: (0, at + i))
        if kind == "tn"
        else pl.BlockSpec((step_rows, depth), lambda j, i: (at + i, 0))
    )
    right_spec = (
        pl.BlockSpec((step_cols, depth), lambda j, i: (j, 0))
        if kind == "nt"
        else pl.BlockSpec((depth, step_cols), lambda j, i: (0, j))
    )
    return pl.pallas_call(
        body,
        grid=(cols // step_cols, rows // step_rows),
        in_specs=[left_spec, right_spec],
        out_specs=pl.BlockSpec((step_rows, step_cols), lambda j, i: (i, j)),
        out_shape=jax.ShapeDtypeStruct((rows, cols), LOW),
        compiler_params=ROOMY,
        cost_estimate=QUICK,
        name="matmul_" + kind,
    )(left_side, right_side)


def member_order():
    return jnp.stack([member_of(k) for k in range(lax.axis_size("fsdp"))]).astype(jnp.int32)


def fc_gradient(mid_all, grad_part):
    peers = lax.axis_size("fsdp")
    rows, width = mid_all.shape
    step, cols = width // peers, grad_part.shape[1]

    def body(order_ref, mid_ref, grad_ref, out_ref):
        out_ref[0] = product_tn(mid_ref[...], grad_ref[...]).astype(LOW)

    return pl.pallas_call(
        body,
        grid_spec=pltpu.PrefetchScalarGridSpec(
            num_scalar_prefetch=1,
            grid=(peers,),
            in_specs=[
                pl.BlockSpec((rows, step), lambda k, order: (0, order[k])),
                pl.BlockSpec((rows, cols), lambda k, order: (0, 0)),
            ],
            out_specs=pl.BlockSpec((1, step, cols), lambda k, order: (k, 0, 0)),
        ),
        out_shape=jax.ShapeDtypeStruct((peers, step, cols), LOW),
        compiler_params=ROOMY,
        cost_estimate=QUICK,
        name="fc_gradient",
    )(member_order(), mid_all, grad_part)


def finish_rows(ends, pairs):
    rows, cols = pairs[0][0].shape
    step = rows // 2 if rows % 32 == 0 else rows

    def body(ends_ref, *refs):
        for c in range(len(pairs)):
            @pl.when(pl.program_id(0) == c)
            def _():
                chosen = jnp.where(ends_ref[0] == 1, refs[2 * c][...], refs[2 * c + 1][...])
                refs[-1][...] = chosen.astype(FULL)

    def spec(c):
        last = rows // step - 1
        return pl.BlockSpec(
            (step, cols), lambda i, j: (jnp.where(i == c, j, jnp.where(i > c, last, 0)), 0)
        )

    return pl.pallas_call(
        body,
        grid=(len(pairs), rows // step),
        in_specs=[pl.BlockSpec(memory_space=pltpu.SMEM)]
        + [spec(c) for c in range(len(pairs)) for unused in range(2)],
        out_specs=pl.BlockSpec((step, cols), lambda i, j: (i * (rows // step) + j, 0)),
        out_shape=jax.ShapeDtypeStruct((rows * len(pairs), cols), FULL),
        compiler_params=ROOMY,
        cost_estimate=QUICK,
        name="finish_rows",
    )(ends, *[array for pair in pairs for array in pair])


def finish_columns(ends, pairs, step):
    peers = lax.axis_size("fsdp")
    rows, cols = pairs[0][0].shape
    blocks = cols // step
    rounds = len(pairs) * blocks // peers

    def body(ends_ref, order_ref, *refs):
        for c in range(len(pairs)):
            @pl.when(pl.program_id(0) == c)
            def _():
                chosen = jnp.where(ends_ref[0] == 1, refs[2 * c][...], refs[2 * c + 1][...])
                refs[-1][...] = chosen.astype(FULL)

    def spec(c):
        return pl.BlockSpec(
            (rows, step),
            lambda i, j, ends, order: (0, jnp.where(i == c, j, jnp.where(i > c, blocks - 1, 0))),
        )

    def placed(i, j, ends, order):
        at = i * blocks + j
        return (0, order[lax.rem(at, peers)] * rounds + at // peers)

    return pl.pallas_call(
        body,
        grid_spec=pltpu.PrefetchScalarGridSpec(
            num_scalar_prefetch=2,
            grid=(len(pairs), blocks),
            in_specs=[spec(c) for c in range(len(pairs)) for unused in range(2)],
            out_specs=pl.BlockSpec((rows, step), placed),
        ),
        out_shape=jax.ShapeDtypeStruct((rows, cols * len(pairs)), FULL),
        compiler_params=ROOMY,
        cost_estimate=QUICK,
        name="finish_columns",
    )(ends, member_order(), *[array for pair in pairs for array in pair])


def feed_forward_body(mid_ref, fc_ref, bias_ref, cot_ref, proj_ref, hidden_ref, grad_ref):
    hidden_act, slope = gelu_pair(product(mid_ref[...], fc_ref[...]) + bias_ref[...])
    hidden_ref[...] = hidden_act.astype(LOW)
    grad_ref[...] = (product_nt(cot_ref[...], proj_ref[...]) * slope).astype(LOW)


def feed_forward(mid_all, fc_all, bias, cot_all, proj, first, count):
    rows, width = mid_all.shape
    step_rows, step = math.gcd(512, rows), math.gcd(512, count)
    at = first // step
    by_row = pl.BlockSpec((step_rows, width), lambda i, j: (i, 0))
    made = pl.BlockSpec((step_rows, step), lambda i, j: (i, j))
    return pl.pallas_call(
        feed_forward_body,
        grid=(rows // step_rows, count // step),
        in_specs=[
            by_row,
            pl.BlockSpec((width, step), lambda i, j: (0, at + j)),
            pl.BlockSpec((1, step), lambda i, j: (0, at + j)),
            by_row,
            pl.BlockSpec((step, width), lambda i, j: (at + j, 0)),
        ],
        out_specs=[made, made],
        out_shape=[jax.ShapeDtypeStruct((rows, count), LOW)] * 2,
        compiler_params=ROOMY,
        cost_estimate=QUICK,
        name="feed_forward",
    )(mid_all, fc_all, bias[None], cot_all, proj)


def by_xor():
    return lax.axis_size("fsdp") == 8


def swap(array, bits):
    return lax.ppermute(array, "fsdp", [(i, i ^ bits) for i in range(8)])


def member_of(k):
    return lax.axis_index("fsdp") ^ k if by_xor() else jnp.int32(k)


def near_rows(own):
    return swap(own, 2), swap(own, 4)


def gather_rows(own, near, whole):
    count = own.shape[0]
    half = count // 2
    along_x, along_y = near
    first_half, second_half = swap(along_x[:half], 4), swap(along_y[half:], 2)
    placed = [
        (0, 0, own),
        (1, 0, swap(own, 1)),
        (2, 0, along_x),
        (3, 0, swap(along_x, 1)),
        (4, 0, along_y),
        (5, 0, swap(along_y, 1)),
        (6, 0, first_half),
        (6, half, second_half),
        (7, 0, swap(first_half, 1)),
        (7, half, swap(second_half, 1)),
    ]
    for k, offset, block in placed:
        start = (member_of(k) * count + offset,) + (0,) * (own.ndim - 1)
        whole = lax.dynamic_update_slice(whole, block, start)
    return whole


def gather_plain(own):
    return lax.all_gather(own, "fsdp", axis=0, tiled=True)


def gather_small(own):
    held = own[None]
    for bits in (1, 2, 4):
        held = jnp.concatenate([held, swap(held, bits)], axis=0)
    return relative(held, 0)


def add_low(first, *others):
    total = first.astype(FULL)
    for other in others:
        total = total + other.astype(FULL)
    return total.astype(LOW)


def scatter_rows(array):
    return lax.psum_scatter(array, "fsdp", scatter_dimension=0, tiled=True)


def in_relative_order(array):
    step = array.shape[0] // lax.axis_size("fsdp")
    return [
        lax.dynamic_slice_in_dim(array, member_of(k) * step, step, 0)
        for k in range(lax.axis_size("fsdp"))
    ]


def scatter_first(blocks):
    if not by_xor():
        return blocks
    return [add_low(blocks[k], swap(blocks[k + 1], 1)) for k in (0, 2, 4, 6)]


def scatter_second(held):
    if not by_xor():
        return held
    mine, along_x, along_y, across = held
    half = mine.shape[0] // 2
    upper, lower = swap(across[:half], 2), swap(across[half:], 4)
    along_y = jnp.concatenate([add_low(along_y[:half], upper), along_y[half:]], axis=0)
    along_x = jnp.concatenate([along_x[:half], add_low(along_x[half:], lower)], axis=0)
    return [mine, along_x, along_y]


def scatter_third(held):
    if not by_xor():
        return scatter_rows(jnp.concatenate(held, axis=0)).astype(FULL)
    mine, along_x, along_y = held
    from_x, from_y = swap(along_x, 2), swap(along_y, 4)
    return mine.astype(FULL) + from_x.astype(FULL) + from_y.astype(FULL)


def exchange_blocks(blocks):
    if not by_xor():
        moved = lax.all_to_all(jnp.stack(blocks), "fsdp", 0, 0, tiled=True)
        return [moved[k] for k in range(len(blocks))]
    return [blocks[0]] + [swap(blocks[k], k) for k in range(1, 8)]


def relative(array, axis):
    if not by_xor():
        return array
    step = array.shape[axis] // 8
    return jnp.concatenate(
        [lax.dynamic_slice_in_dim(array, member_of(k) * step, step, axis) for k in range(8)],
        axis=axis,
    )


def columns_sent(own):
    planes = lax.axis_size("ctx")
    part, share = own.shape[0] // planes, own.shape[1] // 8
    place = lax.axis_index("ctx")
    return [
        lax.dynamic_slice(own, (place * part, member_of(k) * share), (part, share)) for k in range(8)
    ]


def columns_held(moved):
    held = jnp.zeros((8,) + moved[0].shape, moved[0].dtype)
    for k in range(8):
        held = lax.dynamic_update_slice(held, moved[k][None], (member_of(k), 0, 0))
    return held


def next_plane(held):
    planes = lax.axis_size("ctx")
    return lax.ppermute(held, "ctx", [(i, (i + 1) % planes) for i in range(planes)])


def columns_whole(held_parts):
    planes = len(held_parts)
    peers, part, share = held_parts[0].shape
    whole = jnp.zeros((peers, planes, part, share), held_parts[0].dtype)
    for step, held in enumerate(held_parts):
        source = lax.rem(lax.axis_index("ctx") + planes - step, planes)
        whole = lax.dynamic_update_slice(whole, held[:, None], (0, source, 0, 0))
    return whole.reshape(peers * planes * part, share)


def tick_body(at_end_ref, given, *refs):
    names = [name for name, there in given if there]
    held = dict(zip(names, refs))
    made = list(refs[len(names) :])

    def add(first, second):
        return (held[first][...].astype(FULL) + held[second][...].astype(FULL)).astype(LOW)

    if "fresh" in held:
        made.pop(0)[...] = add("fresh", "from_end")
    if "middle" in held:
        total = add("middle", "other")
        if "later" in held:
            total = jnp.where(at_end_ref[0] == 1, held["later"][...], total)
        made.pop(0)[...] = total


class SumOverCtx:
    def __init__(self, first):
        self.on_line = lax.axis_size("ctx") == 4
        place = lax.axis_index("ctx")
        self.ends = ((place == 0) | (place == 3)).astype(jnp.int32)[None]
        self.state = (first, None, None, first)
        self.results = []

    def combine(self, **arrays):
        given = {name: array for name, array in arrays.items() if array is not None}
        shape = next(iter(given.values())).shape
        count = ("fresh" in given) + ("middle" in given)
        pieces = 4 if shape[0] % 64 == 0 else 1
        spec = pl.BlockSpec((shape[0] // pieces, shape[1]), lambda i: (i, 0))
        flags = [(name, name in given) for name in arrays]
        return pl.pallas_call(
            lambda at_end_ref, *refs: tick_body(at_end_ref, flags, *refs),
            grid=(pieces,),
            in_specs=[pl.BlockSpec(memory_space=pltpu.SMEM)] + [spec] * len(given),
            out_specs=[spec] * count,
            out_shape=[jax.ShapeDtypeStruct(shape, LOW)] * count,
            compiler_params=ROOMY,
            cost_estimate=QUICK,
            name="tick",
        )(self.ends, *given.values())

    def move(self, later=None):
        fresh, middle, outgoing, incoming = self.state
        if not self.on_line:
            if fresh is not None:
                total = lax.psum(fresh, "ctx")
                self.results.append((total, total))
            self.state = (later, None, None, None)
            return
        inward, outward = [(0, 1), (3, 2)], [(1, 0), (2, 3)]
        from_end = other = None
        if outgoing is not None and outgoing is incoming:
            from_end = from_middle = lax.ppermute(outgoing, "ctx", inward + outward)
        else:
            if fresh is not None:
                from_end = lax.ppermute(incoming, "ctx", inward)
            if outgoing is not None:
                from_middle = lax.ppermute(outgoing, "ctx", outward)
        if outgoing is not None:
            self.results.append((from_middle, outgoing))
        if middle is not None:
            other = lax.ppermute(middle, "ctx", [(1, 2), (2, 1)])
        pair_sum = total = None
        joined = middle is not None and later is not None and later.shape == middle.shape
        alike = fresh is None or middle is None or fresh.shape == middle.shape
        chosen = later if joined else None
        if alike and (fresh is not None or middle is not None):
            made = self.combine(
                fresh=fresh, from_end=from_end, middle=middle, other=other, later=chosen
            )
            pair_sum = made[0] if fresh is not None else None
            total = made[-1] if middle is not None else None
        elif fresh is not None:
            (pair_sum,) = self.combine(fresh=fresh, from_end=from_end)
            (total,) = self.combine(middle=middle, other=other, later=chosen)
        self.state = (later, pair_sum, total, total if joined else later)

    def fence(self, *values):
        fresh, middle, outgoing, incoming = self.state
        joined = outgoing is not None and outgoing is incoming
        held = (fresh, middle, outgoing, None if joined or incoming is fresh else incoming)
        held, values = lax.optimization_barrier((held, values))
        incoming = held[2] if joined else held[0]
        self.state = (held[0], held[1], held[2], incoming)
        return values


def attend_kernel(query_ref, key_ref, value_t_ref, mask_ref, out_ref, total_ref):
    scores = product_nt(key_ref[...], query_ref[...]) * (SCALING * LOG2E) + mask_ref[...]
    largest = jnp.max(scores, axis=0, keepdims=True)
    weights = jnp.exp2(scores - largest)
    weight_sum = jnp.sum(weights, axis=0, keepdims=True)
    gathered = product(value_t_ref[...], weights.astype(LOW))
    out_ref[...] = (gathered / weight_sum).T.astype(LOW)
    total_ref[0] = largest + jnp.log2(weight_sum)


def attend(queries, keys, values_t, mask):
    rows, key_rows = queries.shape[0], keys.shape[0]
    whole = lambda head: (0, 0)
    by_head = lambda head: (0, head)
    return pl.pallas_call(
        attend_kernel,
        grid=(H,),
        in_specs=[
            pl.BlockSpec((rows, HD), by_head),
            pl.BlockSpec((key_rows, HD), whole),
            pl.BlockSpec((HD, key_rows), whole),
            pl.BlockSpec((key_rows, rows), whole),
        ],
        out_specs=[
            pl.BlockSpec((rows, HD), by_head),
            pl.BlockSpec((1, 1, rows), lambda head: (head, 0, 0)),
        ],
        out_shape=[
            jax.ShapeDtypeStruct((rows, H * HD), LOW),
            jax.ShapeDtypeStruct((H, 1, rows), FULL),
        ],
        compiler_params=ROOMY,
        cost_estimate=QUICK,
        name="attend",
    )(queries, keys, values_t, mask)


def attend_back_kernel(
    query_ref,
    grad_ref,
    out_ref,
    total_ref,
    key_ref,
    key_t_ref,
    value_ref,
    mask_ref,
    grad_query_ref,
    grad_key_ref,
    grad_value_ref,
):
    @pl.when(pl.program_id(0) == 0)
    def _():
        grad_key_ref[...] = jnp.zeros_like(grad_key_ref)
        grad_value_ref[...] = jnp.zeros_like(grad_value_ref)

    query, grad = query_ref[...], grad_ref[...]
    scores = product_nt(key_ref[...], query) * (SCALING * LOG2E) + mask_ref[...]
    probs = jnp.exp2(scores - total_ref[0])
    grad_probs = product_nt(value_ref[...], grad)
    delta = jnp.sum((grad.astype(FULL) * out_ref[...].astype(FULL)).T, axis=0, keepdims=True)
    grad_scores = (probs * (grad_probs - delta)).astype(LOW)
    grad_value_ref[...] += product(probs.astype(LOW), grad)
    grad_key_ref[...] += product(grad_scores, query)
    grad_query_ref[...] = (product(key_t_ref[...], grad_scores).T * SCALING).astype(LOW)


def attend_back(queries, grad_out, out, totals, keys, keys_t, values, mask):
    rows, key_rows = queries.shape[0], keys.shape[0]
    whole = lambda head: (0, 0)
    by_head = lambda head: (0, head)
    return pl.pallas_call(
        attend_back_kernel,
        grid=(H,),
        in_specs=[
            pl.BlockSpec((rows, HD), by_head),
            pl.BlockSpec((rows, HD), by_head),
            pl.BlockSpec((rows, HD), by_head),
            pl.BlockSpec((1, 1, rows), lambda head: (head, 0, 0)),
            pl.BlockSpec((key_rows, HD), whole),
            pl.BlockSpec((HD, key_rows), whole),
            pl.BlockSpec((key_rows, HD), whole),
            pl.BlockSpec((key_rows, rows), whole),
        ],
        out_specs=[
            pl.BlockSpec((rows, HD), by_head),
            pl.BlockSpec((key_rows, HD), whole),
            pl.BlockSpec((key_rows, HD), whole),
        ],
        out_shape=[
            jax.ShapeDtypeStruct((rows, H * HD), LOW),
            jax.ShapeDtypeStruct((key_rows, HD), FULL),
            jax.ShapeDtypeStruct((key_rows, HD), FULL),
        ],
        compiler_params=ROOMY,
        cost_estimate=QUICK,
        name="attend_back",
    )(queries, grad_out, out, totals, keys, keys_t, values, mask)


def normalize(values_in):
    center = values_in - jnp.mean(values_in, axis=-1, keepdims=True)
    spread = jnp.mean(center * center, axis=-1, keepdims=True)
    inverse = lax.rsqrt(spread + EPSILON)
    return center * inverse, inverse


def norm_pullback(normed, inverse, gain_vec, grad_in):
    weighted = grad_in * gain_vec
    grad_values = inverse * (
        weighted
        - jnp.mean(weighted, axis=-1, keepdims=True)
        - normed * jnp.mean(weighted * normed, axis=-1, keepdims=True)
    )
    return grad_values, jnp.sum(grad_in * normed, axis=0), jnp.sum(grad_in, axis=0)


def gelu_pair(values_in):
    root = math.sqrt(2.0 / math.pi)
    square = values_in * values_in
    turned = jnp.tanh(root * values_in * (1.0 + 0.044715 * square))
    slope = 0.5 * (1.0 + turned) + 0.5 * values_in * (1.0 - turned * turned) * root * (
        1.0 + 3.0 * 0.044715 * square
    )
    return 0.5 * values_in * (1.0 + turned), slope


def per_device(
    tokens,
    segments,
    query_weight,
    pair_weight,
    out_weight,
    query_bias,
    value_bias,
    out_bias,
    norm1_gain,
    norm1_bias,
    fc_weight,
    proj_weight,
    fc_bias,
    proj_bias,
    norm2_gain,
    norm2_bias,
    cotangent,
):
    rows, width = tokens.shape[1:]
    peers = lax.axis_size("fsdp")
    depth_share = width // peers
    ctx_count = lax.axis_size("ctx")
    ctx_index = lax.axis_index("ctx")
    members = range(peers)

    spelled = by_xor() and ctx_count == 4
    ff_share = fc_weight.shape[1] // peers
    cot_own = cotangent[0]
    vectors = [query_bias, out_bias, norm1_gain, norm1_bias, proj_bias, norm2_gain, norm2_bias]
    vectors_own = jnp.concatenate(vectors + [value_bias])
    attn_weight = jnp.concatenate([query_weight, pair_weight], axis=1)
    attn_all = gather_plain(attn_weight)
    if spelled:
        packed = gather_small(vectors_own)
        held = columns_held(exchange_blocks(columns_sent(fc_weight)))
        blank_out, blank_mid = jnp.zeros((2, peers * depth_share, width), LOW)
        packed, held, blank_out, blank_mid = lax.optimization_barrier(
            (packed, held, blank_out, blank_mid)
        )
        out_near = near_rows(tie(out_weight, packed))
        held_parts = [held, next_plane(held)]
        out_near, held_parts, cot_sent = lax.optimization_barrier(
            (out_near, held_parts, cot_own)
        )
        out_all = gather_rows(out_weight, out_near, blank_out)
    else:
        packed = lax.all_gather(vectors_own, "fsdp", axis=0)
        out_all = gather_plain(out_weight)
        fc_all = lax.all_to_all(fc_weight, "fsdp", 1, 0, tiled=True)
    small = [
        packed[:, i * depth_share : (i + 1) * depth_share].reshape(-1).astype(FULL)
        for i in range(len(vectors))
    ]
    query_bias_all, out_bias_all, gain1, bias1, proj_bias_all, gain2, bias2 = small
    value_bias_all = packed[:, len(vectors) * depth_share :].reshape(-1).astype(FULL)

    tok_rows = tokens[0].astype(FULL)
    normed1, inverse1 = normalize(tok_rows)
    normed_in = (normed1 * gain1 + bias1).astype(LOW)
    attn_bias = jnp.concatenate([query_bias_all, jnp.zeros((HD,), FULL), value_bias_all])
    projected = (product(normed_in, attn_all) + attn_bias).astype(LOW)
    queries, pair_own = projected[:, :width], projected[:, width:]
    reach = min(ctx_count - 1, -(-(WINDOW - 1) // rows))
    pairs = [pair_own] + [
        lax.ppermute(pair_own, "ctx", [(i, i + d) for i in range(ctx_count - d)])
        for d in range(1, reach + 1)
    ]
    if spelled:
        held_parts, pairs, out_all, cot_sent = lax.optimization_barrier(
            (held_parts, pairs, out_all, cot_sent)
        )
        held_parts = held_parts + [next_plane(held_parts[-1])]
        cot_all = gather_plain(cot_sent)
    else:
        cot_all = gather_plain(cot_own)
    pair_rows = jnp.concatenate(pairs, axis=0)
    seg_row = segments[0]
    query_first = ctx_index * rows
    key_pos = jnp.concatenate(
        [query_first - d * rows + jnp.arange(rows, dtype=jnp.int32) for d in range(reach + 1)]
    )
    query_pos = query_first + jnp.arange(rows, dtype=jnp.int32)
    query_seg = lax.dynamic_slice_in_dim(seg_row, query_first, rows, 0)
    key_seg = jnp.concatenate(
        [
            lax.dynamic_slice_in_dim(seg_row, jnp.maximum(query_first - d * rows, 0), rows, 0)
            for d in range(reach + 1)
        ]
    )
    allowed = (
        (key_seg[:, None] == query_seg[None, :])
        & (key_pos[:, None] <= query_pos[None, :])
        & (query_pos[None, :] - key_pos[:, None] < WINDOW)
        & (key_pos[:, None] >= 0)
    )
    mask = jnp.where(allowed, 0.0, NEGATIVE).astype(FULL)
    keys, values = pair_rows[:, :HD], pair_rows[:, HD:]
    attended, score_totals = attend(queries, keys, values.T, mask)
    middle = tok_rows + (product(attended, out_all) + out_bias_all)
    normed2, inverse2 = normalize(middle)
    normed_mid = (normed2 * gain2 + bias2).astype(LOW)

    if spelled:
        held_parts, normed_mid = lax.optimization_barrier((held_parts, normed_mid))
        held_parts = held_parts + [next_plane(held_parts[-1])]
        fc_all = columns_whole(held_parts)
        mid_all = gather_rows(normed_mid, near_rows(normed_mid), blank_mid)
    else:
        mid_all = gather_plain(normed_mid)
    fc_bias_own = fc_bias.astype(FULL)
    half = ff_share // 2
    piece = half // 2
    ff_args = (mid_all, fc_all, fc_bias_own, cot_all, proj_weight)
    hidden_first, grad_first = feed_forward(*ff_args, 0, half)

    def proj_term(hidden_part, first):
        return matmul(hidden_part, cot_all, "tn", 256, 1024, first, piece)

    sums = SumOverCtx(proj_term(hidden_first, 0))
    mid_all, cot_all, fc_all, hidden_first, grad_first = sums.fence(
        mid_all, cot_all, fc_all, hidden_first, grad_first
    )

    ff_args = (mid_all, fc_all, fc_bias_own, cot_all, proj_weight)
    hidden_second, grad_second = feed_forward(*ff_args, half, half)
    sums.move(proj_term(hidden_first, piece))
    mid_all, cot_all, grad_first, grad_second, hidden_first, hidden_second = sums.fence(
        mid_all, cot_all, grad_first, grad_second, hidden_first, hidden_second
    )

    grad_pre = jnp.concatenate([grad_first, grad_second], axis=1)
    grad_mid_part = matmul(grad_pre, fc_all, "nt")
    sums.move(proj_term(hidden_second, 0))
    mid_all, cot_all, grad_first, grad_second, hidden_second, grad_mid_part = sums.fence(
        mid_all, cot_all, grad_first, grad_second, hidden_second, grad_mid_part
    )

    grad_normed_mid = scatter_rows(grad_mid_part)
    fc_first = fc_gradient(mid_all, grad_first)
    fc_second = fc_gradient(mid_all, grad_second)
    sums.move(proj_term(hidden_second, piece))
    grad_first, grad_second, hidden_second, fc_first, fc_second = sums.fence(
        grad_first, grad_second, hidden_second, fc_first, fc_second
    )

    hidden = jnp.concatenate([hidden_first, hidden_second], axis=1)
    out_part = matmul(hidden, proj_weight, "nn")
    fc_first = exchange_blocks([fc_first[k] for k in members])
    group = peers // 2
    sums.move(jnp.concatenate(fc_first[:group], axis=1))
    fc_first, fc_second, out_part, grad_normed_mid = sums.fence(
        fc_first, fc_second, out_part, grad_normed_mid
    )

    fc_second = exchange_blocks([fc_second[k] for k in members])
    grad_middle_ln, grad_gain2, grad_bias2 = norm_pullback(
        normed2, inverse2, gain2, grad_normed_mid
    )
    grad_middle = cot_own.astype(FULL) + grad_middle_ln
    grad_mid_low = grad_middle.astype(LOW)
    grad_attended = product_nt(grad_mid_low, out_all).astype(LOW)
    out_term = product_tn(attended, grad_mid_low).astype(LOW)
    sums.move(jnp.concatenate(fc_first[group:], axis=1))
    fc_second, grad_middle, grad_mid_low, grad_attended, out_term = sums.fence(
        fc_second, grad_middle, grad_mid_low, grad_attended, out_term
    )

    out_share = scatter_rows(out_term)
    grad_query_low, grad_keys, grad_values = attend_back(
        queries, grad_attended, attended, score_totals, keys, keys.T, values, mask
    )
    sums.move(jnp.concatenate(fc_second[:group], axis=1))
    fc_second, grad_middle, grad_mid_low, grad_query_low, grad_keys, grad_values = sums.fence(
        fc_second, grad_middle, grad_mid_low, grad_query_low, grad_keys, grad_values
    )

    grad_pairs = jnp.concatenate([grad_keys, grad_values], axis=1)
    grad_pair = grad_pairs[:rows]
    for d in range(1, reach + 1):
        sent = grad_pairs[d * rows : (d + 1) * rows].astype(LOW)
        grad_pair = grad_pair + lax.ppermute(
            sent, "ctx", [(i + d, i) for i in range(ctx_count - d)]
        ).astype(FULL)
    pair_scaling = jnp.concatenate([jnp.full((HD,), SCALING, FULL), jnp.ones((HD,), FULL)])
    grad_pair_low = (grad_pair * pair_scaling).astype(LOW)
    grad_projected = jnp.concatenate([grad_query_low, grad_pair_low], axis=1)
    fc_second, grad_middle, grad_mid_low, grad_projected = sums.fence(
        fc_second, grad_middle, grad_mid_low, grad_projected
    )

    attn_term = product_tn(normed_in, grad_projected).astype(LOW)
    sums.move(jnp.concatenate(fc_second[group:], axis=1))
    grad_middle, grad_mid_low, grad_projected, attn_term = sums.fence(
        grad_middle, grad_mid_low, grad_projected, attn_term
    )

    attn_held = scatter_first(in_relative_order(attn_term))
    attn_held = scatter_second(attn_held)
    grad_normed_in = product_nt(grad_projected, attn_all)
    sums.move(out_share)
    grad_middle, grad_mid_low, grad_projected, attn_held, grad_normed_in = sums.fence(
        grad_middle, grad_mid_low, grad_projected, attn_held, grad_normed_in
    )

    attn_share = scatter_third(attn_held).astype(LOW)
    grad_tok_ln, grad_gain1, grad_bias1 = norm_pullback(normed1, inverse1, gain1, grad_normed_in)
    grad_tokens = (grad_middle + grad_tok_ln).astype(LOW)
    grad_projected_bias = jnp.sum(grad_projected.astype(FULL), axis=0)
    vector_terms = [
        grad_projected_bias[:width],
        jnp.sum(grad_mid_low.astype(FULL), axis=0),
        grad_gain1,
        grad_bias1,
        jnp.sum(cot_own.astype(FULL), axis=0),
        grad_gain2,
        grad_bias2,
    ]
    by_member = jnp.concatenate(
        [term.reshape(peers, depth_share) for term in vector_terms]
        + [grad_projected_bias[width + HD :].reshape(peers, HD // peers)],
        axis=1,
    )
    used = by_member.shape[1]
    by_member = jnp.pad(by_member, ((0, 0), (0, -used % 256))).reshape(peers, -1, 256)
    vector_rows = by_member.shape[1]
    by_member = jnp.pad(by_member, ((0, 0), (0, -vector_rows % 16), (0, 0))).astype(LOW)
    vector_pad = by_member.shape[1]
    vector_held = scatter_first(in_relative_order(by_member.reshape(peers * vector_pad, 256)))
    sums.move(attn_share[:, :width])
    vector_held, attn_share = sums.fence(vector_held, attn_share)

    vector_share = scatter_third(scatter_second(vector_held)).astype(LOW)
    grad_fc_bias = jnp.concatenate(
        [jnp.sum(part.astype(FULL), axis=0) for part in (grad_first, grad_second)]
    )
    fc_bias_rows = grad_fc_bias.astype(LOW).reshape(-1, 256)
    fc_rows = fc_bias_rows.shape[0]
    fc_bias_rows = jnp.pad(fc_bias_rows, ((0, -fc_rows % 16), (0, 0)))
    pair_share = attn_share[:, width:]
    sums.move(jnp.concatenate([pair_share, vector_share, fc_bias_rows], axis=0))
    (out_part,) = sums.fence(out_part)

    out_sum = scatter_rows(out_part).astype(FULL)
    output = (middle + (out_sum + proj_bias_all)).astype(LOW)
    sums.move()
    sums.fence()
    sums.move()
    sums.fence()
    sums.move()

    grad_proj = finish_rows(sums.ends, sums.results[:4])
    grad_fc = finish_columns(sums.ends, sums.results[4:8], half)
    grad_out, grad_query, last = [
        jnp.where(sums.ends[0] == 1, at_end, inside).astype(FULL)
        for at_end, inside in sums.results[8:]
    ]
    pair_count = pair_share.shape[0]
    vector_sum = last[pair_count : pair_count + vector_rows].reshape(-1)
    fc_at = pair_count + vector_share.shape[0]
    grad_fc_bias = last[fc_at : fc_at + fc_rows].reshape(-1)
    shares = [vector_sum[i * depth_share : (i + 1) * depth_share] for i in range(len(vectors))]
    value_share = vector_sum[len(vectors) * depth_share : used]
    return (
        output[None],
        grad_tokens[None],
        grad_query,
        last[:pair_count],
        grad_out,
        shares[0],
        value_share,
        shares[1],
        shares[2],
        shares[3],
        grad_fc,
        grad_proj,
        grad_fc_bias,
        shares[4],
        shares[5],
        shares[6],
    )


def solution(mesh):
    weight, vector, token = P("fsdp", None), P("fsdp"), P("fsdp", "ctx", None)
    return jax.shard_map(
        per_device,
        mesh=mesh,
        in_specs=(
            token,
            weight,
            weight,
            weight,
            weight,
            vector,
            vector,
            vector,
            vector,
            vector,
            weight,
            weight,
            vector,
            vector,
            vector,
            vector,
            token,
        ),
        out_specs=(
            token,
            token,
            weight,
            weight,
            weight,
            vector,
            vector,
            vector,
            vector,
            vector,
            weight,
            weight,
            vector,
            vector,
            vector,
            vector,
        ),
        check_vma=False,
    )
```

time: 1580 us -> 790 us (0.50)
  waiting for transfers between devices: 1160 us -> 247 us
  Pallas kernels: 0 us -> 212 us
  matrix products: 200 us -> 38.5 us
  blocking collectives: 121 us -> 0 us
  starting transfers between devices: 17 us -> 117 us
  local copies, waits for them, and re-layouts: 16.2 us -> 93.3 us
    reduce_scatter x5 -> x3, waiting for transfers between devices: 544 us -> 5.26 us  [scatter_rows(): return lax.psum_scatter(array, 'fsdp', scatter_dimension=0, tiled=True)]
    all_gather x5 -> x2, waiting for transfers between devices: 315 us -> 0.01 us  [gather_plain(): return lax.all_gather(own, 'fsdp', axis=0, tiled=True)]
    psum x1 -> x0, waiting for transfers between devices: 276 us -> none  [per_device(): lax.psum(shares[0].astype(jnp.bfloat16), 'ctx').astype(jnp.float32)]
    ppermute x7 -> x92, waiting for transfers between devices: 17.7 us -> 242 us  [the longest x58 165 us: swap(): return lax.ppermute(array, 'fsdp', [(i, i ^ bits) for i in range(8)])]
    pallas_call x0 -> x27, Pallas kernels: none -> 212 us  [the longest x13 50.3 us: combine(): pl.pallas_call(lambda at_end_ref, *refs: tick_body(at_end_ref, flags, *re...]
    ppermute x7 -> x92, starting transfers between devices: 16.4 us -> 117 us  [the longest x58 41.7 us: swap(): return lax.ppermute(array, 'fsdp', [(i, i ^ bits) for i in range(8)])]
    dot_general x29 -> x2, matrix products: 92.6 us -> 12.7 us  [product(): return jnp.dot(left_side, right_side, preferred_element_type=FULL)]
    all_gather x8 -> x0, blocking collectives: 69.5 us -> none  [the longest x1 10.3 us: per_device(): lax.all_gather(norm1_bias, 'fsdp', axis=0, tiled=True)]
  transfers between devices with their start and end apart: 18 -> 97, of which waited for: 12 -> 36; matrix products, arithmetic and copies ran while one was open for 10% -> 22% of each run, Pallas kernels for 0% -> 22%
where the time goes in v1:
time: 790 us; the launch traced here: 776 us
  waiting for transfers between devices  247 us (31%)
  Pallas kernels  212 us (27%)
  starting transfers between devices  117 us (15%)
  local copies, waits for them, and re-layouts  93.3 us (12%)
  other arithmetic  51.8 us (7%)
  matrix products  38.5 us (5%)
  between operations  15.8 us (2%)
    ppermute x58, waiting for transfers between devices, swap(): return lax.ppermute(array, 'fsdp', [(i, i ^ bits) for i in range(8)])  165 us
    pallas_call x13, Pallas kernels, combine(): pl.pallas_call(lambda at_end_ref, *refs: tick_body(at_end_ref, flags, *re...  50.3 us
    pallas_call x6, Pallas kernels, matmul(): pl.pallas_call(body, grid=(cols // step_cols, rows // step_rows), in_spec...  50.1 us
    ppermute x58, starting transfers between devices, swap(): return lax.ppermute(array, 'fsdp', [(i, i ^ bits) for i in range(8)])  41.7 us
    ppermute x8, waiting for transfers between devices, move(): from_end = from_middle = lax.ppermute(outgoing, 'ctx', inward + outward)  34.7 us
    unnamed x148, local copies, waits for them, and re-layouts  29.9 us
    pallas_call x2, Pallas kernels, feed_forward(): pl.pallas_call(feed_forward_body, grid=(rows // step_rows, count // step)...  29.7 us
    dynamic_update_slice x20, local copies, waits for them, and re-layouts, gather_rows(): whole = lax.dynamic_update_slice(whole, block, start)  27.6 us
  transfers between devices with their start and end apart: 97, of which 36 were waited for; matrix products, arithmetic and copies ran while one was open for 22% of the time, Pallas kernels for 22%

profile of v1, /device:TPU:0, one launch (start us, length us, event | category | flops | bytes accessed | tf_op | source)
XLA Modules:
  0.0 776.1 jit_solution(7760367287287115379)
XLA Ops:
  38.0 6.5 collective-permute-done.9
  47.9 37.7 %collective-permute-done.10 = bf16[256,2048]{1,0:T(8,128)(2,1)} collective-permute-done((bf16[256,2048]{1,0:T(8,128)(2,1)}, bf16[256,2048]{1,0:T(8,128)(2,1)}, u32[]{:S(2)}, u32[]{:S(2)}) %collective-permute-start.10) | collective-permute-done | bytes 1048608 | tf_op jit(solution)/shard_map/ppermute | solution.py:211
  90.9 8.5 %copy.79 = bf16[2048,2048]{1,0:T(8,128)(2,1)} copy(bf16[2048,2048]{1,0:T(8,128)(2,1)} %broadcast.99) | data formatting | bytes 16777216
  111.0 6.4 collective-permute-done.19
  125.7 6.5 fusion
  154.4 15.7 %attend.1 = (bf16[256,2048]{1,0:T(8,128)(2,1)}, f32[16,1,256]{2,1,0:T(1,128)}) custom-call(bf16[256,2048]{1,0:T(8,128)(2,1)} %slice.311.query_ref, bf16[1024,128]{1,0:T(8,128)(2,1)} %get-tuple-element.380.key_ref, bf16[128,1024]{1,0:T(8,128)(2,1)} %copy.33.value_t_ref, f32[1024,256]{1,0:T(8,128)} %fusion.30.mask_ref), custom_call_target="tpu_custom_call" | custom-call | tf_op jit(solution)/shard_map/attend/pallas_call | solution.py:451
  170.1 6.2 fusion.48
  188.5 35.7 %collective-permute-done.25 = bf16[256,2048]{1,0:T(8,128)(2,1)} collective-permute-done((bf16[256,2048]{1,0:T(8,128)(2,1)}, bf16[256,2048]{1,0:T(8,128)(2,1)}, u32[]{:S(2)}, u32[]{:S(2)}) %collective-permute-start.25) | collective-permute-done | bytes 1048608 | tf_op jit(solution)/shard_map/ppermute | solution.py:211
  232.4 8.7 %collective-permute-done.29 = bf16[128,2048]{1,0:T(8,128)(2,1)S(1)} collective-permute-done((bf16[128,2048]{1,0:T(8,128)(2,1)S(1)}, bf16[128,2048]{1,0:T(8,128)(2,1)S(1)}, u32[]{:S(2)}, u32[]{:S(2)}) %collective-permute-start.29) | collective-permute-done | bytes 524320 | tf_op jit(solution)/shard_map/ppermute | solution.py:211
  248.9 14.9 %feed_forward.2 = (bf16[2048,512]{1,0:T(8,128)(2,1)}, bf16[2048,512]{1,0:T(8,128)(2,1)}) custom-call(bf16[2048,2048]{1,0:T(8,128)(2,1)} %constant_dynamic-update-slice_fusion.26.mid_ref, bf16[2048,1024]{1,0:T(8,128)(2,1)} %bitcast.178, f32[1,1024]{1,0:T(1,128)} %bitcast.195, bf16[2048,2048]{1,0:T(8,128)(2,1)} %all-gather.5.cloned.1.call-done.cot_ref.right_ref, ...), custom_call_target="tpu_custom_call" | custom-call | tf_op jit(solution)/shard_map/feed_forward/pallas_call | solution.py:188
  263.8 5.9 matmul_tn.4.refs_0_
  279.4 14.9 %feed_forward.3 = (bf16[2048,512]{1,0:T(8,128)(2,1)}, bf16[2048,512]{1,0:T(8,128)(2,1)}) custom-call(bf16[2048,2048]{1,0:T(8,128)(2,1)} %constant_dynamic-update-slice_fusion.26.mid_ref, bf16[2048,1024]{1,0:T(8,128)(2,1)} %bitcast.179, f32[1,1024]{1,0:T(1,128)} %bitcast.196, bf16[2048,2048]{1,0:T(8,128)(2,1)} %all-gather.5.cloned.1.call-done.cot_ref.right_ref, ...), custom_call_target="tpu_custom_call" | custom-call | tf_op jit(solution)/shard_map/feed_forward/pallas_call | solution.py:188
  311.1 13.4 %matmul_nt.1 = bf16[2048,2048]{1,0:T(8,128)(2,1)} custom-call(bf16[2048,1024]{1,0:T(8,128)(2,1)} %pad_maximum_fusion.left_ref, bf16[2048,1024]{1,0:T(8,128)(2,1)} %bitcast.180), custom_call_target="tpu_custom_call" | custom-call | tf_op jit(solution)/shard_map/matmul_nt/pallas_call | solution.py:66
  324.5 5.9 matmul_tn.6.refs_4_.refs_0_
  337.8 12.2 %fc_gradient.2 = bf16[8,256,512]{2,1,0:T(8,128)(2,1)} custom-call(s32[8]{0:T(128)} %stack.26.order_ref, bf16[2048,2048]{1,0:T(8,128)(2,1)} %constant_dynamic-update-slice_fusion.26.mid_ref, bf16[2048,512]{1,0:T(8,128)(2,1)} %get-tuple-element.317.grad_ref), custom_call_target="tpu_custom_call" | custom-call | tf_op jit(solution)/shard_map/fc_gradient/pallas_call | solution.py:90
  350.0 11.4 %fc_gradient.3 = bf16[8,256,512]{2,1,0:T(8,128)(2,1)} custom-call(s32[8]{0:T(128)} %stack.26.order_ref, bf16[2048,2048]{1,0:T(8,128)(2,1)} %constant_dynamic-update-slice_fusion.26.mid_ref, bf16[2048,512]{1,0:T(8,128)(2,1)} %get-tuple-element.318.grad_ref), custom_call_target="tpu_custom_call" | custom-call | tf_op jit(solution)/shard_map/fc_gradient/pallas_call | solution.py:90
  380.7 8.6 %collective-permute-done.41 = bf16[256,512]{1,0:T(8,128)(2,1)S(1)} collective-permute-done((bf16[256,512]{1,0:T(8,128)(2,1)S(1)}, bf16[256,512]{1,0:T(8,128)(2,1)S(1)}, u32[]{:S(2)}, u32[]{:S(2)}) %collective-permute-start.41) | collective-permute-done | bytes 262176 | tf_op jit(solution)/shard_map/ppermute | solution.py:211
  400.8 13.2 %matmul_nn.1 = bf16[2048,2048]{1,0:T(8,128)(2,1)} custom-call(bf16[2048,1024]{1,0:T(8,128)(2,1)} %pad_maximum_fusion.1.left_ref, bf16[1024,2048]{1,0:T(8,128)(2,1)} %right_ref.1), custom_call_target="tpu_custom_call" | custom-call | tf_op jit(solution)/shard_map/matmul_nn/pallas_call | solution.py:66
  437.1 7.1 convolution_convert_fusion.2.grad_ref
  464.7 7.9 %collective-permute-done.53 = bf16[256,512]{1,0:T(8,128)(2,1)} collective-permute-done((bf16[256,512]{1,0:T(8,128)(2,1)}, bf16[256,512]{1,0:T(8,128)(2,1)}, u32[]{:S(2)}, u32[]{:S(2)}) %collective-permute-start.53) | collective-permute-done | bytes 262176 | tf_op jit(solution)/shard_map/ppermute | solution.py:211
  484.3 17.6 %attend_back.1 = (bf16[256,2048]{1,0:T(8,128)(2,1)}, f32[1024,128]{1,0:T(8,128)}, f32[1024,128]{1,0:T(8,128)}) custom-call(bf16[256,2048]{1,0:T(8,128)(2,1)} %slice.311.query_ref, bf16[256,2048]{1,0:T(8,128)(2,1)} %convolution_convert_fusion.2.grad_ref, bf16[256,2048]{1,0:T(8,128)(2,1)} %get-tuple-element.187.out_ref, ...), custom_call_target="tpu_custom_call" | custom-call | tf_op jit(solution)/shard_map/attend_back/pallas_call | solution.py:507
  514.8 6.2 collective-permute-done.61
  539.7 13.1 %collective-permute-done.62.refs_1_.refs_0_ = bf16[256,2048]{1,0:T(8,128)(2,1)S(1)} collective-permute-done((bf16[256,2048]{1,0:T(8,128)(2,1)S(1)}, bf16[256,2048]{1,0:T(8,128)(2,1)S(1)}, u32[]{:S(2)}, u32[]{:S(2)}) %collective-permute-start.62) | collective-permute-done | bytes 1048608 | tf_op jit(solution)/shard_map/ppermute | solution.py:402
  579.1 7.7 fusion.49
  587.4 6.0 collective-permute-done.69
  594.6 7.7 collective-permute-done.71
  620.0 15.3 %collective-permute-done.73 = bf16[256,2304]{1,0:T(8,128)(2,1)} collective-permute-done((bf16[256,2304]{1,0:T(8,128)(2,1)}, bf16[256,2304]{1,0:T(8,128)(2,1)}, u32[]{:S(2)}, u32[]{:S(2)}) %collective-permute-start.73) | collective-permute-done | bytes 1179680 | tf_op jit(solution)/shard_map/ppermute | solution.py:211
  664.3 16.8 %collective-permute-done.84.refs_1_.refs_6_ = bf16[256,2048]{1,0:T(8,128)(2,1)S(1)} collective-permute-done((bf16[256,2048]{1,0:T(8,128)(2,1)}, bf16[256,2048]{1,0:T(8,128)(2,1)S(1)}, u32[]{:S(2)}, u32[]{:S(2)}) %collective-permute-start.84) | collective-permute-done | bytes 1048608 | tf_op jit(solution)/shard_map/ppermute | solution.py:402
  689.2 10.6 %finish_rows.1 = f32[1024,2048]{1,0:T(8,128)} custom-call(s32[1]{0:T(128)} %bitcast.25.at_end_ref.ends_ref, bf16[256,2048]{1,0:T(8,128)(2,1)} %collective-permute-done.37.refs_1_.refs_0_, bf16[256,2048]{1,0:T(8,128)(2,1)} %get-tuple-element.219.refs_1_, bf16[256,2048]{1,0:T(8,128)(2,1)} %collective-permute-done.42.refs_1_.refs_2_, ...), custom_call_target="tpu_custom_call" | custom-call | tf_op jit(solution)/shard_map/finish_rows/pallas_call | solution.py:125
  701.5 6.8 collective-permute-start.86
  719.4 14.3 %finish_columns.1 = f32[256,8192]{1,0:T(8,128)} custom-call(s32[1]{0:T(128)} %bitcast.25.at_end_ref.ends_ref, s32[8]{0:T(128)} %stack.26.order_ref, bf16[256,2048]{1,0:T(8,128)(2,1)} %copy-done.22, bf16[256,2048]{1,0:T(8,128)(2,1)} %get-tuple-element.285.refs_1_, bf16[256,2048]{1,0:T(8,128)(2,1)} %collective-permute-done.64.refs_1_.refs_2_, ...), custom_call_target="tpu_custom_call" | custom-call | tf_op jit(solution)/shard_map/finish_columns/pallas_call | solution.py:161
  741.4 21.3 %collective-permute-done.90 = bf16[288,256]{1,0:T(8,128)(2,1)S(1)} collective-permute-done((bf16[288,256]{1,0:T(8,128)(2,1)}, bf16[288,256]{1,0:T(8,128)(2,1)S(1)}, u32[]{:S(2)}, u32[]{:S(2)}) %collective-permute-start.90) | collective-permute-done | bytes 147488 | tf_op jit(solution)/shard_map/ppermute | solution.py:407
  (500 shorter events, 369.6 us)
Async XLA Ops:
  7.3 118.4 %all-gather.3.cloned.1.call-start = ((), (), s32[]{:S(2)}) async-start(), calls=%async_computation.3 | async-start | bytes 10616832 | tf_op jit(solution)/shard_map/all_gather | solution.py:246
  9.7 239.1 %all-gather.5.cloned.1.call-start = ((), (), s32[]{:S(2)}) async-start(), calls=%async_computation.4 | async-start | bytes 9437184 | tf_op jit(solution)/shard_map/all_gather | solution.py:246
  44.5 41.1 %collective-permute-start.10 = (bf16[256,2048]{1,0:T(8,128)(2,1)}, bf16[256,2048]{1,0:T(8,128)(2,1)}, u32[]{:S(2)}, u32[]{:S(2)}) collective-permute-start(bf16[256,2048]{1,0:T(8,128)(2,1)} %param.21), channel_id=1, source_target_pairs={{0,2},{1,3},{2,0},{3,1},{4,6},{5,7},{6,4},{7,5},{8,10},{9,11},{10,... | collective-permute-start | bytes 3145736 | tf_op jit(solution)/shard_map/ppermute | solution.py:211
  44.6 41.2 %collective-permute-start.11 = (bf16[256,2048]{1,0:T(8,128)(2,1)}, bf16[256,2048]{1,0:T(8,128)(2,1)S(1)}, u32[]{:S(2)}, u32[]{:S(2)}) collective-permute-start(bf16[256,2048]{1,0:T(8,128)(2,1)} %param.21), channel_id=1, source_target_pairs={{0,4},{1,5},{2,6},{3,7},{4,0},{5,1},{6,2},{7,3},{8,12},{9,13},{10,... | collective-permute-start | bytes 3145736 | tf_op jit(solution)/shard_map/ppermute | solution.py:211
  45.5 40.3 %collective-permute-start.12 = (bf16[8,64,1024]{2,1,0:T(8,128)(2,1)S(1)}, bf16[8,64,1024]{2,1,0:T(8,128)(2,1)}, u32[]{:S(2)}, u32[]{:S(2)}) collective-permute-start(bf16[8,64,1024]{2,1,0:T(8,128)(2,1)S(1)} %bitcast_dynamic-update-slice_fusion.4), channel_id=1, source_target_pairs={{0,8},{8,16},{16,24},{24,0},{1,9},{9,17},{17,25},{25,1},{2,10},{10... | collective-permute-start | bytes 3145736 | tf_op jit(solution)/shard_map/ppermute | solution.py:335
  47.1 59.3 %collective-permute-start.16 = (bf16[256,2048]{1,0:T(8,128)(2,1)}, bf16[256,2048]{1,0:T(8,128)(2,1)}, u32[]{:S(2)}, u32[]{:S(2)}) collective-permute-start(bf16[256,2048]{1,0:T(8,128)(2,1)} %param.21), channel_id=1, source_target_pairs={{0,1},{1,0},{2,3},{3,2},{4,5},{5,4},{6,7},{7,6},{8,9},{9,8},{10,11... | collective-permute-start | bytes 3145736 | tf_op jit(solution)/shard_map/ppermute | solution.py:211
  85.8 33.1 %collective-permute-start.17 = (bf16[256,2048]{1,0:T(8,128)(2,1)}, bf16[256,2048]{1,0:T(8,128)(2,1)S(1)}, u32[]{:S(2)}, u32[]{:S(2)}) collective-permute-start(bf16[256,2048]{1,0:T(8,128)(2,1)} %collective-permute-done.10), channel_id=1, source_target_pairs={{0,1},{1,0},{2,3},{3,2},{4,5},{5,4},{6,7},{7,6},{8,9},{9,8},{10,11... | collective-permute-start | bytes 3145736 | tf_op jit(solution)/shard_map/ppermute | solution.py:211
  146.4 280.1 %reduce-scatter.4.cloned.1.call-start = ((), (), s32[]{:S(2)}) async-start(), calls=%async_computation.5 | async-start | bytes 9437184 | tf_op jit(solution)/shard_map/reduce_scatter | solution.py:264
  151.3 29.3 %collective-permute-start.23 = (bf16[8,64,1024]{2,1,0:T(8,128)(2,1)}, bf16[8,64,1024]{2,1,0:T(8,128)(2,1)}, u32[]{:S(2)}, u32[]{:S(2)}) collective-permute-start(bf16[8,64,1024]{2,1,0:T(8,128)(2,1)} %collective-permute-done.12), channel_id=1, source_target_pairs={{0,8},{8,16},{16,24},{24,0},{1,9},{9,17},{17,25},{25,1},{2,10},{10... | collective-permute-start | bytes 3145736 | tf_op jit(solution)/shard_map/ppermute | solution.py:335
  180.6 43.7 %collective-permute-start.25 = (bf16[256,2048]{1,0:T(8,128)(2,1)}, bf16[256,2048]{1,0:T(8,128)(2,1)}, u32[]{:S(2)}, u32[]{:S(2)}) collective-permute-start(bf16[256,2048]{1,0:T(8,128)(2,1)} %add_convert_fusion.6), channel_id=1, source_target_pairs={{0,2},{1,3},{2,0},{3,1},{4,6},{5,7},{6,4},{7,5},{8,10},{9,11},{10,... | collective-permute-start | bytes 3145736 | tf_op jit(solution)/shard_map/ppermute | solution.py:211
  182.4 46.6 %collective-permute-start.24 = (bf16[256,2048]{1,0:T(8,128)(2,1)}, bf16[256,2048]{1,0:T(8,128)(2,1)S(1)}, u32[]{:S(2)}, u32[]{:S(2)}) collective-permute-start(bf16[256,2048]{1,0:T(8,128)(2,1)} %add_convert_fusion.6), channel_id=1, source_target_pairs={{0,1},{1,0},{2,3},{3,2},{4,5},{5,4},{6,7},{7,6},{8,9},{9,8},{10,11... | collective-permute-start | bytes 3145736 | tf_op jit(solution)/shard_map/ppermute | solution.py:211
  182.4 45.9 %collective-permute-start.27 = (bf16[256,2048]{1,0:T(8,128)(2,1)}, bf16[256,2048]{1,0:T(8,128)(2,1)S(1)}, u32[]{:S(2)}, u32[]{:S(2)}) collective-permute-start(bf16[256,2048]{1,0:T(8,128)(2,1)} %add_convert_fusion.6), channel_id=1, source_target_pairs={{0,4},{1,5},{2,6},{3,7},{4,0},{5,1},{6,2},{7,3},{8,12},{9,13},{10,... | collective-permute-start | bytes 3145736 | tf_op jit(solution)/shard_map/ppermute | solution.py:211
  183.5 48.8 %collective-permute-start.33 = (bf16[8,64,1024]{2,1,0:T(8,128)(2,1)}, bf16[8,64,1024]{2,1,0:T(8,128)(2,1)S(1)}, u32[]{:S(2)}, u32[]{:S(2)}) collective-permute-start(bf16[8,64,1024]{2,1,0:T(8,128)(2,1)} %collective-permute-done.23), channel_id=1, source_target_pairs={{0,8},{8,16},{16,24},{24,0},{1,9},{9,17},{17,25},{25,1},{2,10},{10... | collective-permute-start | bytes 3145736 | tf_op jit(solution)/shard_map/ppermute | solution.py:335
  299.6 30.8 %collective-permute-start.35 = (bf16[256,2048]{1,0:T(8,128)(2,1)}, bf16[256,2048]{1,0:T(8,128)(2,1)}, u32[]{:S(2)}, u32[]{:S(2)}) collective-permute-start(bf16[256,2048]{1,0:T(8,128)(2,1)} %matmul_tn.5.refs_0_), channel_id=1, source_target_pairs={{0,8},{24,16},{1,9},{25,17},{2,10},{26,18},{3,11},{27,19},{4,12},{... | collective-permute-start | bytes 3145736 | tf_op jit(solution)/shard_map/ppermute | solution.py:405
  334.8 268.8 %reduce-scatter.6.cloned.1.call-start = ((), (), s32[]{:S(2)}) async-start(), calls=%async_computation.6 | async-start | bytes 9437184 | tf_op jit(solution)/shard_map/reduce_scatter | solution.py:264
  334.9 32.4 %collective-permute-start.37 = (bf16[256,2048]{1,0:T(8,128)(2,1)}, bf16[256,2048]{1,0:T(8,128)(2,1)}, u32[]{:S(2)}, u32[]{:S(2)}) collective-permute-start(bf16[256,2048]{1,0:T(8,128)(2,1)} %get-tuple-element.219.refs_1_), channel_id=1, source_target_pairs={{0,8},{24,16},{8,0},{16,24},{1,9},{25,17},{9,1},{17,25},{2,10},{26... | collective-permute-start | bytes 3145736 | tf_op jit(solution)/shard_map/ppermute | solution.py:402
  335.6 31.7 %collective-permute-start.38 = (bf16[256,2048]{1,0:T(8,128)(2,1)}, bf16[256,2048]{1,0:T(8,128)(2,1)}, u32[]{:S(2)}, u32[]{:S(2)}) collective-permute-start(bf16[256,2048]{1,0:T(8,128)(2,1)} %get-tuple-element.220.refs_2_), channel_id=1, source_target_pairs={{8,16},{16,8},{9,17},{17,9},{10,18},{18,10},{11,19},{19,11},{12,20... | collective-permute-start | bytes 3145736 | tf_op jit(solution)/shard_map/ppermute | solution.py:411
  376.2 40.1 %collective-permute-start.43 = (bf16[256,2048]{1,0:T(8,128)(2,1)}, bf16[256,2048]{1,0:T(8,128)(2,1)}, u32[]{:S(2)}, u32[]{:S(2)}) collective-permute-start(bf16[256,2048]{1,0:T(8,128)(2,1)} %get-tuple-element.229.refs_2_), channel_id=1, source_target_pairs={{8,16},{16,8},{9,17},{17,9},{10,18},{18,10},{11,19},{19,11},{12,20... | collective-permute-start | bytes 3145736 | tf_op jit(solution)/shard_map/ppermute | solution.py:411
  389.3 31.3 %collective-permute-start.44 = (bf16[256,512]{1,0:T(8,128)(2,1)}, bf16[256,512]{1,0:T(8,128)(2,1)}, u32[]{:S(2)}, u32[]{:S(2)}) collective-permute-start(bf16[256,512]{1,0:T(8,128)(2,1)} %get-tuple-element.367), channel_id=1, source_target_pairs={{0,4},{1,5},{2,6},{3,7},{4,0},{5,1},{6,2},{7,3},{8,12},{9,13},{10,... | collective-permute-start | bytes 786440 | tf_op jit(solution)/shard_map/ppermute | solution.py:211
  393.9 27.4 %collective-permute-start.45 = (bf16[256,512]{1,0:T(8,128)(2,1)}, bf16[256,512]{1,0:T(8,128)(2,1)}, u32[]{:S(2)}, u32[]{:S(2)}) collective-permute-start(bf16[256,512]{1,0:T(8,128)(2,1)} %get-tuple-element.366), channel_id=1, source_target_pairs={{0,5},{1,4},{2,7},{3,6},{4,1},{5,0},{6,3},{7,2},{8,13},{9,12},{10,... | collective-permute-start | bytes 786440 | tf_op jit(solution)/shard_map/ppermute | solution.py:211
  426.6 27.1 %collective-permute-start.48 = (bf16[256,2048]{1,0:T(8,128)(2,1)}, bf16[256,2048]{1,0:T(8,128)(2,1)}, u32[]{:S(2)}, u32[]{:S(2)}) collective-permute-start(bf16[256,2048]{1,0:T(8,128)(2,1)} %get-tuple-element.241.refs_5_), channel_id=1, source_target_pairs={{0,8},{24,16},{8,0},{16,24},{1,9},{25,17},{9,1},{17,25},{2,10},{26... | collective-permute-start | bytes 3145736 | tf_op jit(solution)/shard_map/ppermute | solution.py:402
  428.3 27.0 %collective-permute-start.49 = (bf16[256,2048]{1,0:T(8,128)(2,1)}, bf16[256,2048]{1,0:T(8,128)(2,1)}, u32[]{:S(2)}, u32[]{:S(2)}) collective-permute-start(bf16[256,2048]{1,0:T(8,128)(2,1)} %get-tuple-element.242.refs_2_), channel_id=1, source_target_pairs={{8,16},{16,8},{9,17},{17,9},{10,18},{18,10},{11,19},{19,11},{12,20... | collective-permute-start | bytes 3145736 | tf_op jit(solution)/shard_map/ppermute | solution.py:411
  477.2 289.5 %reduce-scatter.8.cloned.1.call-start = ((), (), s32[]{:S(2)}) async-start(), calls=%async_computation.7 | async-start | bytes 9437184 | tf_op jit(solution)/shard_map/reduce_scatter | solution.py:264
  477.2 27.8 %collective-permute-start.57 = (bf16[256,2048]{1,0:T(8,128)(2,1)}, bf16[256,2048]{1,0:T(8,128)(2,1)}, u32[]{:S(2)}, u32[]{:S(2)}) collective-permute-start(bf16[256,2048]{1,0:T(8,128)(2,1)} %get-tuple-element.253.refs_7_), channel_id=1, source_target_pairs={{0,8},{24,16},{8,0},{16,24},{1,9},{25,17},{9,1},{17,25},{2,10},{26... | collective-permute-start | bytes 3145736 | tf_op jit(solution)/shard_map/ppermute | solution.py:402
  526.0 26.7 %collective-permute-start.62 = (bf16[256,2048]{1,0:T(8,128)(2,1)S(1)}, bf16[256,2048]{1,0:T(8,128)(2,1)S(1)}, u32[]{:S(2)}, u32[]{:S(2)}) collective-permute-start(bf16[256,2048]{1,0:T(8,128)(2,1)S(1)} %copy-done.24), channel_id=1, source_target_pairs={{0,8},{24,16},{8,0},{16,24},{1,9},{25,17},{9,1},{17,25},{2,10},{26... | collective-permute-start | bytes 3145736 | tf_op jit(solution)/shard_map/ppermute | solution.py:402
  567.6 35.9 %collective-permute-start.64 = (bf16[256,2048]{1,0:T(8,128)(2,1)}, bf16[256,2048]{1,0:T(8,128)(2,1)}, u32[]{:S(2)}, u32[]{:S(2)}) collective-permute-start(bf16[256,2048]{1,0:T(8,128)(2,1)} %get-tuple-element.293.refs_3_), channel_id=1, source_target_pairs={{0,8},{24,16},{8,0},{16,24},{1,9},{25,17},{9,1},{17,25},{2,10},{26... | collective-permute-start | bytes 3145736 | tf_op jit(solution)/shard_map/ppermute | solution.py:402
  570.3 33.2 %collective-permute-start.65 = (bf16[256,2048]{1,0:T(8,128)(2,1)}, bf16[256,2048]{1,0:T(8,128)(2,1)}, u32[]{:S(2)}, u32[]{:S(2)}) collective-permute-start(bf16[256,2048]{1,0:T(8,128)(2,1)} %get-tuple-element.294.refs_2_), channel_id=1, source_target_pairs={{8,16},{16,8},{9,17},{17,9},{10,18},{18,10},{11,19},{19,11},{12,20... | collective-permute-start | bytes 3145736 | tf_op jit(solution)/shard_map/ppermute | solution.py:411
  607.9 27.5 %collective-permute-start.73 = (bf16[256,2304]{1,0:T(8,128)(2,1)}, bf16[256,2304]{1,0:T(8,128)(2,1)}, u32[]{:S(2)}, u32[]{:S(2)}) collective-permute-start(bf16[256,2304]{1,0:T(8,128)(2,1)} %pad_maximum_fusion.5), channel_id=1, source_target_pairs={{0,4},{1,5},{2,6},{3,7},{4,0},{5,1},{6,2},{7,3},{8,12},{9,13},{10,... | collective-permute-start | bytes 3538952 | tf_op jit(solution)/shard_map/ppermute | solution.py:211
  608.8 27.2 %collective-permute-start.72 = (bf16[256,2304]{1,0:T(8,128)(2,1)}, bf16[256,2304]{1,0:T(8,128)(2,1)}, u32[]{:S(2)}, u32[]{:S(2)}) collective-permute-start(bf16[256,2304]{1,0:T(8,128)(2,1)} %pad_maximum_fusion.4), channel_id=1, source_target_pairs={{0,2},{1,3},{2,0},{3,1},{4,6},{5,7},{6,4},{7,5},{8,10},{9,11},{10,... | collective-permute-start | bytes 3538952 | tf_op jit(solution)/shard_map/ppermute | solution.py:211
  616.6 26.5 %collective-permute-start.74 = (bf16[256,2048]{1,0:T(8,128)(2,1)}, bf16[256,2048]{1,0:T(8,128)(2,1)S(1)}, u32[]{:S(2)}, u32[]{:S(2)}) collective-permute-start(bf16[256,2048]{1,0:T(8,128)(2,1)} %get-tuple-element.305.refs_5_), channel_id=1, source_target_pairs={{0,8},{24,16},{8,0},{16,24},{1,9},{25,17},{9,1},{17,25},{2,10},{26... | collective-permute-start | bytes 3145736 | tf_op jit(solution)/shard_map/ppermute | solution.py:402
  699.9 38.8 %collective-permute-start.91 = (bf16[256,2048]{1,0:T(8,128)(2,1)}, bf16[256,2048]{1,0:T(8,128)(2,1)}, u32[]{:S(2)}, u32[]{:S(2)}) collective-permute-start(bf16[256,2048]{1,0:T(8,128)(2,1)} %get-tuple-element.331), channel_id=1, source_target_pairs={{8,0},{16,24},{9,1},{17,25},{10,2},{18,26},{11,3},{19,27},{12,4},{... | collective-permute-start | bytes 3145736 | tf_op jit(solution)/shard_map/ppermute | solution.py:407
  733.6 31.6 %collective-permute-start.88 = (bf16[256,2048]{1,0:T(8,128)(2,1)S(1)}, bf16[256,2048]{1,0:T(8,128)(2,1)S(1)}, u32[]{:S(2)}, u32[]{:S(2)}) collective-permute-start(bf16[256,2048]{1,0:T(8,128)(2,1)S(1)} %copy-done.19), channel_id=1, source_target_pairs={{8,0},{16,24},{9,1},{17,25},{10,2},{18,26},{11,3},{19,27},{12,4},{... | collective-permute-start | bytes 3145736 | tf_op jit(solution)/shard_map/ppermute | solution.py:407
  (120 other events, 1463.4 us)
Sparse Core Ops, SparseCore 0:
  10.6 85.9 all-gather.2
  146.5 75.5 all-gather.4
  334.9 91.5 reduce-scatter.3
  477.3 71.3 reduce-scatter.5
  687.4 70.0 reduce-scatter.7

commit v2 on v1

--- a/solution.py
+++ b/solution.py
@@ -42,7 +42,16 @@
 ROOMY = pltpu.CompilerParams(vmem_limit_bytes=56 * 2**20)
 
 
-def matmul(left_side, right_side, kind, step_rows=512, step_cols=2048, first=0, count=None):
+def matmul(
+    left_side,
+    right_side,
+    kind,
+    step_rows=512,
+    step_cols=2048,
+    first=0,
+    count=None,
+    out_type=LOW,
+):
     rows = count or (left_side.shape[1] if kind == "tn" else left_side.shape[0])
     depth = left_side.shape[0] if kind == "tn" else left_side.shape[1]
     cols = right_side.shape[0] if kind == "nt" else right_side.shape[1]
@@ -51,7 +60,7 @@
     at = first // step_rows
 
     def body(left_ref, right_ref, out_ref):
-        out_ref[...] = inner(left_ref[...], right_ref[...]).astype(LOW)
+        out_ref[...] = inner(left_ref[...], right_ref[...]).astype(out_type)
 
     left_spec = (
         pl.BlockSpec((depth, step_rows), lambda j, i: (0, at + i))
@@ -68,7 +77,7 @@
         grid=(cols // step_cols, rows // step_rows),
         in_specs=[left_spec, right_spec],
         out_specs=pl.BlockSpec((step_rows, step_cols), lambda j, i: (i, j)),
-        out_shape=jax.ShapeDtypeStruct((rows, cols), LOW),
+        out_shape=jax.ShapeDtypeStruct((rows, cols), out_type),
         compiler_params=ROOMY,
         cost_estimate=QUICK,
         name="matmul_" + kind,
@@ -79,10 +88,10 @@
     return jnp.stack([member_of(k) for k in range(lax.axis_size("fsdp"))]).astype(jnp.int32)
 
 
-def fc_gradient(mid_all, grad_part):
+def fc_gradient(mid_all, grad_pre):
     peers = lax.axis_size("fsdp")
     rows, width = mid_all.shape
-    step, cols = width // peers, grad_part.shape[1]
+    step, cols = width // peers, grad_pre.shape[1]
 
     def body(order_ref, mid_ref, grad_ref, out_ref):
         out_ref[0] = product_tn(mid_ref[...], grad_ref[...]).astype(LOW)
@@ -102,74 +111,68 @@
         compiler_params=ROOMY,
         cost_estimate=QUICK,
         name="fc_gradient",
-    )(member_order(), mid_all, grad_part)
-
-
-def finish_rows(ends, pairs):
-    rows, cols = pairs[0][0].shape
-    step = rows // 2 if rows % 32 == 0 else rows
-
-    def body(ends_ref, *refs):
-        for c in range(len(pairs)):
-            @pl.when(pl.program_id(0) == c)
-            def _():
-                chosen = jnp.where(ends_ref[0] == 1, refs[2 * c][...], refs[2 * c + 1][...])
-                refs[-1][...] = chosen.astype(FULL)
-
-    def spec(c):
-        last = rows // step - 1
-        return pl.BlockSpec(
-            (step, cols), lambda i, j: (jnp.where(i == c, j, jnp.where(i > c, last, 0)), 0)
-        )
+    )(member_order(), mid_all, grad_pre)
+
+
+def attn_gradient(normed_in, grad_projected, extra):
+    peers = lax.axis_size("fsdp")
+    rows, width = normed_in.shape
+    step, cols, more = width // peers, grad_projected.shape[1], extra.shape[1]
+
+    def body(normed_ref, grad_ref, extra_ref, out_ref):
+        out_ref[0, :step] = product_tn(normed_ref[...], grad_ref[...]).astype(LOW)
+        out_ref[0, step:] = extra_ref[0]
 
     return pl.pallas_call(
         body,
-        grid=(len(pairs), rows // step),
-        in_specs=[pl.BlockSpec(memory_space=pltpu.SMEM)]
-        + [spec(c) for c in range(len(pairs)) for unused in range(2)],
-        out_specs=pl.BlockSpec((step, cols), lambda i, j: (i * (rows // step) + j, 0)),
-        out_shape=jax.ShapeDtypeStruct((rows * len(pairs), cols), FULL),
+        grid=(peers,),
+        in_specs=[
+            pl.BlockSpec((rows, step), lambda k: (0, k)),
+            pl.BlockSpec((rows, cols), lambda k: (0, 0)),
+            pl.BlockSpec((1, more, cols), lambda k: (k, 0, 0)),
+        ],
+        out_specs=pl.BlockSpec((1, step + more, cols), lambda k: (k, 0, 0)),
+        out_shape=jax.ShapeDtypeStruct((peers, step + more, cols), LOW),
         compiler_params=ROOMY,
         cost_estimate=QUICK,
-        name="finish_rows",
-    )(ends, *[array for pair in pairs for array in pair])
-
-
-def finish_columns(ends, pairs, step):
-    peers = lax.axis_size("fsdp")
+        name="attn_gradient",
+    )(normed_in, grad_projected, extra)
+
+
+def finish(ends, pairs, across, parts=1):
     rows, cols = pairs[0][0].shape
-    blocks = cols // step
-    rounds = len(pairs) * blocks // peers
+    step = cols // parts
 
     def body(ends_ref, order_ref, *refs):
         for c in range(len(pairs)):
             @pl.when(pl.program_id(0) == c)
             def _():
-                chosen = jnp.where(ends_ref[0] == 1, refs[2 * c][...], refs[2 * c + 1][...])
-                refs[-1][...] = chosen.astype(FULL)
-
-    def spec(c):
-        return pl.BlockSpec(
-            (rows, step),
-            lambda i, j, ends, order: (0, jnp.where(i == c, j, jnp.where(i > c, blocks - 1, 0))),
-        )
-
-    def placed(i, j, ends, order):
-        at = i * blocks + j
-        return (0, order[lax.rem(at, peers)] * rounds + at // peers)
-
+                for j in range(parts):
+                    at = (slice(None), slice(j * step, (j + 1) * step))
+                    chosen = jnp.where(ends_ref[0] == 1, refs[2 * c][at], refs[2 * c + 1][at])
+                    place = j
+                    if parts > 1:
+                        place = lax.rem(order_ref[(c % across) * parts + j], parts)
+                    start = pl.multiple_of(place * step, step)
+                    refs[-1][:, pl.ds(start, step)] = chosen.astype(FULL)
+
+    def placed(c, ends, order):
+        row, at = c // across, lax.rem(c, across)
+        return (row, order[at * parts] // parts if parts > 1 else at)
+
+    whole = pl.BlockSpec((rows, cols), lambda c, ends, order: (0, 0))
     return pl.pallas_call(
         body,
         grid_spec=pltpu.PrefetchScalarGridSpec(
             num_scalar_prefetch=2,
-            grid=(len(pairs), blocks),
-            in_specs=[spec(c) for c in range(len(pairs)) for unused in range(2)],
-            out_specs=pl.BlockSpec((rows, step), placed),
+            grid=(len(pairs),),
+            in_specs=[whole] * (2 * len(pairs)),
+            out_specs=pl.BlockSpec((rows, cols), placed),
         ),
-        out_shape=jax.ShapeDtypeStruct((rows, cols * len(pairs)), FULL),
+        out_shape=jax.ShapeDtypeStruct((rows * len(pairs) // across, cols * across), FULL),
         compiler_params=ROOMY,
         cost_estimate=QUICK,
-        name="finish_columns",
+        name="finish",
     )(ends, member_order(), *[array for pair in pairs for array in pair])
 
 
@@ -179,28 +182,35 @@
     grad_ref[...] = (product_nt(cot_ref[...], proj_ref[...]) * slope).astype(LOW)
 
 
-def feed_forward(mid_all, fc_all, bias, cot_all, proj, first, count):
+def feed_forward(mid_all, fc_all, bias, cot_all, proj, part, made=None):
     rows, width = mid_all.shape
-    step_rows, step = math.gcd(512, rows), math.gcd(512, count)
-    at = first // step
-    by_row = pl.BlockSpec((step_rows, width), lambda i, j: (i, 0))
-    made = pl.BlockSpec((step_rows, step), lambda i, j: (i, j))
+    cols = fc_all.shape[1]
+    step_rows, step = math.gcd(512, rows), cols // 2
+    by_row = pl.BlockSpec((step_rows, width), lambda i: (i, 0))
+    placed = pl.BlockSpec((step_rows, step), lambda i: (i, part))
+    held = [] if made is None else list(made)
+
+    def body(*refs):
+        feed_forward_body(*refs[:5], *refs[-2:])
+
     return pl.pallas_call(
-        feed_forward_body,
-        grid=(rows // step_rows, count // step),
+        body,
+        grid=(rows // step_rows,),
         in_specs=[
             by_row,
-            pl.BlockSpec((width, step), lambda i, j: (0, at + j)),
-            pl.BlockSpec((1, step), lambda i, j: (0, at + j)),
+            pl.BlockSpec((width, step), lambda i: (0, part)),
+            pl.BlockSpec((1, step), lambda i: (0, part)),
             by_row,
-            pl.BlockSpec((step, width), lambda i, j: (at + j, 0)),
-        ],
-        out_specs=[made, made],
-        out_shape=[jax.ShapeDtypeStruct((rows, count), LOW)] * 2,
+            pl.BlockSpec((step, width), lambda i: (part, 0)),
+        ]
+        + [pl.BlockSpec(memory_space=pl.ANY)] * len(held),
+        out_specs=[placed, placed],
+        out_shape=[jax.ShapeDtypeStruct((rows, cols), LOW)] * 2,
+        input_output_aliases={5: 0, 6: 1} if held else {},
         compiler_params=ROOMY,
         cost_estimate=QUICK,
         name="feed_forward",
-    )(mid_all, fc_all, bias[None], cot_all, proj)
+    )(mid_all, fc_all, bias[None], cot_all, proj, *held)
 
 
 def by_xor():
@@ -219,26 +229,44 @@
     return swap(own, 2), swap(own, 4)
 
 
-def gather_rows(own, near, whole):
+def placed_own(own):
+    def body(order_ref, own_ref, out_ref):
+        out_ref[...] = own_ref[...]
+
+    return pl.pallas_call(
+        body,
+        grid_spec=pltpu.PrefetchScalarGridSpec(
+            num_scalar_prefetch=1,
+            grid=(1,),
+            in_specs=[pl.BlockSpec(own.shape, lambda k, order: (0, 0))],
+            out_specs=pl.BlockSpec(own.shape, lambda k, order: (order[0], 0)),
+        ),
+        out_shape=jax.ShapeDtypeStruct((8 * own.shape[0], own.shape[1]), own.dtype),
+        compiler_params=ROOMY,
+        cost_estimate=QUICK,
+        name="placed_own",
+    )(member_order(), own)
+
+
+def gather_rows(own, near):
     count = own.shape[0]
     half = count // 2
     along_x, along_y = near
     first_half, second_half = swap(along_x[:half], 4), swap(along_y[half:], 2)
     placed = [
-        (0, 0, own),
         (1, 0, swap(own, 1)),
         (2, 0, along_x),
+        (4, 0, along_y),
         (3, 0, swap(along_x, 1)),
-        (4, 0, along_y),
         (5, 0, swap(along_y, 1)),
         (6, 0, first_half),
         (6, half, second_half),
         (7, 0, swap(first_half, 1)),
         (7, half, swap(second_half, 1)),
     ]
+    whole = placed_own(own)
     for k, offset, block in placed:
-        start = (member_of(k) * count + offset,) + (0,) * (own.ndim - 1)
-        whole = lax.dynamic_update_slice(whole, block, start)
+        whole = lax.dynamic_update_slice(whole, block, (member_of(k) * count + offset, 0))
     return whole
 
 
@@ -253,55 +281,18 @@
     return relative(held, 0)
 
 
-def add_low(first, *others):
-    total = first.astype(FULL)
-    for other in others:
-        total = total + other.astype(FULL)
-    return total.astype(LOW)
-
-
 def scatter_rows(array):
     return lax.psum_scatter(array, "fsdp", scatter_dimension=0, tiled=True)
-
-
-def in_relative_order(array):
-    step = array.shape[0] // lax.axis_size("fsdp")
-    return [
-        lax.dynamic_slice_in_dim(array, member_of(k) * step, step, 0)
-        for k in range(lax.axis_size("fsdp"))
-    ]
-
-
-def scatter_first(blocks):
-    if not by_xor():
-        return blocks
-    return [add_low(blocks[k], swap(blocks[k + 1], 1)) for k in (0, 2, 4, 6)]
-
-
-def scatter_second(held):
-    if not by_xor():
-        return held
-    mine, along_x, along_y, across = held
-    half = mine.shape[0] // 2
-    upper, lower = swap(across[:half], 2), swap(across[half:], 4)
-    along_y = jnp.concatenate([add_low(along_y[:half], upper), along_y[half:]], axis=0)
-    along_x = jnp.concatenate([along_x[:half], add_low(along_x[half:], lower)], axis=0)
-    return [mine, along_x, along_y]
-
-
-def scatter_third(held):
-    if not by_xor():
-        return scatter_rows(jnp.concatenate(held, axis=0)).astype(FULL)
-    mine, along_x, along_y = held
-    from_x, from_y = swap(along_x, 2), swap(along_y, 4)
-    return mine.astype(FULL) + from_x.astype(FULL) + from_y.astype(FULL)
 
 
 def exchange_blocks(blocks):
     if not by_xor():
         moved = lax.all_to_all(jnp.stack(blocks), "fsdp", 0, 0, tiled=True)
         return [moved[k] for k in range(len(blocks))]
-    return [blocks[0]] + [swap(blocks[k], k) for k in range(1, 8)]
+    moved = {0: blocks[0]}
+    for k in (2, 4, 6, 1, 3, 5, 7):
+        moved[k] = swap(blocks[k], k)
+    return [moved[k] for k in range(8)]
 
 
 def relative(array, axis):
@@ -369,21 +360,20 @@
         self.ends = ((place == 0) | (place == 3)).astype(jnp.int32)[None]
         self.state = (first, None, None, first)
         self.results = []
+        self.fenced = 0
 
     def combine(self, **arrays):
         given = {name: array for name, array in arrays.items() if array is not None}
         shape = next(iter(given.values())).shape
         count = ("fresh" in given) + ("middle" in given)
-        pieces = 4 if shape[0] % 64 == 0 else 1
-        spec = pl.BlockSpec((shape[0] // pieces, shape[1]), lambda i: (i, 0))
+        spec = pl.BlockSpec(memory_space=pltpu.VMEM)
         flags = [(name, name in given) for name in arrays]
         return pl.pallas_call(
             lambda at_end_ref, *refs: tick_body(at_end_ref, flags, *refs),
-            grid=(pieces,),
             in_specs=[pl.BlockSpec(memory_space=pltpu.SMEM)] + [spec] * len(given),
             out_specs=[spec] * count,
             out_shape=[jax.ShapeDtypeStruct(shape, LOW)] * count,
-            compiler_params=ROOMY,
+            compiler_params=pltpu.CompilerParams(vmem_limit_bytes=32 * 2**20),
             cost_estimate=QUICK,
             name="tick",
         )(self.ends, *given.values())
@@ -428,7 +418,10 @@
         fresh, middle, outgoing, incoming = self.state
         joined = outgoing is not None and outgoing is incoming
         held = (fresh, middle, outgoing, None if joined or incoming is fresh else incoming)
-        held, values = lax.optimization_barrier((held, values))
+        made = self.results[self.fenced :]
+        held, made, values = lax.optimization_barrier((held, made, values))
+        self.results[self.fenced :] = made
+        self.fenced = len(self.results)
         incoming = held[2] if joined else held[0]
         self.state = (held[0], held[1], held[2], incoming)
         return values
@@ -596,19 +589,17 @@
     if spelled:
         packed = gather_small(vectors_own)
         held = columns_held(exchange_blocks(columns_sent(fc_weight)))
-        blank_out, blank_mid = jnp.zeros((2, peers * depth_share, width), LOW)
-        packed, held, blank_out, blank_mid = lax.optimization_barrier(
-            (packed, held, blank_out, blank_mid)
+        packed, held = lax.optimization_barrier((packed, held))
+        held_parts = [held, next_plane(held)]
+        attn_all, packed, held_parts, out_sent = lax.optimization_barrier(
+            (attn_all, packed, held_parts, out_weight)
         )
-        out_near = near_rows(tie(out_weight, packed))
-        held_parts = [held, next_plane(held)]
-        out_near, held_parts, cot_sent = lax.optimization_barrier(
-            (out_near, held_parts, cot_own)
-        )
-        out_all = gather_rows(out_weight, out_near, blank_out)
+        out_near = near_rows(out_sent)
+        cot_all = gather_plain(tie(cot_own, attn_all))
     else:
         packed = lax.all_gather(vectors_own, "fsdp", axis=0)
         out_all = gather_plain(out_weight)
+        cot_all = gather_plain(cot_own)
         fc_all = lax.all_to_all(fc_weight, "fsdp", 1, 0, tiled=True)
     small = [
         packed[:, i * depth_share : (i + 1) * depth_share].reshape(-1).astype(FULL)
@@ -629,13 +620,9 @@
         for d in range(1, reach + 1)
     ]
     if spelled:
-        held_parts, pairs, out_all, cot_sent = lax.optimization_barrier(
-            (held_parts, pairs, out_all, cot_sent)
-        )
+        held_parts, pairs, out_near = lax.optimization_barrier((held_parts, pairs, out_near))
         held_parts = held_parts + [next_plane(held_parts[-1])]
-        cot_all = gather_plain(cot_sent)
-    else:
-        cot_all = gather_plain(cot_own)
+        out_all = gather_rows(out_sent, out_near)
     pair_rows = jnp.concatenate(pairs, axis=0)
     seg_row = segments[0]
     query_first = ctx_index * rows
@@ -667,55 +654,46 @@
         held_parts, normed_mid = lax.optimization_barrier((held_parts, normed_mid))
         held_parts = held_parts + [next_plane(held_parts[-1])]
         fc_all = columns_whole(held_parts)
-        mid_all = gather_rows(normed_mid, near_rows(normed_mid), blank_mid)
+        mid_all = gather_rows(normed_mid, near_rows(normed_mid))
     else:
         mid_all = gather_plain(normed_mid)
     fc_bias_own = fc_bias.astype(FULL)
-    half = ff_share // 2
-    piece = half // 2
+    piece = ff_share // 4
     ff_args = (mid_all, fc_all, fc_bias_own, cot_all, proj_weight)
-    hidden_first, grad_first = feed_forward(*ff_args, 0, half)
-
-    def proj_term(hidden_part, first):
-        return matmul(hidden_part, cot_all, "tn", 256, 1024, first, piece)
-
-    sums = SumOverCtx(proj_term(hidden_first, 0))
-    mid_all, cot_all, fc_all, hidden_first, grad_first = sums.fence(
-        mid_all, cot_all, fc_all, hidden_first, grad_first
-    )
-
-    ff_args = (mid_all, fc_all, fc_bias_own, cot_all, proj_weight)
-    hidden_second, grad_second = feed_forward(*ff_args, half, half)
-    sums.move(proj_term(hidden_first, piece))
-    mid_all, cot_all, grad_first, grad_second, hidden_first, hidden_second = sums.fence(
-        mid_all, cot_all, grad_first, grad_second, hidden_first, hidden_second
-    )
-
-    grad_pre = jnp.concatenate([grad_first, grad_second], axis=1)
+    hidden, grad_pre = feed_forward(*ff_args, 0)
+
+    def proj_term(j):
+        return matmul(hidden, cot_all, "tn", 256, 1024, j * piece, piece)
+
+    sums = SumOverCtx(proj_term(0))
+    ff_args, hidden, grad_pre = sums.fence(ff_args, hidden, grad_pre)
+
+    mid_all, fc_all, unused, cot_all, unused = ff_args
+    later = proj_term(1)
+    hidden, grad_pre = feed_forward(*ff_args, 1, (hidden, grad_pre))
+    sums.move(later)
+    mid_all, fc_all, cot_all, hidden, grad_pre = sums.fence(
+        mid_all, fc_all, cot_all, hidden, grad_pre
+    )
+
     grad_mid_part = matmul(grad_pre, fc_all, "nt")
-    sums.move(proj_term(hidden_second, 0))
-    mid_all, cot_all, grad_first, grad_second, hidden_second, grad_mid_part = sums.fence(
-        mid_all, cot_all, grad_first, grad_second, hidden_second, grad_mid_part
+    sums.move(proj_term(2))
+    mid_all, cot_all, hidden, grad_pre, grad_mid_part = sums.fence(
+        mid_all, cot_all, hidden, grad_pre, grad_mid_part
     )
 
     grad_normed_mid = scatter_rows(grad_mid_part)
-    fc_first = fc_gradient(mid_all, grad_first)
-    fc_second = fc_gradient(mid_all, grad_second)
-    sums.move(proj_term(hidden_second, piece))
-    grad_first, grad_second, hidden_second, fc_first, fc_second = sums.fence(
-        grad_first, grad_second, hidden_second, fc_first, fc_second
-    )
-
-    hidden = jnp.concatenate([hidden_first, hidden_second], axis=1)
-    out_part = matmul(hidden, proj_weight, "nn")
-    fc_first = exchange_blocks([fc_first[k] for k in members])
-    group = peers // 2
+    fc_terms = fc_gradient(mid_all, grad_pre)
+    sums.move(proj_term(3))
+    hidden, grad_pre, fc_terms = sums.fence(hidden, grad_pre, fc_terms)
+
+    share_half, group = depth_share // 2, peers // 2
+    fc_first = exchange_blocks([fc_terms[k, :share_half] for k in members])
     sums.move(jnp.concatenate(fc_first[:group], axis=1))
-    fc_first, fc_second, out_part, grad_normed_mid = sums.fence(
-        fc_first, fc_second, out_part, grad_normed_mid
-    )
-
-    fc_second = exchange_blocks([fc_second[k] for k in members])
+    fc_first, fc_terms, grad_normed_mid = sums.fence(fc_first, fc_terms, grad_normed_mid)
+    grad_normed_mid = grad_normed_mid.astype(FULL)
+
+    fc_second = exchange_blocks([fc_terms[k, share_half:] for k in members])
     grad_middle_ln, grad_gain2, grad_bias2 = norm_pullback(
         normed2, inverse2, gain2, grad_normed_mid
     )
@@ -746,28 +724,17 @@
         ).astype(FULL)
     pair_scaling = jnp.concatenate([jnp.full((HD,), SCALING, FULL), jnp.ones((HD,), FULL)])
     grad_pair_low = (grad_pair * pair_scaling).astype(LOW)
-    grad_projected = jnp.concatenate([grad_query_low, grad_pair_low], axis=1)
-    fc_second, grad_middle, grad_mid_low, grad_projected = sums.fence(
-        fc_second, grad_middle, grad_mid_low, grad_projected
-    )
-
-    attn_term = product_tn(normed_in, grad_projected).astype(LOW)
-    sums.move(jnp.concatenate(fc_second[group:], axis=1))
-    grad_middle, grad_mid_low, grad_projected, attn_term = sums.fence(
-        grad_middle, grad_mid_low, grad_projected, attn_term
-    )
-
-    attn_held = scatter_first(in_relative_order(attn_term))
-    attn_held = scatter_second(attn_held)
-    grad_normed_in = product_nt(grad_projected, attn_all)
-    sums.move(out_share)
-    grad_middle, grad_mid_low, grad_projected, attn_held, grad_normed_in = sums.fence(
-        grad_middle, grad_mid_low, grad_projected, attn_held, grad_normed_in
-    )
-
-    attn_share = scatter_third(attn_held).astype(LOW)
+    grad_normed_in = matmul(grad_query_low, attn_all, "nt", 256, 512, out_type=FULL)
+    fc_second, grad_middle, grad_mid_low, grad_query_low, grad_pair_low, grad_normed_in = (
+        sums.fence(
+            fc_second, grad_middle, grad_mid_low, grad_query_low, grad_pair_low, grad_normed_in
+        )
+    )
+
+    grad_normed_in = grad_normed_in + product_nt(grad_pair_low, attn_all[:, width:])
     grad_tok_ln, grad_gain1, grad_bias1 = norm_pullback(normed1, inverse1, gain1, grad_normed_in)
     grad_tokens = (grad_middle + grad_tok_ln).astype(LOW)
+    grad_projected = jnp.concatenate([grad_query_low, grad_pair_low], axis=1)
     grad_projected_bias = jnp.sum(grad_projected.astype(FULL), axis=0)
     vector_terms = [
         grad_projected_bias[:width],
@@ -783,51 +750,56 @@
         + [grad_projected_bias[width + HD :].reshape(peers, HD // peers)],
         axis=1,
     )
-    used = by_member.shape[1]
-    by_member = jnp.pad(by_member, ((0, 0), (0, -used % 256))).reshape(peers, -1, 256)
-    vector_rows = by_member.shape[1]
-    by_member = jnp.pad(by_member, ((0, 0), (0, -vector_rows % 16), (0, 0))).astype(LOW)
-    vector_pad = by_member.shape[1]
-    vector_held = scatter_first(in_relative_order(by_member.reshape(peers * vector_pad, 256)))
-    sums.move(attn_share[:, :width])
-    vector_held, attn_share = sums.fence(vector_held, attn_share)
-
-    vector_share = scatter_third(scatter_second(vector_held)).astype(LOW)
-    grad_fc_bias = jnp.concatenate(
-        [jnp.sum(part.astype(FULL), axis=0) for part in (grad_first, grad_second)]
-    )
-    fc_bias_rows = grad_fc_bias.astype(LOW).reshape(-1, 256)
-    fc_rows = fc_bias_rows.shape[0]
-    fc_bias_rows = jnp.pad(fc_bias_rows, ((0, -fc_rows % 16), (0, 0)))
-    pair_share = attn_share[:, width:]
-    sums.move(jnp.concatenate([pair_share, vector_share, fc_bias_rows], axis=0))
+    used, extra_cols = by_member.shape[1], grad_projected.shape[1]
+    by_member = jnp.pad(by_member, ((0, 0), (0, extra_cols - used)))
+    grad_fc_bias = jnp.pad(jnp.sum(grad_pre.astype(FULL), axis=0), (0, extra_cols - ff_share))
+    is_own = jnp.arange(peers)[:, None] == lax.axis_index("fsdp")
+    fc_bias_rows = jnp.where(is_own, grad_fc_bias[None], 0.0)
+    extra = jnp.stack([by_member, fc_bias_rows], axis=1).astype(LOW)
+    extra = jnp.pad(extra, ((0, 0), (0, 14), (0, 0)))
+    attn_term = attn_gradient(normed_in, grad_projected, extra)
+    attn_rows = attn_term.shape[1]
+    attn_term = attn_term.reshape(peers * attn_rows, extra_cols)
+    sums.move(jnp.concatenate(fc_second[group:], axis=1))
+    hidden, attn_term = sums.fence(hidden, attn_term)
+
+    attn_share = scatter_rows(attn_term)
+    out_part = matmul(hidden, proj_weight, "nn")
+    sums.move(out_share)
     (out_part,) = sums.fence(out_part)
+
+    grad_proj = finish(sums.ends, sums.results[:4], 1)
+    attn_cut = (attn_rows + 16) // 32 * 16
+    sums.move(attn_share[:attn_cut])
+    grad_proj, out_part = sums.fence(grad_proj, out_part)
 
     out_sum = scatter_rows(out_part).astype(FULL)
     output = (middle + (out_sum + proj_bias_all)).astype(LOW)
+    sums.move(attn_share[attn_cut:])
+    sums.fence()
+    if spelled:
+        grad_fc = finish(sums.ends, sums.results[4:8], 2, group)
     sums.move()
     sums.fence()
     sums.move()
     sums.fence()
     sums.move()
-
-    grad_proj = finish_rows(sums.ends, sums.results[:4])
-    grad_fc = finish_columns(sums.ends, sums.results[4:8], half)
-    grad_out, grad_query, last = [
+    sums.fence()
+    if not spelled:
+        grad_fc = finish(sums.ends, sums.results[4:8], 2, group)
+    grad_out, attn_first, attn_second = [
         jnp.where(sums.ends[0] == 1, at_end, inside).astype(FULL)
         for at_end, inside in sums.results[8:]
     ]
-    pair_count = pair_share.shape[0]
-    vector_sum = last[pair_count : pair_count + vector_rows].reshape(-1)
-    fc_at = pair_count + vector_share.shape[0]
-    grad_fc_bias = last[fc_at : fc_at + fc_rows].reshape(-1)
+    attn_sums = jnp.concatenate([attn_first, attn_second], axis=0)
+    vector_sum, grad_fc_bias = attn_sums[depth_share], attn_sums[depth_share + 1, :ff_share]
     shares = [vector_sum[i * depth_share : (i + 1) * depth_share] for i in range(len(vectors))]
     value_share = vector_sum[len(vectors) * depth_share : used]
     return (
         output[None],
         grad_tokens[None],
-        grad_query,
-        last[:pair_count],
+        attn_sums[:depth_share, :width],
+        attn_sums[:depth_share, width:],
         grad_out,
         shares[0],
         value_share,

time: 790 us -> 730 us (0.924)
  Pallas kernels: 212 us -> 189 us
  local copies, waits for them, and re-layouts: 93.3 us -> 75.1 us
  other arithmetic: 51.8 us -> 34 us
  starting transfers between devices: 117 us -> 129 us
  matrix products: 38.5 us -> 29.7 us
    ppermute x58 -> x42, waiting for transfers between devices: 165 us -> 106 us  [swap(): return lax.ppermute(array, 'fsdp', [(i, i ^ bits) for i in range(8)])]
    ppermute x3 -> x7, waiting for transfers between devices: 4.32 us -> 36.7 us  [move(): from_end = lax.ppermute(incoming, 'ctx', inward)]
    pallas_call x13 -> x16, Pallas kernels: 50.3 us -> 20.1 us  [combine(): pl.pallas_call(lambda at_end_ref, *refs: tick_body(at_end_ref, flags, *re...]
    reduce_scatter x3 -> x4, waiting for transfers between devices: 5.26 us -> 28.9 us  [scatter_rows(): return lax.psum_scatter(array, 'fsdp', scatter_dimension=0, tiled=True)]
    ppermute x3 -> x7, starting transfers between devices: 16 us -> 39 us  [move(): from_end = lax.ppermute(incoming, 'ctx', inward)]
    ppermute x3, waiting for transfers between devices: 2.49 us -> 25.1 us  [next_plane(): lax.ppermute(held, 'ctx', [(i, (i + 1) % planes) for i in range(planes)])]
    ppermute x8 -> x4, waiting for transfers between devices: 34.7 us -> 12.7 us  [move(): from_end = from_middle = lax.ppermute(outgoing, 'ctx', inward + outward)]
    unnamed x148 -> x172, local copies, waits for them, and re-layouts: 29.9 us -> 18 us
  transfers between devices with their start and end apart: 97 -> 86, of which waited for: 36 -> 34; matrix products, arithmetic and copies ran while one was open for 22% -> 17% of each run, Pallas kernels for 22% -> 23%
where the time goes in v2:
time: 730 us; the launch traced here: 718 us
  waiting for transfers between devices  245 us (34%)
  Pallas kernels  189 us (26%)
  starting transfers between devices  129 us (18%)
  local copies, waits for them, and re-layouts  75.1 us (10%)
  other arithmetic  34 us (5%)
  matrix products  29.7 us (4%)
  between operations  16.2 us (2%)
    ppermute x42, waiting for transfers between devices, swap(): return lax.ppermute(array, 'fsdp', [(i, i ^ bits) for i in range(8)])  106 us
    pallas_call x7, Pallas kernels, matmul(): pl.pallas_call(body, grid=(cols // step_cols, rows // step_rows), in_spec...  58.9 us
    ppermute x7, starting transfers between devices, move(): from_end = lax.ppermute(incoming, 'ctx', inward)  39 us
    ppermute x7, waiting for transfers between devices, move(): from_end = lax.ppermute(incoming, 'ctx', inward)  36.7 us
    ppermute x42, starting transfers between devices, swap(): return lax.ppermute(array, 'fsdp', [(i, i ^ bits) for i in range(8)])  33.5 us
    pallas_call x2, Pallas kernels, feed_forward(): pl.pallas_call(body, grid=(rows // step_rows,), in_specs=[by_row, pl.Bloc...  30.1 us
    reduce_scatter x4, waiting for transfers between devices, scatter_rows(): return lax.psum_scatter(array, 'fsdp', scatter_dimension=0, tiled=True)  28.9 us
    dynamic_update_slice x18, local copies, waits for them, and re-layouts, gather_rows(): lax.dynamic_update_slice(whole, block, (member_of(k) * count + offset, 0))  25.6 us
  transfers between devices with their start and end apart: 86, of which 34 were waited for; matrix products, arithmetic and copies ran while one was open for 17% of the time, Pallas kernels for 23%

profile of v2, /device:TPU:0, one launch (start us, length us, event | category | flops | bytes accessed | tf_op | source)
XLA Modules:
  0.0 718.1 jit_solution(11232807987543317932)
XLA Ops:
  46.9 25.1 %collective-permute-done.10 = bf16[8,64,1024]{2,1,0:T(8,128)(2,1)} collective-permute-done((bf16[8,64,1024]{2,1,0:T(8,128)(2,1)S(1)}, bf16[8,64,1024]{2,1,0:T(8,128)(2,1)}, u32[]{:S(2)}, u32[]{:S(2)}) %collective-permute-start.10) | collective-permute-done | bytes 1048608 | tf_op jit(solution)/shard_map/ppermute | solution.py:326
  72.0 9.6 %all-gather.3.cloned.1.call-done.right_ref = bf16[2048,2304]{1,0:T(8,128)(2,1)} async-done(((bf16[256,2304]{1,0:T(8,128)(2,1)}), bf16[2048,2304]{1,0:T(8,128)(2,1)}) %all-gather.3.cloned.1.call-update) | async-done | bytes 9437200 | tf_op jit(solution)/shard_map/all_gather | solution.py:274
  85.2 6.7 fusion
  112.0 7.4 %collective-permute-done.14 = bf16[256,2048]{1,0:T(8,128)(2,1)} collective-permute-done((bf16[256,2048]{1,0:T(8,128)(2,1)}, bf16[256,2048]{1,0:T(8,128)(2,1)}, u32[]{:S(2)}, u32[]{:S(2)}) %collective-permute-start.14) | collective-permute-done | bytes 1048608 | tf_op jit(solution)/shard_map/ppermute | solution.py:221
  130.2 15.6 %attend.1 = (bf16[256,2048]{1,0:T(8,128)(2,1)}, f32[16,1,256]{2,1,0:T(1,128)}) custom-call(bf16[256,2048]{1,0:T(8,128)(2,1)} %slice.273.query_ref, bf16[1024,128]{1,0:T(8,128)(2,1)} %get-tuple-element.381.key_ref, bf16[128,1024]{1,0:T(8,128)(2,1)} %copy.40.value_t_ref, f32[1024,256]{1,0:T(8,128)} %fusion.34.mask_ref), custom_call_target="tpu_custom_call" | custom-call | tf_op jit(solution)/shard_map/attend/pallas_call | solution.py:444
  174.8 19.5 %collective-permute-done.25 = bf16[256,2048]{1,0:T(8,128)(2,1)} collective-permute-done((bf16[256,2048]{1,0:T(8,128)(2,1)S(1)}, bf16[256,2048]{1,0:T(8,128)(2,1)}, u32[]{:S(2)}, u32[]{:S(2)}) %collective-permute-start.25) | collective-permute-done | bytes 1048608 | tf_op jit(solution)/shard_map/ppermute | solution.py:221
  220.9 15.0 %feed_forward.2 = (bf16[2048,1024]{1,0:T(8,128)(2,1)}, bf16[2048,1024]{1,0:T(8,128)(2,1)}) custom-call(bf16[2048,2048]{1,0:T(8,128)(2,1)} %constant_dynamic-update-slice_fusion.24.refs_0_.mid_ref, bf16[2048,1024]{1,0:T(8,128)(2,1)} %bitcast.171, f32[1,1024]{1,0:T(1,128)} %bitcast.182, bf16[2048,2048]{1,0:T(8,128)(2,1)} %all-gather.5.cloned.1.call-done.refs_3_.right_ref, ...), custom_call_target="tpu_custom_call" | custom-call | tf_op jit(solution)/shard_map/feed_forward/pallas_call | solution.py:196
  235.9 5.9 matmul_tn.4.refs_0_
  251.2 15.1 %feed_forward.3 = (bf16[2048,1024]{1,0:T(8,128)(2,1)}, bf16[2048,1024]{1,0:T(8,128)(2,1)}) custom-call(bf16[2048,2048]{1,0:T(8,128)(2,1)} %constant_dynamic-update-slice_fusion.24.refs_0_.mid_ref, bf16[2048,1024]{1,0:T(8,128)(2,1)} %bitcast.172, f32[1,1024]{1,0:T(1,128)} %bitcast.183, ...), custom_call_target="tpu_custom_call", output_to_operand_aliasing={{0}: (5, {}), {1}: (6, {})} | custom-call | tf_op jit(solution)/shard_map/feed_forward/pallas_call | solution.py:196
  281.5 13.4 %matmul_nt.2 = bf16[2048,2048]{1,0:T(8,128)(2,1)} custom-call(bf16[2048,1024]{1,0:T(8,128)(2,1)} %get-tuple-element.289.left_ref.grad_ref, bf16[2048,1024]{1,0:T(8,128)(2,1)} %bitcast.173), custom_call_target="tpu_custom_call" | custom-call | tf_op jit(solution)/shard_map/matmul_nt/pallas_call | solution.py:75
  305.1 7.3 %matmul_tn.7.refs_4_.refs_0_ = bf16[256,2048]{1,0:T(8,128)(2,1)} custom-call(bf16[2048,1024]{1,0:T(8,128)(2,1)} %get-tuple-element.297.left_ref, bf16[2048,2048]{1,0:T(8,128)(2,1)} %all-gather.5.cloned.1.call-done.refs_3_.right_ref), custom_call_target="tpu_custom_call" | custom-call | tf_op jit(solution)/shard_map/matmul_tn/pallas_call | solution.py:75
  312.4 16.1 %fc_gradient.1 = bf16[8,256,1024]{2,1,0:T(8,128)(2,1)} custom-call(s32[8]{0:T(128)} %stack.32.order_ref, bf16[2048,2048]{1,0:T(8,128)(2,1)} %constant_dynamic-update-slice_fusion.24.refs_0_.mid_ref, bf16[2048,1024]{1,0:T(8,128)(2,1)} %get-tuple-element.289.left_ref.grad_ref), custom_call_target="tpu_custom_call" | custom-call | tf_op jit(solution)/shard_map/fc_gradient/pallas_call | solution.py:99
  334.8 12.3 %collective-permute-done.41 = bf16[128,1024]{1,0:T(8,128)(2,1)S(1)} collective-permute-done((bf16[128,1024]{1,0:T(8,128)(2,1)S(1)}, bf16[128,1024]{1,0:T(8,128)(2,1)S(1)}, u32[]{:S(2)}, u32[]{:S(2)}) %collective-permute-start.41) | collective-permute-done | bytes 262176 | tf_op jit(solution)/shard_map/ppermute | solution.py:221
  348.1 9.6 %collective-permute-done.40 = bf16[128,1024]{1,0:T(8,128)(2,1)S(1)} collective-permute-done((bf16[128,1024]{1,0:T(8,128)(2,1)S(1)}, bf16[128,1024]{1,0:T(8,128)(2,1)S(1)}, u32[]{:S(2)}, u32[]{:S(2)}) %collective-permute-start.40) | collective-permute-done | bytes 262176 | tf_op jit(solution)/shard_map/ppermute | solution.py:221
  362.2 19.0 %collective-permute-done.45 = bf16[128,1024]{1,0:T(8,128)(2,1)S(1)} collective-permute-done((bf16[128,1024]{1,0:T(8,128)(2,1)S(1)}, bf16[128,1024]{1,0:T(8,128)(2,1)S(1)}, u32[]{:S(2)}, u32[]{:S(2)}) %collective-permute-start.45) | collective-permute-done | bytes 262176 | tf_op jit(solution)/shard_map/ppermute | solution.py:221
  382.6 7.7 %reduce-scatter.5.cloned.1.call-done = bf16[256,2048]{1,0:T(8,128)(2,1)} async-done(((bf16[2048,2048]{1,0:T(8,128)(2,1)}), bf16[256,2048]{1,0:T(8,128)(2,1)}) %reduce-scatter.5.cloned.1.call-update) | async-done | bytes 1048592 | tf_op jit(solution)/shard_map/reduce_scatter | solution.py:285
  406.4 7.1 convolution_convert_fusion.1.grad_ref
  431.7 8.9 %collective-permute-done.54 = bf16[128,1024]{1,0:T(8,128)(2,1)S(1)} collective-permute-done((bf16[128,1024]{1,0:T(8,128)(2,1)}, bf16[128,1024]{1,0:T(8,128)(2,1)S(1)}, u32[]{:S(2)}, u32[]{:S(2)}) %collective-permute-start.54) | collective-permute-done | bytes 262176 | tf_op jit(solution)/shard_map/ppermute | solution.py:221
  460.1 17.4 %attend_back.1 = (bf16[256,2048]{1,0:T(8,128)(2,1)}, f32[1024,128]{1,0:T(8,128)}, f32[1024,128]{1,0:T(8,128)}) custom-call(bf16[256,2048]{1,0:T(8,128)(2,1)} %slice.273.query_ref, bf16[256,2048]{1,0:T(8,128)(2,1)} %convolution_convert_fusion.1.grad_ref, bf16[256,2048]{1,0:T(8,128)(2,1)} %get-tuple-element.187.out_ref, ...), custom_call_target="tpu_custom_call" | custom-call | tf_op jit(solution)/shard_map/attend_back/pallas_call | solution.py:500
  488.5 7.0 matmul_nt.3
  516.0 9.4 %attn_gradient.1 = bf16[8,272,2304]{2,1,0:T(8,128)(2,1)} custom-call(bf16[256,2048]{1,0:T(8,128)(2,1)} %copy-done.37, bf16[256,2304]{1,0:T(8,128)(2,1)} %constant_dynamic-update-slice_fusion.14.grad_ref, bf16[8,16,2304]{2,1,0:T(8,128)(2,1)} %fusion.35.extra_ref), custom_call_target="tpu_custom_call" | custom-call | tf_op jit(solution)/shard_map/attn_gradient/pallas_call | solution.py:126
  541.6 13.5 %matmul_nn.1 = bf16[2048,2048]{1,0:T(8,128)(2,1)} custom-call(bf16[2048,1024]{1,0:T(8,128)(2,1)} %get-tuple-element.297.left_ref, bf16[1024,2048]{1,0:T(8,128)(2,1)} %right_ref.1), custom_call_target="tpu_custom_call" | custom-call | tf_op jit(solution)/shard_map/matmul_nn/pallas_call | solution.py:75
  555.1 7.4 %collective-permute-done.66.refs_1_.refs_2_ = bf16[128,4096]{1,0:T(8,128)(2,1)S(1)} collective-permute-done((bf16[128,4096]{1,0:T(8,128)(2,1)S(1)}, bf16[128,4096]{1,0:T(8,128)(2,1)S(1)}, u32[]{:S(2)}, u32[]{:S(2)}) %collective-permute-start.66) | collective-permute-done | bytes 1048608 | tf_op jit(solution)/shard_map/ppermute | solution.py:392
  574.5 8.1 %finish.2 = f32[1024,2048]{1,0:T(8,128)} custom-call(s32[1]{0:T(128)} %bitcast.33.at_end_ref.ends_ref, s32[8]{0:T(128)} %stack.32.order_ref, bf16[256,2048]{1,0:T(8,128)(2,1)} %copy-done.6, bf16[256,2048]{1,0:T(8,128)(2,1)} %copy-done.10, bf16[256,2048]{1,0:T(8,128)(2,1)} %copy-done.2, bf16[256,2048]{1,0:T(8,128)(2,1)} %copy-done.12, ...), custom_call_target="tpu_custom_call" | custom-call | tf_op jit(solution)/shard_map/finish/pallas_call | solution.py:164
  582.5 11.0 %collective-permute-done.68.refs_1_ = bf16[256,2048]{1,0:T(8,128)(2,1)S(1)} collective-permute-done((bf16[256,2048]{1,0:T(8,128)(2,1)}, bf16[256,2048]{1,0:T(8,128)(2,1)S(1)}, u32[]{:S(2)}, u32[]{:S(2)}) %collective-permute-start.68) | collective-permute-done | bytes 1048608 | tf_op jit(solution)/shard_map/ppermute | solution.py:395
  594.1 21.2 %reduce-scatter.7.cloned.1.call-done = bf16[272,2304]{1,0:T(8,128)(2,1)} async-done(((bf16[2176,2304]{1,0:T(8,128)(2,1)}), bf16[272,2304]{1,0:T(8,128)(2,1)}) %reduce-scatter.7.cloned.1.call-update) | async-done | bytes 1253392 | tf_op jit(solution)/shard_map/reduce_scatter | solution.py:285
  618.5 6.1 collective-permute-start.71
  626.6 11.9 %collective-permute-done.71.refs_1_ = bf16[144,2304]{1,0:T(8,128)(2,1)S(1)} collective-permute-done((bf16[144,2304]{1,0:T(8,128)(2,1)S(1)}, bf16[144,2304]{1,0:T(8,128)(2,1)S(1)}, u32[]{:S(2)}, u32[]{:S(2)}) %collective-permute-start.71) | collective-permute-done | bytes 663584 | tf_op jit(solution)/shard_map/ppermute | solution.py:395
  647.7 7.8 %collective-permute-start.74 = (bf16[128,2304]{1,0:T(8,128)(2,1)}, bf16[128,2304]{1,0:T(8,128)(2,1)S(1)}, u32[]{:S(2)}, u32[]{:S(2)}) collective-permute-start(bf16[128,2304]{1,0:T(8,128)(2,1)} %slice.286.refs_0_), channel_id=1, source_target_pairs={{0,8},{24,16},{1,9},{25,17},{2,10},{26,18},{3,11},{27,19},{4,12},{... | collective-permute-start | bytes 1769480 | tf_op jit(solution)/shard_map/ppermute | solution.py:395
  655.5 11.2 %collective-permute-done.74.refs_1_ = bf16[128,2304]{1,0:T(8,128)(2,1)S(1)} collective-permute-done((bf16[128,2304]{1,0:T(8,128)(2,1)}, bf16[128,2304]{1,0:T(8,128)(2,1)S(1)}, u32[]{:S(2)}, u32[]{:S(2)}) %collective-permute-start.74) | collective-permute-done | bytes 589856 | tf_op jit(solution)/shard_map/ppermute | solution.py:395
  677.1 7.8 %finish.3 = f32[256,8192]{1,0:T(8,128)} custom-call(s32[1]{0:T(128)} %bitcast.33.at_end_ref.ends_ref, s32[8]{0:T(128)} %stack.32.order_ref, bf16[128,4096]{1,0:T(8,128)(2,1)} %copy-done.7, bf16[128,4096]{1,0:T(8,128)(2,1)} %get-tuple-element.328.refs_1_, bf16[128,4096]{1,0:T(8,128)(2,1)} %copy-done.3, bf16[128,4096]{1,0:T(8,128)(2,1)} %copy-done.14, ...), custom_call_target="tpu_custom_call" | custom-call | tf_op jit(solution)/shard_map/finish/pallas_call | solution.py:164
  690.5 12.9 %collective-permute-done.79 = bf16[128,2304]{1,0:T(8,128)(2,1)S(1)} collective-permute-done((bf16[128,2304]{1,0:T(8,128)(2,1)S(1)}, bf16[128,2304]{1,0:T(8,128)(2,1)S(1)}, u32[]{:S(2)}, u32[]{:S(2)}) %collective-permute-start.79) | collective-permute-done | bytes 589856 | tf_op jit(solution)/shard_map/ppermute | solution.py:397
  (483 shorter events, 327.9 us)
Async XLA Ops:
  7.3 74.3 %all-gather.3.cloned.1.call-start = ((), (), s32[]{:S(2)}) async-start(), calls=%async_computation.4 | async-start | bytes 10616832 | tf_op jit(solution)/shard_map/all_gather | solution.py:274
  9.7 211.1 %all-gather.5.cloned.1.call-start = ((), (), s32[]{:S(2)}) async-start(), calls=%async_computation.5 | async-start | bytes 9437184 | tf_op jit(solution)/shard_map/all_gather | solution.py:274
  45.2 26.8 %collective-permute-start.10 = (bf16[8,64,1024]{2,1,0:T(8,128)(2,1)S(1)}, bf16[8,64,1024]{2,1,0:T(8,128)(2,1)}, u32[]{:S(2)}, u32[]{:S(2)}) collective-permute-start(bf16[8,64,1024]{2,1,0:T(8,128)(2,1)S(1)} %bitcast_dynamic-update-slice_fusion.4), channel_id=1, source_target_pairs={{0,8},{8,16},{16,24},{24,0},{1,9},{9,17},{17,25},{25,1},{2,10},{10... | collective-permute-start | bytes 3145736 | tf_op jit(solution)/shard_map/ppermute | solution.py:326
  81.6 308.7 %reduce-scatter.5.cloned.1.call-start = ((), (), s32[]{:S(2)}) async-start(), calls=%async_computation.6 | async-start | bytes 9437184 | tf_op jit(solution)/shard_map/reduce_scatter | solution.py:285
  82.5 36.9 %collective-permute-start.14 = (bf16[256,2048]{1,0:T(8,128)(2,1)}, bf16[256,2048]{1,0:T(8,128)(2,1)}, u32[]{:S(2)}, u32[]{:S(2)}) collective-permute-start(bf16[256,2048]{1,0:T(8,128)(2,1)} %own_ref), channel_id=1, source_target_pairs={{0,2},{1,3},{2,0},{3,1},{4,6},{5,7},{6,4},{7,5},{8,10},{9,11},{10,... | collective-permute-start | bytes 3145736 | tf_op jit(solution)/shard_map/ppermute | solution.py:221
  84.0 36.5 %collective-permute-start.15 = (bf16[256,2048]{1,0:T(8,128)(2,1)}, bf16[256,2048]{1,0:T(8,128)(2,1)S(1)}, u32[]{:S(2)}, u32[]{:S(2)}) collective-permute-start(bf16[256,2048]{1,0:T(8,128)(2,1)} %own_ref), channel_id=1, source_target_pairs={{0,4},{1,5},{2,6},{3,7},{4,0},{5,1},{6,2},{7,3},{8,12},{9,13},{10,... | collective-permute-start | bytes 3145736 | tf_op jit(solution)/shard_map/ppermute | solution.py:221
  97.0 29.4 %collective-permute-start.16 = (bf16[256,2048]{1,0:T(8,128)(2,1)}, bf16[256,2048]{1,0:T(8,128)(2,1)S(1)}, u32[]{:S(2)}, u32[]{:S(2)}) collective-permute-start(bf16[256,2048]{1,0:T(8,128)(2,1)} %own_ref), channel_id=1, source_target_pairs={{0,1},{1,0},{2,3},{3,2},{4,5},{5,4},{6,7},{7,6},{8,9},{9,8},{10,11... | collective-permute-start | bytes 3145736 | tf_op jit(solution)/shard_map/ppermute | solution.py:221
  120.5 30.9 %collective-permute-start.17 = (bf16[256,2048]{1,0:T(8,128)(2,1)}, bf16[256,2048]{1,0:T(8,128)(2,1)}, u32[]{:S(2)}, u32[]{:S(2)}) collective-permute-start(bf16[256,2048]{1,0:T(8,128)(2,1)} %collective-permute-done.14), channel_id=1, source_target_pairs={{0,1},{1,0},{2,3},{3,2},{4,5},{5,4},{6,7},{7,6},{8,9},{9,8},{10,11... | collective-permute-start | bytes 3145736 | tf_op jit(solution)/shard_map/ppermute | solution.py:221
  120.5 33.2 %collective-permute-start.18 = (bf16[256,2048]{1,0:T(8,128)(2,1)S(1)}, bf16[256,2048]{1,0:T(8,128)(2,1)}, u32[]{:S(2)}, u32[]{:S(2)}) collective-permute-start(bf16[256,2048]{1,0:T(8,128)(2,1)S(1)} %collective-permute-done.15), channel_id=1, source_target_pairs={{0,1},{1,0},{2,3},{3,2},{4,5},{5,4},{6,7},{7,6},{8,9},{9,8},{10,11... | collective-permute-start | bytes 3145736 | tf_op jit(solution)/shard_map/ppermute | solution.py:221
  126.4 42.4 %collective-permute-start.23 = (bf16[8,64,1024]{2,1,0:T(8,128)(2,1)}, bf16[8,64,1024]{2,1,0:T(8,128)(2,1)}, u32[]{:S(2)}, u32[]{:S(2)}) collective-permute-start(bf16[8,64,1024]{2,1,0:T(8,128)(2,1)} %collective-permute-done.10), channel_id=1, source_target_pairs={{0,8},{8,16},{16,24},{24,0},{1,9},{9,17},{17,25},{25,1},{2,10},{10... | collective-permute-start | bytes 3145736 | tf_op jit(solution)/shard_map/ppermute | solution.py:326
  169.7 31.6 %collective-permute-start.26 = (bf16[256,2048]{1,0:T(8,128)(2,1)S(1)}, bf16[256,2048]{1,0:T(8,128)(2,1)S(1)}, u32[]{:S(2)}, u32[]{:S(2)}) collective-permute-start(bf16[256,2048]{1,0:T(8,128)(2,1)S(1)} %add_convert_fusion.1.own_ref), channel_id=1, source_target_pairs={{0,4},{1,5},{2,6},{3,7},{4,0},{5,1},{6,2},{7,3},{8,12},{9,13},{10,... | collective-permute-start | bytes 3145736 | tf_op jit(solution)/shard_map/ppermute | solution.py:221
  170.7 31.1 %collective-permute-start.24 = (bf16[256,2048]{1,0:T(8,128)(2,1)S(1)}, bf16[256,2048]{1,0:T(8,128)(2,1)}, u32[]{:S(2)}, u32[]{:S(2)}) collective-permute-start(bf16[256,2048]{1,0:T(8,128)(2,1)S(1)} %add_convert_fusion.1.own_ref), channel_id=1, source_target_pairs={{0,1},{1,0},{2,3},{3,2},{4,5},{5,4},{6,7},{7,6},{8,9},{9,8},{10,11... | collective-permute-start | bytes 3145736 | tf_op jit(solution)/shard_map/ppermute | solution.py:221
  171.3 36.2 %collective-permute-start.33 = (bf16[8,64,1024]{2,1,0:T(8,128)(2,1)}, bf16[8,64,1024]{2,1,0:T(8,128)(2,1)}, u32[]{:S(2)}, u32[]{:S(2)}) collective-permute-start(bf16[8,64,1024]{2,1,0:T(8,128)(2,1)} %collective-permute-done.23), channel_id=1, source_target_pairs={{0,8},{8,16},{16,24},{24,0},{1,9},{9,17},{17,25},{25,1},{2,10},{10... | collective-permute-start | bytes 3145736 | tf_op jit(solution)/shard_map/ppermute | solution.py:326
  241.8 26.6 %collective-permute-start.34 = (bf16[256,2048]{1,0:T(8,128)(2,1)}, bf16[256,2048]{1,0:T(8,128)(2,1)S(1)}, u32[]{:S(2)}, u32[]{:S(2)}) collective-permute-start(bf16[256,2048]{1,0:T(8,128)(2,1)} %matmul_tn.4.refs_0_), channel_id=1, source_target_pairs={{0,8},{24,16},{1,9},{25,17},{2,10},{26,18},{3,11},{27,19},{4,12},{... | collective-permute-start | bytes 3145736 | tf_op jit(solution)/shard_map/ppermute | solution.py:395
  268.7 26.6 %collective-permute-start.35 = (bf16[256,2048]{1,0:T(8,128)(2,1)S(1)}, bf16[256,2048]{1,0:T(8,128)(2,1)}, u32[]{:S(2)}, u32[]{:S(2)}) collective-permute-start(bf16[256,2048]{1,0:T(8,128)(2,1)S(1)} %copy-done.9), channel_id=1, source_target_pairs={{0,8},{24,16},{1,9},{25,17},{2,10},{26,18},{3,11},{27,19},{4,12},{... | collective-permute-start | bytes 3145736 | tf_op jit(solution)/shard_map/ppermute | solution.py:395
  299.3 267.5 %reduce-scatter.9.cloned.1.call-start = ((), (), s32[]{:S(2)}) async-start(), calls=%async_computation.8 | async-start | bytes 9437184 | tf_op jit(solution)/shard_map/reduce_scatter | solution.py:285
  300.5 28.0 %collective-permute-start.37 = (bf16[256,2048]{1,0:T(8,128)(2,1)S(1)}, bf16[256,2048]{1,0:T(8,128)(2,1)S(1)}, u32[]{:S(2)}, u32[]{:S(2)}) collective-permute-start(bf16[256,2048]{1,0:T(8,128)(2,1)S(1)} %copy-done.11), channel_id=1, source_target_pairs={{0,8},{24,16},{8,0},{16,24},{1,9},{25,17},{9,1},{17,25},{2,10},{26... | collective-permute-start | bytes 3145736 | tf_op jit(solution)/shard_map/ppermute | solution.py:392
  329.5 31.0 %collective-permute-start.42 = (bf16[256,2048]{1,0:T(8,128)(2,1)S(1)}, bf16[256,2048]{1,0:T(8,128)(2,1)S(1)}, u32[]{:S(2)}, u32[]{:S(2)}) collective-permute-start(bf16[256,2048]{1,0:T(8,128)(2,1)S(1)} %get-tuple-element.304.refs_3_), channel_id=1, source_target_pairs={{0,8},{24,16},{8,0},{16,24},{1,9},{25,17},{9,1},{17,25},{2,10},{26... | collective-permute-start | bytes 3145736 | tf_op jit(solution)/shard_map/ppermute | solution.py:392
  331.9 29.7 %collective-permute-start.43 = (bf16[256,2048]{1,0:T(8,128)(2,1)S(1)}, bf16[256,2048]{1,0:T(8,128)(2,1)S(1)}, u32[]{:S(2)}, u32[]{:S(2)}) collective-permute-start(bf16[256,2048]{1,0:T(8,128)(2,1)S(1)} %get-tuple-element.230.refs_2_), channel_id=1, source_target_pairs={{8,16},{16,8},{9,17},{17,9},{10,18},{18,10},{11,19},{19,11},{12,20... | collective-permute-start | bytes 3145736 | tf_op jit(solution)/shard_map/ppermute | solution.py:401
  390.3 32.5 %collective-permute-start.48 = (bf16[128,4096]{1,0:T(8,128)(2,1)S(1)}, bf16[128,4096]{1,0:T(8,128)(2,1)}, u32[]{:S(2)}, u32[]{:S(2)}) collective-permute-start(bf16[128,4096]{1,0:T(8,128)(2,1)S(1)} %pad_maximum_fusion.1.refs_0_), channel_id=1, source_target_pairs={{0,8},{24,16},{1,9},{25,17},{2,10},{26,18},{3,11},{27,19},{4,12},{... | collective-permute-start | bytes 3145736 | tf_op jit(solution)/shard_map/ppermute | solution.py:395
  395.1 29.3 %collective-permute-start.49 = (bf16[256,2048]{1,0:T(8,128)(2,1)S(1)}, bf16[256,2048]{1,0:T(8,128)(2,1)}, u32[]{:S(2)}, u32[]{:S(2)}) collective-permute-start(bf16[256,2048]{1,0:T(8,128)(2,1)S(1)} %get-tuple-element.239.refs_0_), channel_id=1, source_target_pairs={{8,16},{16,8},{9,17},{17,9},{10,18},{18,10},{11,19},{19,11},{12,20... | collective-permute-start | bytes 3145736 | tf_op jit(solution)/shard_map/ppermute | solution.py:401
  396.8 48.0 %collective-permute-start.50 = (bf16[256,2048]{1,0:T(8,128)(2,1)S(1)}, bf16[256,2048]{1,0:T(8,128)(2,1)}, u32[]{:S(2)}, u32[]{:S(2)}) collective-permute-start(bf16[256,2048]{1,0:T(8,128)(2,1)S(1)} %get-tuple-element.306.refs_5_), channel_id=1, source_target_pairs={{8,0},{16,24},{9,1},{17,25},{10,2},{18,26},{11,3},{19,27},{12,4},{... | collective-permute-start | bytes 3145736 | tf_op jit(solution)/shard_map/ppermute | solution.py:397
  445.7 169.6 %reduce-scatter.7.cloned.1.call-start = ((), (), s32[]{:S(2)}) async-start(), calls=%async_computation.7 | async-start | bytes 11280384 | tf_op jit(solution)/shard_map/reduce_scatter | solution.py:285
  445.8 33.8 %collective-permute-start.58 = (bf16[128,4096]{1,0:T(8,128)(2,1)}, bf16[128,4096]{1,0:T(8,128)(2,1)S(1)}, u32[]{:S(2)}, u32[]{:S(2)}) collective-permute-start(bf16[128,4096]{1,0:T(8,128)(2,1)} %pad_maximum_fusion.2.refs_0_), channel_id=1, source_target_pairs={{0,8},{24,16},{1,9},{25,17},{2,10},{26,18},{3,11},{27,19},{4,12},{... | collective-permute-start | bytes 3145736 | tf_op jit(solution)/shard_map/ppermute | solution.py:395
  451.5 28.1 %collective-permute-start.59 = (bf16[128,4096]{1,0:T(8,128)(2,1)}, bf16[128,4096]{1,0:T(8,128)(2,1)}, u32[]{:S(2)}, u32[]{:S(2)}) collective-permute-start(bf16[128,4096]{1,0:T(8,128)(2,1)} %tick.20.refs_2_), channel_id=1, source_target_pairs={{8,16},{16,8},{9,17},{17,9},{10,18},{18,10},{11,19},{19,11},{12,20... | collective-permute-start | bytes 3145736 | tf_op jit(solution)/shard_map/ppermute | solution.py:401
  453.1 29.9 %collective-permute-start.60 = (bf16[256,2048]{1,0:T(8,128)(2,1)S(1)}, bf16[256,2048]{1,0:T(8,128)(2,1)}, u32[]{:S(2)}, u32[]{:S(2)}) collective-permute-start(bf16[256,2048]{1,0:T(8,128)(2,1)S(1)} %tick.21.refs_7_), channel_id=1, source_target_pairs={{8,0},{16,24},{9,1},{17,25},{10,2},{18,26},{11,3},{19,27},{12,4},{... | collective-permute-start | bytes 3145736 | tf_op jit(solution)/shard_map/ppermute | solution.py:397
  503.6 27.3 %collective-permute-start.64 = (bf16[128,4096]{1,0:T(8,128)(2,1)}, bf16[128,4096]{1,0:T(8,128)(2,1)S(1)}, u32[]{:S(2)}, u32[]{:S(2)}) collective-permute-start(bf16[128,4096]{1,0:T(8,128)(2,1)} %get-tuple-element.328.refs_1_), channel_id=1, source_target_pairs={{0,8},{24,16},{8,0},{16,24},{1,9},{25,17},{9,1},{17,25},{2,10},{26... | collective-permute-start | bytes 3145736 | tf_op jit(solution)/shard_map/ppermute | solution.py:392
  535.4 172.2 %reduce-scatter.11.cloned.1.call-start = ((), (), s32[]{:S(2)}) async-start(), calls=%async_computation.9 | async-start | bytes 9437184 | tf_op jit(solution)/shard_map/reduce_scatter | solution.py:285
  566.8 26.8 %collective-permute-start.68 = (bf16[256,2048]{1,0:T(8,128)(2,1)}, bf16[256,2048]{1,0:T(8,128)(2,1)S(1)}, u32[]{:S(2)}, u32[]{:S(2)}) collective-permute-start(bf16[256,2048]{1,0:T(8,128)(2,1)} %reduce-scatter.9.cloned.1.call-done.refs_0_), channel_id=1, source_target_pairs={{0,8},{24,16},{1,9},{25,17},{2,10},{26,18},{3,11},{27,19},{4,12},{... | collective-permute-start | bytes 3145736 | tf_op jit(solution)/shard_map/ppermute | solution.py:395
  573.2 43.3 %collective-permute-start.70 = (bf16[128,4096]{1,0:T(8,128)(2,1)}, bf16[128,4096]{1,0:T(8,128)(2,1)}, u32[]{:S(2)}, u32[]{:S(2)}) collective-permute-start(bf16[128,4096]{1,0:T(8,128)(2,1)} %get-tuple-element.332.refs_5_), channel_id=1, source_target_pairs={{8,0},{16,24},{9,1},{17,25},{10,2},{18,26},{11,3},{19,27},{12,4},{... | collective-permute-start | bytes 3145736 | tf_op jit(solution)/shard_map/ppermute | solution.py:397
  617.2 28.3 %collective-permute-start.73 = (bf16[128,4096]{1,0:T(8,128)(2,1)S(1)}, bf16[128,4096]{1,0:T(8,128)(2,1)S(1)}, u32[]{:S(2)}, u32[]{:S(2)}) collective-permute-start(bf16[128,4096]{1,0:T(8,128)(2,1)S(1)} %tick.26.refs_7_), channel_id=1, source_target_pairs={{8,0},{16,24},{9,1},{17,25},{10,2},{18,26},{11,3},{19,27},{12,4},{... | collective-permute-start | bytes 3145736 | tf_op jit(solution)/shard_map/ppermute | solution.py:397
  645.5 26.1 %collective-permute-start.76 = (bf16[256,2048]{1,0:T(8,128)(2,1)S(1)}, bf16[256,2048]{1,0:T(8,128)(2,1)}, u32[]{:S(2)}, u32[]{:S(2)}) collective-permute-start(bf16[256,2048]{1,0:T(8,128)(2,1)S(1)} %tick.28), channel_id=1, source_target_pairs={{8,0},{16,24},{9,1},{17,25},{10,2},{18,26},{11,3},{19,27},{12,4},{... | collective-permute-start | bytes 3145736 | tf_op jit(solution)/shard_map/ppermute | solution.py:397
  (124 other events, 1530.3 us)
Sparse Core Ops, SparseCore 0:
  10.6 70.9 all-gather.2
  83.4 76.9 all-gather.4
  299.4 90.7 reduce-scatter.4
  445.8 73.0 reduce-scatter.8
  535.5 79.7 reduce-scatter.6
  619.0 71.2 reduce-scatter.10

commit v3 on v2

--- a/solution.py
+++ b/solution.py
@@ -251,6 +251,7 @@
 def gather_rows(own, near):
     count = own.shape[0]
     half = count // 2
+    near, whole = lax.optimization_barrier((near, placed_own(own)))
     along_x, along_y = near
     first_half, second_half = swap(along_x[:half], 4), swap(along_y[half:], 2)
     placed = [
@@ -264,7 +265,6 @@
         (7, 0, swap(first_half, 1)),
         (7, half, swap(second_half, 1)),
     ]
-    whole = placed_own(own)
     for k, offset, block in placed:
         whole = lax.dynamic_update_slice(whole, block, (member_of(k) * count + offset, 0))
     return whole
@@ -533,14 +533,48 @@
     return center * inverse, inverse
 
 
-def norm_pullback(normed, inverse, gain_vec, grad_in):
-    weighted = grad_in * gain_vec
-    grad_values = inverse * (
-        weighted
-        - jnp.mean(weighted, axis=-1, keepdims=True)
-        - normed * jnp.mean(weighted * normed, axis=-1, keepdims=True)
-    )
-    return grad_values, jnp.sum(grad_in * normed, axis=0), jnp.sum(grad_in, axis=0)
+def norm_pullback(normed, inverse, gain, grad_in, base, pair=None, weight=None, out_type=FULL):
+    rows, width = normed.shape
+    more = [] if pair is None else [pair, weight]
+
+    def body(normed_ref, inverse_ref, gain_ref, grad_ref, base_ref, *refs):
+        out_ref, sums_ref = refs[-2:]
+        grad = grad_ref[...].astype(FULL)
+        if more:
+            grad = grad + product_nt(refs[0][...], refs[1][...])
+        held = normed_ref[...]
+        weighted = grad * gain_ref[...]
+        turned = inverse_ref[...] * (
+            weighted
+            - jnp.mean(weighted, axis=-1, keepdims=True)
+            - held * jnp.mean(weighted * held, axis=-1, keepdims=True)
+        )
+        made = base_ref[...].astype(FULL) + turned
+        out_ref[...] = made.astype(out_type)
+        sums_ref[0:1] = jnp.sum(grad * held, axis=0, keepdims=True)
+        sums_ref[1:2] = jnp.sum(grad, axis=0, keepdims=True)
+        sums_ref[2:3] = jnp.sum(made.astype(LOW).astype(FULL), axis=0, keepdims=True)
+
+    at = lambda i: (0, 0)
+    specs = [pl.BlockSpec(array.shape, at) for array in (normed, inverse, gain[None], grad_in, base)]
+    if more:
+        cols = pair.shape[1]
+        last = weight.shape[1] // cols - 1
+        specs += [pl.BlockSpec(pair.shape, at), pl.BlockSpec((width, cols), lambda i: (0, last))]
+    made, sums = pl.pallas_call(
+        body,
+        grid=(1,),
+        in_specs=specs,
+        out_specs=[pl.BlockSpec((rows, width), at), pl.BlockSpec((8, width), at)],
+        out_shape=[
+            jax.ShapeDtypeStruct((rows, width), out_type),
+            jax.ShapeDtypeStruct((8, width), FULL),
+        ],
+        compiler_params=ROOMY,
+        cost_estimate=QUICK,
+        name="norm_pullback",
+    )(normed, inverse, gain[None], grad_in, base, *more)
+    return made, sums[0], sums[1], sums[2]
 
 
 def gelu_pair(values_in):
@@ -613,7 +647,7 @@
     normed_in = (normed1 * gain1 + bias1).astype(LOW)
     attn_bias = jnp.concatenate([query_bias_all, jnp.zeros((HD,), FULL), value_bias_all])
     projected = (product(normed_in, attn_all) + attn_bias).astype(LOW)
-    queries, pair_own = projected[:, :width], projected[:, width:]
+    pair_own = projected[:, width:]
     reach = min(ctx_count - 1, -(-(WINDOW - 1) // rows))
     pairs = [pair_own] + [
         lax.ppermute(pair_own, "ctx", [(i, i + d) for i in range(ctx_count - d)])
@@ -645,7 +679,7 @@
     )
     mask = jnp.where(allowed, 0.0, NEGATIVE).astype(FULL)
     keys, values = pair_rows[:, :HD], pair_rows[:, HD:]
-    attended, score_totals = attend(queries, keys, values.T, mask)
+    attended, score_totals = attend(projected, keys, values.T, mask)
     middle = tok_rows + (product(attended, out_all) + out_bias_all)
     normed2, inverse2 = normalize(middle)
     normed_mid = (normed2 * gain2 + bias2).astype(LOW)
@@ -677,42 +711,44 @@
     )
 
     grad_mid_part = matmul(grad_pre, fc_all, "nt")
-    sums.move(proj_term(2))
-    mid_all, cot_all, hidden, grad_pre, grad_mid_part = sums.fence(
-        mid_all, cot_all, hidden, grad_pre, grad_mid_part
-    )
-
     grad_normed_mid = scatter_rows(grad_mid_part)
     fc_terms = fc_gradient(mid_all, grad_pre)
-    sums.move(proj_term(3))
-    hidden, grad_pre, fc_terms = sums.fence(hidden, grad_pre, fc_terms)
+    sums.move(proj_term(2))
+    cot_all, hidden, grad_pre, grad_mid_part, fc_terms = sums.fence(
+        cot_all, hidden, grad_pre, grad_mid_part, fc_terms
+    )
 
     share_half, group = depth_share // 2, peers // 2
     fc_first = exchange_blocks([fc_terms[k, :share_half] for k in members])
+    grad_fc_bias = jnp.sum(grad_pre.astype(FULL), axis=0)
+    cot_sum = jnp.sum(cot_own.astype(FULL), axis=0)
+    sums.move(proj_term(3))
+    hidden, fc_terms, fc_first, grad_fc_bias, cot_sum = sums.fence(
+        hidden, fc_terms, fc_first, grad_fc_bias, cot_sum
+    )
+
+    fc_second = exchange_blocks([fc_terms[k, share_half:] for k in members])
     sums.move(jnp.concatenate(fc_first[:group], axis=1))
-    fc_first, fc_terms, grad_normed_mid = sums.fence(fc_first, fc_terms, grad_normed_mid)
-    grad_normed_mid = grad_normed_mid.astype(FULL)
-
-    fc_second = exchange_blocks([fc_terms[k, share_half:] for k in members])
-    grad_middle_ln, grad_gain2, grad_bias2 = norm_pullback(
-        normed2, inverse2, gain2, grad_normed_mid
-    )
-    grad_middle = cot_own.astype(FULL) + grad_middle_ln
+    fc_first, fc_second, grad_normed_mid = sums.fence(fc_first, fc_second, grad_normed_mid)
+
+    grad_middle, grad_gain2, grad_bias2, grad_mid_sum = norm_pullback(
+        normed2, inverse2, gain2, grad_normed_mid, cot_own
+    )
     grad_mid_low = grad_middle.astype(LOW)
-    grad_attended = product_nt(grad_mid_low, out_all).astype(LOW)
-    out_term = product_tn(attended, grad_mid_low).astype(LOW)
+    grad_attended = matmul(grad_mid_low, out_all, "nt", 256, 512)
+    out_term = matmul(attended, grad_mid_low, "tn", 512, 2048)
     sums.move(jnp.concatenate(fc_first[group:], axis=1))
-    fc_second, grad_middle, grad_mid_low, grad_attended, out_term = sums.fence(
-        fc_second, grad_middle, grad_mid_low, grad_attended, out_term
+    fc_second, grad_middle, grad_attended, out_term, grad_mid_sum = sums.fence(
+        fc_second, grad_middle, grad_attended, out_term, grad_mid_sum
     )
 
     out_share = scatter_rows(out_term)
     grad_query_low, grad_keys, grad_values = attend_back(
-        queries, grad_attended, attended, score_totals, keys, keys.T, values, mask
+        projected, grad_attended, attended, score_totals, keys, keys.T, values, mask
     )
     sums.move(jnp.concatenate(fc_second[:group], axis=1))
-    fc_second, grad_middle, grad_mid_low, grad_query_low, grad_keys, grad_values = sums.fence(
-        fc_second, grad_middle, grad_mid_low, grad_query_low, grad_keys, grad_values
+    fc_second, grad_query_low, grad_keys, grad_values = sums.fence(
+        fc_second, grad_query_low, grad_keys, grad_values
     )
 
     grad_pairs = jnp.concatenate([grad_keys, grad_values], axis=1)
@@ -725,34 +761,40 @@
     pair_scaling = jnp.concatenate([jnp.full((HD,), SCALING, FULL), jnp.ones((HD,), FULL)])
     grad_pair_low = (grad_pair * pair_scaling).astype(LOW)
     grad_normed_in = matmul(grad_query_low, attn_all, "nt", 256, 512, out_type=FULL)
-    fc_second, grad_middle, grad_mid_low, grad_query_low, grad_pair_low, grad_normed_in = (
-        sums.fence(
-            fc_second, grad_middle, grad_mid_low, grad_query_low, grad_pair_low, grad_normed_in
-        )
-    )
-
-    grad_normed_in = grad_normed_in + product_nt(grad_pair_low, attn_all[:, width:])
-    grad_tok_ln, grad_gain1, grad_bias1 = norm_pullback(normed1, inverse1, gain1, grad_normed_in)
-    grad_tokens = (grad_middle + grad_tok_ln).astype(LOW)
+    query_sum = jnp.sum(grad_query_low.astype(FULL), axis=0)
+    fc_second, grad_query_low, grad_pair_low, grad_normed_in, query_sum = sums.fence(
+        fc_second, grad_query_low, grad_pair_low, grad_normed_in, query_sum
+    )
+
+    grad_tokens, grad_gain1, grad_bias1, unused = norm_pullback(
+        normed1,
+        inverse1,
+        gain1,
+        grad_normed_in,
+        grad_middle,
+        grad_pair_low,
+        attn_all,
+        LOW,
+    )
     grad_projected = jnp.concatenate([grad_query_low, grad_pair_low], axis=1)
-    grad_projected_bias = jnp.sum(grad_projected.astype(FULL), axis=0)
+    pair_sum = jnp.sum(grad_pair_low.astype(FULL), axis=0)
     vector_terms = [
-        grad_projected_bias[:width],
-        jnp.sum(grad_mid_low.astype(FULL), axis=0),
+        query_sum,
+        grad_mid_sum,
         grad_gain1,
         grad_bias1,
-        jnp.sum(cot_own.astype(FULL), axis=0),
+        cot_sum,
         grad_gain2,
         grad_bias2,
     ]
     by_member = jnp.concatenate(
         [term.reshape(peers, depth_share) for term in vector_terms]
-        + [grad_projected_bias[width + HD :].reshape(peers, HD // peers)],
+        + [pair_sum[HD:].reshape(peers, HD // peers)],
         axis=1,
     )
     used, extra_cols = by_member.shape[1], grad_projected.shape[1]
     by_member = jnp.pad(by_member, ((0, 0), (0, extra_cols - used)))
-    grad_fc_bias = jnp.pad(jnp.sum(grad_pre.astype(FULL), axis=0), (0, extra_cols - ff_share))
+    grad_fc_bias = jnp.pad(grad_fc_bias, (0, extra_cols - ff_share))
     is_own = jnp.arange(peers)[:, None] == lax.axis_index("fsdp")
     fc_bias_rows = jnp.where(is_own, grad_fc_bias[None], 0.0)
     extra = jnp.stack([by_member, fc_bias_rows], axis=1).astype(LOW)
@@ -760,10 +802,10 @@
     attn_term = attn_gradient(normed_in, grad_projected, extra)
     attn_rows = attn_term.shape[1]
     attn_term = attn_term.reshape(peers * attn_rows, extra_cols)
+    attn_share = scatter_rows(attn_term)
     sums.move(jnp.concatenate(fc_second[group:], axis=1))
     hidden, attn_term = sums.fence(hidden, attn_term)
 
-    attn_share = scatter_rows(attn_term)
     out_part = matmul(hidden, proj_weight, "nn")
     sums.move(out_share)
     (out_part,) = sums.fence(out_part)

time: 730 us -> 698 us (0.956)
  Pallas kernels: 189 us -> 207 us
  matrix products: 29.7 us -> 13.3 us
  waiting for transfers between devices: 245 us -> 230 us
  starting transfers between devices: 129 us -> 116 us
    reduce_scatter x4, waiting for transfers between devices: 28.9 us -> 0.03 us  [scatter_rows(): return lax.psum_scatter(array, 'fsdp', scatter_dimension=0, tiled=True)]
    ppermute x4, waiting for transfers between devices: 12.7 us -> 40.3 us  [move(): from_end = from_middle = lax.ppermute(outgoing, 'ctx', inward + outward)]
    ppermute x42, waiting for transfers between devices: 106 us -> 82 us  [swap(): return lax.ppermute(array, 'fsdp', [(i, i ^ bits) for i in range(8)])]
    dot_general x3 -> x0, matrix products: 17.1 us -> none  [the longest x2 11.4 us: product_nt(): lax.dot_general(left_side, right_side, (((1,), (1,)), ((), ())), preferre...]
    pallas_call x7 -> x9, Pallas kernels: 58.9 us -> 71.7 us  [matmul(): pl.pallas_call(body, grid=(cols // step_cols, rows // step_rows), in_spec...]
    pallas_call x0 -> x2, Pallas kernels: none -> 10.7 us  [norm_pullback(): pl.pallas_call(body, grid=(1,), in_specs=specs, out_specs=[pl.BlockSpec((...]
    ppermute x3, waiting for transfers between devices: 3.89 us -> 13.3 us  [per_device(): lax.ppermute(sent, 'ctx', [(i + d, i) for i in range(ctx_count - d)])]
    ppermute x7, waiting for transfers between devices: 22.5 us -> 30.6 us  [move(): from_middle = lax.ppermute(outgoing, 'ctx', outward)]
  transfers between devices with their start and end apart: 86 -> 86, of which waited for: 34 -> 37; matrix products, arithmetic and copies ran while one was open for 17% -> 15% of each run, Pallas kernels for 23% -> 25%
where the time goes in v3:
time: 698 us; the launch traced here: 687 us
  waiting for transfers between devices  230 us (33%)
  Pallas kernels  207 us (30%)
  starting transfers between devices  116 us (17%)
  local copies, waits for them, and re-layouts  69.3 us (10%)
  other arithmetic  34.8 us (5%)
  between operations  16.4 us (2%)
  matrix products  13.3 us (2%)
    ppermute x42, waiting for transfers between devices, swap(): return lax.ppermute(array, 'fsdp', [(i, i ^ bits) for i in range(8)])  82 us
    pallas_call x9, Pallas kernels, matmul(): pl.pallas_call(body, grid=(cols // step_cols, rows // step_rows), in_spec...  71.7 us
    ppermute x4, waiting for transfers between devices, move(): from_end = from_middle = lax.ppermute(outgoing, 'ctx', inward + outward)  40.3 us
    ppermute x7, starting transfers between devices, move(): from_end = lax.ppermute(incoming, 'ctx', inward)  39.4 us
    ppermute x42, starting transfers between devices, swap(): return lax.ppermute(array, 'fsdp', [(i, i ^ bits) for i in range(8)])  30.8 us
    ppermute x7, waiting for transfers between devices, move(): from_middle = lax.ppermute(outgoing, 'ctx', outward)  30.6 us
    pallas_call x2, Pallas kernels, feed_forward(): pl.pallas_call(body, grid=(rows // step_rows,), in_specs=[by_row, pl.Bloc...  29.9 us
    ppermute x7, waiting for transfers between devices, move(): from_end = lax.ppermute(incoming, 'ctx', inward)  29.2 us
  transfers between devices with their start and end apart: 86, of which 37 were waited for; matrix products, arithmetic and copies ran while one was open for 15% of the time, Pallas kernels for 25%

profile of v3, /device:TPU:0, one launch (start us, length us, event | category | flops | bytes accessed | tf_op | source)
XLA Modules:
  0.0 686.9 jit_solution(18418002917656729481)
XLA Ops:
  46.9 25.1 %collective-permute-done.10 = bf16[8,64,1024]{2,1,0:T(8,128)(2,1)} collective-permute-done((bf16[8,64,1024]{2,1,0:T(8,128)(2,1)S(1)}, bf16[8,64,1024]{2,1,0:T(8,128)(2,1)}, u32[]{:S(2)}, u32[]{:S(2)}) %collective-permute-start.10) | collective-permute-done | bytes 1048608 | tf_op jit(solution)/shard_map/ppermute | solution.py:326
  72.0 9.6 %all-gather.3.cloned.1.call-done.right_ref.refs_1_ = bf16[2048,2304]{1,0:T(8,128)(2,1)} async-done(((bf16[256,2304]{1,0:T(8,128)(2,1)}), bf16[2048,2304]{1,0:T(8,128)(2,1)}) %all-gather.3.cloned.1.call-update) | async-done | bytes 9437200 | tf_op jit(solution)/shard_map/all_gather | solution.py:274
  90.0 7.4 %fusion.query_ref = bf16[256,2304]{1,0:T(8,128)(2,1)S(1)} fusion(bf16[256,2048]{1,0:T(8,128)(2,1)S(1)} %get-tuple-element.415.normed_ref, bf16[2048,2304]{1,0:T(8,128)(2,1)} %all-gather.3.cloned.1.call-done.right_ref.refs_1_, f32[2304]{0:T(1024)S(1)} %pad_maximum_fusion.7), kind=kOutput, calls=%fused_computation.2 | convolution fusion | flops 2417098752 | bytes 11674624 | tf_op jit(solution)/shard_map/dot_general | solution.py:26
  134.3 15.6 %attend.1 = (bf16[256,2048]{1,0:T(8,128)(2,1)}, f32[16,1,256]{2,1,0:T(1,128)}) custom-call(bf16[256,2304]{1,0:T(8,128)(2,1)} %copy-done.31, bf16[1024,128]{1,0:T(8,128)(2,1)} %get-tuple-element.422.key_ref, bf16[128,1024]{1,0:T(8,128)(2,1)} %copy.40.value_t_ref, f32[1024,256]{1,0:T(8,128)} %fusion.12.mask_ref), custom_call_target="tpu_custom_call" | custom-call | tf_op jit(solution)/shard_map/attend/pallas_call | solution.py:444
  181.4 15.9 %collective-permute-done.24 = bf16[256,2048]{1,0:T(8,128)(2,1)} collective-permute-done((bf16[256,2048]{1,0:T(8,128)(2,1)S(1)}, bf16[256,2048]{1,0:T(8,128)(2,1)}, u32[]{:S(2)}, u32[]{:S(2)}) %collective-permute-start.24) | collective-permute-done | bytes 1048608 | tf_op jit(solution)/shard_map/ppermute | solution.py:221
  221.4 14.9 %feed_forward.2 = (bf16[2048,1024]{1,0:T(8,128)(2,1)}, bf16[2048,1024]{1,0:T(8,128)(2,1)}) custom-call(bf16[2048,2048]{1,0:T(8,128)(2,1)} %constant_dynamic-update-slice_fusion.22.refs_0_.mid_ref, bf16[2048,1024]{1,0:T(8,128)(2,1)} %bitcast.151, f32[1,1024]{1,0:T(1,128)} %bitcast.157, bf16[2048,2048]{1,0:T(8,128)(2,1)} %all-gather.5.cloned.1.call-done.refs_3_.right_ref, ...), custom_call_target="tpu_custom_call" | custom-call | tf_op jit(solution)/shard_map/feed_forward/pallas_call | solution.py:196
  251.8 15.0 %feed_forward.3 = (bf16[2048,1024]{1,0:T(8,128)(2,1)}, bf16[2048,1024]{1,0:T(8,128)(2,1)}) custom-call(bf16[2048,2048]{1,0:T(8,128)(2,1)} %constant_dynamic-update-slice_fusion.22.refs_0_.mid_ref, bf16[2048,1024]{1,0:T(8,128)(2,1)} %bitcast.152, f32[1,1024]{1,0:T(1,128)} %bitcast.158, ...), custom_call_target="tpu_custom_call", output_to_operand_aliasing={{0}: (5, {}), {1}: (6, {})} | custom-call | tf_op jit(solution)/shard_map/feed_forward/pallas_call | solution.py:196
  269.3 13.4 %matmul_nt.3 = bf16[2048,2048]{1,0:T(8,128)(2,1)} custom-call(bf16[2048,1024]{1,0:T(8,128)(2,1)} %get-tuple-element.253.left_ref.grad_ref, bf16[2048,1024]{1,0:T(8,128)(2,1)} %bitcast.153), custom_call_target="tpu_custom_call" | custom-call | tf_op jit(solution)/shard_map/matmul_nt/pallas_call | solution.py:75
  289.0 16.3 %fc_gradient.1 = bf16[8,256,1024]{2,1,0:T(8,128)(2,1)} custom-call(s32[8]{0:T(128)} %stack.32.order_ref, bf16[2048,2048]{1,0:T(8,128)(2,1)} %constant_dynamic-update-slice_fusion.22.refs_0_.mid_ref, bf16[2048,1024]{1,0:T(8,128)(2,1)} %get-tuple-element.253.left_ref.grad_ref), custom_call_target="tpu_custom_call" | custom-call | tf_op jit(solution)/shard_map/fc_gradient/pallas_call | solution.py:99
  305.2 6.6 matmul_tn.7.refs_4_.refs_0_
  360.6 11.2 %collective-permute-done.49 = bf16[128,1024]{1,0:T(8,128)(2,1)S(1)} collective-permute-done((bf16[128,1024]{1,0:T(8,128)(2,1)S(1)}, bf16[128,1024]{1,0:T(8,128)(2,1)S(1)}, u32[]{:S(2)}, u32[]{:S(2)}) %collective-permute-start.49) | collective-permute-done | bytes 262176 | tf_op jit(solution)/shard_map/ppermute | solution.py:221
  372.6 7.9 %collective-permute-done.46.refs_1_.refs_2_ = bf16[256,2048]{1,0:T(8,128)(2,1)S(1)} collective-permute-done((bf16[256,2048]{1,0:T(8,128)(2,1)S(1)}, bf16[256,2048]{1,0:T(8,128)(2,1)S(1)}, u32[]{:S(2)}, u32[]{:S(2)}) %collective-permute-start.46) | collective-permute-done | bytes 1048608 | tf_op jit(solution)/shard_map/ppermute | solution.py:392
  383.6 7.0 %collective-permute-done.53 = bf16[128,1024]{1,0:T(8,128)(2,1)S(1)} collective-permute-done((bf16[128,1024]{1,0:T(8,128)(2,1)S(1)}, bf16[128,1024]{1,0:T(8,128)(2,1)S(1)}, u32[]{:S(2)}, u32[]{:S(2)}) %collective-permute-start.53) | collective-permute-done | bytes 262176 | tf_op jit(solution)/shard_map/ppermute | solution.py:221
  393.8 7.3 %collective-permute-start.55 = (bf16[128,4096]{1,0:T(8,128)(2,1)S(1)}, bf16[128,4096]{1,0:T(8,128)(2,1)}, u32[]{:S(2)}, u32[]{:S(2)}) collective-permute-start(bf16[128,4096]{1,0:T(8,128)(2,1)S(1)} %pad_maximum_fusion.2.refs_0_), channel_id=1, source_target_pairs={{0,8},{24,16},{1,9},{25,17},{2,10},{26,18},{3,11},{27,19},{4,12},{... | collective-permute-start | bytes 3145736 | tf_op jit(solution)/shard_map/ppermute | solution.py:395
  411.6 6.6 matmul_tn.9
  418.1 6.8 matmul_nt.4.grad_ref
  443.6 17.5 %attend_back.1 = (bf16[256,2048]{1,0:T(8,128)(2,1)}, f32[1024,128]{1,0:T(8,128)}, f32[1024,128]{1,0:T(8,128)}) custom-call(bf16[256,2304]{1,0:T(8,128)(2,1)} %copy-done.31, bf16[256,2048]{1,0:T(8,128)(2,1)} %matmul_nt.4.grad_ref, bf16[256,2048]{1,0:T(8,128)(2,1)} %get-tuple-element.208.left_ref.out_ref, f32[16,1,256]{2,1,0:T(1,128)} %get-tuple-element.300.total_ref, ...), custom_call_target="tpu_custom_call" | custom-call | tf_op jit(solution)/shard_map/attend_back/pallas_call | solution.py:500
  469.1 7.1 %matmul_nt.5.grad_ref = f32[256,2048]{1,0:T(8,128)} custom-call(bf16[256,2048]{1,0:T(8,128)(2,1)} %get-tuple-element.314.left_ref, bf16[2048,2304]{1,0:T(8,128)(2,1)} %all-gather.3.cloned.1.call-done.right_ref.refs_1_), custom_call_target="tpu_custom_call" | custom-call | tf_op jit(solution)/shard_map/matmul_nt/pallas_call | solution.py:75
  484.8 9.2 %collective-permute-done.62 = bf16[256,256]{1,0:T(8,128)(2,1)S(1)} collective-permute-done((bf16[256,256]{1,0:T(8,128)(2,1)S(1)}, bf16[256,256]{1,0:T(8,128)(2,1)S(1)}, u32[]{:S(2)}, u32[]{:S(2)}) %collective-permute-start.62) | collective-permute-done | bytes 131104 | tf_op jit(solution)/shard_map/ppermute | solution.py:758
  504.6 9.4 %attn_gradient.1 = bf16[8,272,2304]{2,1,0:T(8,128)(2,1)} custom-call(bf16[256,2048]{1,0:T(8,128)(2,1)} %copy-done.34, bf16[256,2304]{1,0:T(8,128)(2,1)} %pad_maximum_fusion.1.grad_ref, bf16[8,16,2304]{2,1,0:T(8,128)(2,1)} %fusion.13.extra_ref), custom_call_target="tpu_custom_call" | custom-call | tf_op jit(solution)/shard_map/attn_gradient/pallas_call | solution.py:126
  518.2 19.5 %collective-permute-done.64.refs_1_.refs_0_ = bf16[128,4096]{1,0:T(8,128)(2,1)S(1)} collective-permute-done((bf16[128,4096]{1,0:T(8,128)(2,1)}, bf16[128,4096]{1,0:T(8,128)(2,1)S(1)}, u32[]{:S(2)}, u32[]{:S(2)}) %collective-permute-start.64) | collective-permute-done | bytes 1048608 | tf_op jit(solution)/shard_map/ppermute | solution.py:392
  543.6 13.4 %matmul_nn.1 = bf16[2048,2048]{1,0:T(8,128)(2,1)} custom-call(bf16[2048,1024]{1,0:T(8,128)(2,1)} %get-tuple-element.339.left_ref, bf16[1024,2048]{1,0:T(8,128)(2,1)} %right_ref.1), custom_call_target="tpu_custom_call" | custom-call | tf_op jit(solution)/shard_map/matmul_nn/pallas_call | solution.py:75
  568.3 7.0 %collective-permute-start.68 = (bf16[256,2048]{1,0:T(8,128)(2,1)}, bf16[256,2048]{1,0:T(8,128)(2,1)S(1)}, u32[]{:S(2)}, u32[]{:S(2)}) collective-permute-start(bf16[256,2048]{1,0:T(8,128)(2,1)} %reduce-scatter.9.cloned.1.call-done.refs_0_), channel_id=1, source_target_pairs={{0,8},{24,16},{1,9},{25,17},{2,10},{26,18},{3,11},{27,19},{4,12},{... | collective-permute-start | bytes 3145736 | tf_op jit(solution)/shard_map/ppermute | solution.py:395
  576.5 7.8 %finish.2 = f32[1024,2048]{1,0:T(8,128)} custom-call(s32[1]{0:T(128)} %bitcast.33.at_end_ref.ends_ref, s32[8]{0:T(128)} %stack.32.order_ref, bf16[256,2048]{1,0:T(8,128)(2,1)} %copy-done.7, bf16[256,2048]{1,0:T(8,128)(2,1)} %copy-done.11, bf16[256,2048]{1,0:T(8,128)(2,1)} %copy-done.3, bf16[256,2048]{1,0:T(8,128)(2,1)} %copy-done.12, ...), custom_call_target="tpu_custom_call" | custom-call | tf_op jit(solution)/shard_map/finish/pallas_call | solution.py:164
  584.6 9.6 %collective-permute-done.68.refs_1_ = bf16[256,2048]{1,0:T(8,128)(2,1)S(1)} collective-permute-done((bf16[256,2048]{1,0:T(8,128)(2,1)}, bf16[256,2048]{1,0:T(8,128)(2,1)S(1)}, u32[]{:S(2)}, u32[]{:S(2)}) %collective-permute-start.68) | collective-permute-done | bytes 1048608 | tf_op jit(solution)/shard_map/ppermute | solution.py:395
  606.3 7.8 %collective-permute-done.71.refs_1_ = bf16[144,2304]{1,0:T(8,128)(2,1)S(1)} collective-permute-done((bf16[144,2304]{1,0:T(8,128)(2,1)S(1)}, bf16[144,2304]{1,0:T(8,128)(2,1)S(1)}, u32[]{:S(2)}, u32[]{:S(2)}) %collective-permute-start.71) | collective-permute-done | bytes 663584 | tf_op jit(solution)/shard_map/ppermute | solution.py:395
  614.6 7.9 %collective-permute-done.73.refs_6_ = bf16[128,4096]{1,0:T(8,128)(2,1)S(1)} collective-permute-done((bf16[128,4096]{1,0:T(8,128)(2,1)S(1)}, bf16[128,4096]{1,0:T(8,128)(2,1)S(1)}, u32[]{:S(2)}, u32[]{:S(2)}) %collective-permute-start.73) | collective-permute-done | bytes 1048608 | tf_op jit(solution)/shard_map/ppermute | solution.py:397
  624.5 7.0 %collective-permute-start.74 = (bf16[128,2304]{1,0:T(8,128)(2,1)S(1)}, bf16[128,2304]{1,0:T(8,128)(2,1)S(1)}, u32[]{:S(2)}, u32[]{:S(2)}) collective-permute-start(bf16[128,2304]{1,0:T(8,128)(2,1)S(1)} %slice.285.refs_0_), channel_id=1, source_target_pairs={{0,8},{24,16},{1,9},{25,17},{2,10},{26,18},{3,11},{27,19},{4,12},{... | collective-permute-start | bytes 1769480 | tf_op jit(solution)/shard_map/ppermute | solution.py:395
  631.6 7.3 %collective-permute-done.74.refs_1_ = bf16[128,2304]{1,0:T(8,128)(2,1)S(1)} collective-permute-done((bf16[128,2304]{1,0:T(8,128)(2,1)S(1)}, bf16[128,2304]{1,0:T(8,128)(2,1)S(1)}, u32[]{:S(2)}, u32[]{:S(2)}) %collective-permute-start.74) | collective-permute-done | bytes 589856 | tf_op jit(solution)/shard_map/ppermute | solution.py:395
  639.2 6.5 collective-permute-done.76
  647.8 8.0 %finish.3 = f32[256,8192]{1,0:T(8,128)} custom-call(s32[1]{0:T(128)} %bitcast.33.at_end_ref.ends_ref, s32[8]{0:T(128)} %stack.32.order_ref, bf16[128,4096]{1,0:T(8,128)(2,1)} %copy-done.8, bf16[128,4096]{1,0:T(8,128)(2,1)} %get-tuple-element.370.refs_1_, bf16[128,4096]{1,0:T(8,128)(2,1)} %copy-done.4, bf16[128,4096]{1,0:T(8,128)(2,1)} %get-tuple-element.372.refs_3_, ...), custom_call_target="tpu_custom_call" | custom-call | tf_op jit(solution)/shard_map/finish/pallas_call | solution.py:164
  663.6 9.4 %collective-permute-done.79 = bf16[128,2304]{1,0:T(8,128)(2,1)S(1)} collective-permute-done((bf16[128,2304]{1,0:T(8,128)(2,1)S(1)}, bf16[128,2304]{1,0:T(8,128)(2,1)S(1)}, u32[]{:S(2)}, u32[]{:S(2)}) %collective-permute-start.79) | collective-permute-done | bytes 589856 | tf_op jit(solution)/shard_map/ppermute | solution.py:397
  (528 shorter events, 329.5 us)
Async XLA Ops:
  7.3 74.3 %all-gather.3.cloned.1.call-start = ((), (), s32[]{:S(2)}) async-start(), calls=%async_computation.4 | async-start | bytes 10616832 | tf_op jit(solution)/shard_map/all_gather | solution.py:274
  9.7 211.7 %all-gather.5.cloned.1.call-start = ((), (), s32[]{:S(2)}) async-start(), calls=%async_computation.5 | async-start | bytes 9437184 | tf_op jit(solution)/shard_map/all_gather | solution.py:274
  45.2 26.8 %collective-permute-start.10 = (bf16[8,64,1024]{2,1,0:T(8,128)(2,1)S(1)}, bf16[8,64,1024]{2,1,0:T(8,128)(2,1)}, u32[]{:S(2)}, u32[]{:S(2)}) collective-permute-start(bf16[8,64,1024]{2,1,0:T(8,128)(2,1)S(1)} %bitcast_dynamic-update-slice_fusion.4), channel_id=1, source_target_pairs={{0,8},{8,16},{16,24},{24,0},{1,9},{9,17},{17,25},{25,1},{2,10},{10... | collective-permute-start | bytes 3145736 | tf_op jit(solution)/shard_map/ppermute | solution.py:326
  81.6 311.5 %reduce-scatter.5.cloned.1.call-start = ((), (), s32[]{:S(2)}) async-start(), calls=%async_computation.6 | async-start | bytes 9437184 | tf_op jit(solution)/shard_map/reduce_scatter | solution.py:285
  85.2 36.9 %collective-permute-start.14 = (bf16[256,2048]{1,0:T(8,128)(2,1)}, bf16[256,2048]{1,0:T(8,128)(2,1)}, u32[]{:S(2)}, u32[]{:S(2)}) collective-permute-start(bf16[256,2048]{1,0:T(8,128)(2,1)} %own_ref), channel_id=1, source_target_pairs={{0,2},{1,3},{2,0},{3,1},{4,6},{5,7},{6,4},{7,5},{8,10},{9,11},{10,... | collective-permute-start | bytes 3145736 | tf_op jit(solution)/shard_map/ppermute | solution.py:221
  86.8 36.6 %collective-permute-start.15 = (bf16[256,2048]{1,0:T(8,128)(2,1)}, bf16[256,2048]{1,0:T(8,128)(2,1)}, u32[]{:S(2)}, u32[]{:S(2)}) collective-permute-start(bf16[256,2048]{1,0:T(8,128)(2,1)} %own_ref), channel_id=1, source_target_pairs={{0,4},{1,5},{2,6},{3,7},{4,0},{5,1},{6,2},{7,3},{8,12},{9,13},{10,... | collective-permute-start | bytes 3145736 | tf_op jit(solution)/shard_map/ppermute | solution.py:221
  102.2 28.2 %collective-permute-start.16 = (bf16[256,2048]{1,0:T(8,128)(2,1)}, bf16[256,2048]{1,0:T(8,128)(2,1)S(1)}, u32[]{:S(2)}, u32[]{:S(2)}) collective-permute-start(bf16[256,2048]{1,0:T(8,128)(2,1)} %own_ref), channel_id=1, source_target_pairs={{0,1},{1,0},{2,3},{3,2},{4,5},{5,4},{6,7},{7,6},{8,9},{9,8},{10,11... | collective-permute-start | bytes 3145736 | tf_op jit(solution)/shard_map/ppermute | solution.py:221
  123.4 31.7 %collective-permute-start.17 = (bf16[256,2048]{1,0:T(8,128)(2,1)}, bf16[256,2048]{1,0:T(8,128)(2,1)}, u32[]{:S(2)}, u32[]{:S(2)}) collective-permute-start(bf16[256,2048]{1,0:T(8,128)(2,1)} %collective-permute-done.14), channel_id=1, source_target_pairs={{0,1},{1,0},{2,3},{3,2},{4,5},{5,4},{6,7},{7,6},{8,9},{9,8},{10,11... | collective-permute-start | bytes 3145736 | tf_op jit(solution)/shard_map/ppermute | solution.py:221
  125.3 32.1 %collective-permute-start.18 = (bf16[256,2048]{1,0:T(8,128)(2,1)}, bf16[256,2048]{1,0:T(8,128)(2,1)S(1)}, u32[]{:S(2)}, u32[]{:S(2)}) collective-permute-start(bf16[256,2048]{1,0:T(8,128)(2,1)} %collective-permute-done.15), channel_id=1, source_target_pairs={{0,1},{1,0},{2,3},{3,2},{4,5},{5,4},{6,7},{7,6},{8,9},{9,8},{10,11... | collective-permute-start | bytes 3145736 | tf_op jit(solution)/shard_map/ppermute | solution.py:221
  127.6 26.9 %collective-permute-start.19 = (bf16[128,2048]{1,0:T(8,128)(2,1)}, bf16[128,2048]{1,0:T(8,128)(2,1)}, u32[]{:S(2)}, u32[]{:S(2)}) collective-permute-start(bf16[128,2048]{1,0:T(8,128)(2,1)} %slice.218), channel_id=1, source_target_pairs={{0,4},{1,5},{2,6},{3,7},{4,0},{5,1},{6,2},{7,3},{8,12},{9,13},{10,... | collective-permute-start | bytes 1572872 | tf_op jit(solution)/shard_map/ppermute | solution.py:221
  128.4 26.2 %collective-permute-start.20 = (bf16[128,2048]{1,0:T(8,128)(2,1)}, bf16[128,2048]{1,0:T(8,128)(2,1)}, u32[]{:S(2)}, u32[]{:S(2)}) collective-permute-start(bf16[128,2048]{1,0:T(8,128)(2,1)} %slice.219), channel_id=1, source_target_pairs={{0,2},{1,3},{2,0},{3,1},{4,6},{5,7},{6,4},{7,5},{8,10},{9,11},{10,... | collective-permute-start | bytes 1572872 | tf_op jit(solution)/shard_map/ppermute | solution.py:221
  130.5 41.6 %collective-permute-start.23 = (bf16[8,64,1024]{2,1,0:T(8,128)(2,1)}, bf16[8,64,1024]{2,1,0:T(8,128)(2,1)}, u32[]{:S(2)}, u32[]{:S(2)}) collective-permute-start(bf16[8,64,1024]{2,1,0:T(8,128)(2,1)} %collective-permute-done.10), channel_id=1, source_target_pairs={{0,8},{8,16},{16,24},{24,0},{1,9},{9,17},{17,25},{25,1},{2,10},{10... | collective-permute-start | bytes 3145736 | tf_op jit(solution)/shard_map/ppermute | solution.py:326
  172.0 25.3 %collective-permute-start.24 = (bf16[256,2048]{1,0:T(8,128)(2,1)S(1)}, bf16[256,2048]{1,0:T(8,128)(2,1)}, u32[]{:S(2)}, u32[]{:S(2)}) collective-permute-start(bf16[256,2048]{1,0:T(8,128)(2,1)S(1)} %get-tuple-element.216.own_ref), channel_id=1, source_target_pairs={{0,2},{1,3},{2,0},{3,1},{4,6},{5,7},{6,4},{7,5},{8,10},{9,11},{10,... | collective-permute-start | bytes 3145736 | tf_op jit(solution)/shard_map/ppermute | solution.py:221
  173.0 24.9 %collective-permute-start.25 = (bf16[256,2048]{1,0:T(8,128)(2,1)S(1)}, bf16[256,2048]{1,0:T(8,128)(2,1)S(1)}, u32[]{:S(2)}, u32[]{:S(2)}) collective-permute-start(bf16[256,2048]{1,0:T(8,128)(2,1)S(1)} %get-tuple-element.216.own_ref), channel_id=1, source_target_pairs={{0,4},{1,5},{2,6},{3,7},{4,0},{5,1},{6,2},{7,3},{8,12},{9,13},{10,... | collective-permute-start | bytes 3145736 | tf_op jit(solution)/shard_map/ppermute | solution.py:221
  174.3 28.0 %collective-permute-start.26 = (bf16[256,2048]{1,0:T(8,128)(2,1)S(1)}, bf16[256,2048]{1,0:T(8,128)(2,1)}, u32[]{:S(2)}, u32[]{:S(2)}) collective-permute-start(bf16[256,2048]{1,0:T(8,128)(2,1)S(1)} %get-tuple-element.216.own_ref), channel_id=1, source_target_pairs={{0,1},{1,0},{2,3},{3,2},{4,5},{5,4},{6,7},{7,6},{8,9},{9,8},{10,11... | collective-permute-start | bytes 3145736 | tf_op jit(solution)/shard_map/ppermute | solution.py:221
  174.9 33.7 %collective-permute-start.33 = (bf16[8,64,1024]{2,1,0:T(8,128)(2,1)}, bf16[8,64,1024]{2,1,0:T(8,128)(2,1)}, u32[]{:S(2)}, u32[]{:S(2)}) collective-permute-start(bf16[8,64,1024]{2,1,0:T(8,128)(2,1)} %collective-permute-done.23), channel_id=1, source_target_pairs={{0,8},{8,16},{16,24},{24,0},{1,9},{9,17},{17,25},{25,1},{2,10},{10... | collective-permute-start | bytes 3145736 | tf_op jit(solution)/shard_map/ppermute | solution.py:326
  242.2 26.8 %collective-permute-start.34 = (bf16[256,2048]{1,0:T(8,128)(2,1)}, bf16[256,2048]{1,0:T(8,128)(2,1)S(1)}, u32[]{:S(2)}, u32[]{:S(2)}) collective-permute-start(bf16[256,2048]{1,0:T(8,128)(2,1)} %matmul_tn.5.refs_0_), channel_id=1, source_target_pairs={{0,8},{24,16},{1,9},{25,17},{2,10},{26,18},{3,11},{27,19},{4,12},{... | collective-permute-start | bytes 3145736 | tf_op jit(solution)/shard_map/ppermute | solution.py:395
  282.7 284.7 %reduce-scatter.9.cloned.1.call-start = ((), (), s32[]{:S(2)}) async-start(), calls=%async_computation.8 | async-start | bytes 9437184 | tf_op jit(solution)/shard_map/reduce_scatter | solution.py:285
  283.9 27.9 %collective-permute-start.35 = (bf16[256,2048]{1,0:T(8,128)(2,1)S(1)}, bf16[256,2048]{1,0:T(8,128)(2,1)S(1)}, u32[]{:S(2)}, u32[]{:S(2)}) collective-permute-start(bf16[256,2048]{1,0:T(8,128)(2,1)S(1)} %copy-done.10), channel_id=1, source_target_pairs={{0,8},{24,16},{1,9},{25,17},{2,10},{26,18},{3,11},{27,19},{4,12},{... | collective-permute-start | bytes 3145736 | tf_op jit(solution)/shard_map/ppermute | solution.py:395
  313.6 24.8 %collective-permute-start.37 = (bf16[256,2048]{1,0:T(8,128)(2,1)S(1)}, bf16[256,2048]{1,0:T(8,128)(2,1)S(1)}, u32[]{:S(2)}, u32[]{:S(2)}) collective-permute-start(bf16[256,2048]{1,0:T(8,128)(2,1)S(1)} %get-tuple-element.344.refs_1_), channel_id=1, source_target_pairs={{0,8},{24,16},{8,0},{16,24},{1,9},{25,17},{9,1},{17,25},{2,10},{26... | collective-permute-start | bytes 3145736 | tf_op jit(solution)/shard_map/ppermute | solution.py:392
  318.0 25.0 %collective-permute-start.41 = (bf16[128,1024]{1,0:T(8,128)(2,1)S(1)}, bf16[128,1024]{1,0:T(8,128)(2,1)S(1)}, u32[]{:S(2)}, u32[]{:S(2)}) collective-permute-start(bf16[128,1024]{1,0:T(8,128)(2,1)S(1)} %get-tuple-element.396), channel_id=1, source_target_pairs={{0,3},{1,2},{2,1},{3,0},{4,7},{5,6},{6,5},{7,4},{8,11},{9,10},{10,... | collective-permute-start | bytes 786440 | tf_op jit(solution)/shard_map/ppermute | solution.py:221
  355.3 25.2 %collective-permute-start.46 = (bf16[256,2048]{1,0:T(8,128)(2,1)S(1)}, bf16[256,2048]{1,0:T(8,128)(2,1)S(1)}, u32[]{:S(2)}, u32[]{:S(2)}) collective-permute-start(bf16[256,2048]{1,0:T(8,128)(2,1)S(1)} %get-tuple-element.346.refs_3_), channel_id=1, source_target_pairs={{0,8},{24,16},{8,0},{16,24},{1,9},{25,17},{9,1},{17,25},{2,10},{26... | collective-permute-start | bytes 3145736 | tf_op jit(solution)/shard_map/ppermute | solution.py:392
  356.9 24.8 %collective-permute-start.47 = (bf16[256,2048]{1,0:T(8,128)(2,1)S(1)}, bf16[256,2048]{1,0:T(8,128)(2,1)S(1)}, u32[]{:S(2)}, u32[]{:S(2)}) collective-permute-start(bf16[256,2048]{1,0:T(8,128)(2,1)S(1)} %get-tuple-element.260.refs_2_), channel_id=1, source_target_pairs={{8,16},{16,8},{9,17},{17,9},{10,18},{18,10},{11,19},{19,11},{12,20... | collective-permute-start | bytes 3145736 | tf_op jit(solution)/shard_map/ppermute | solution.py:401
  358.8 24.8 %collective-permute-start.50 = (bf16[128,1024]{1,0:T(8,128)(2,1)S(1)}, bf16[128,1024]{1,0:T(8,128)(2,1)S(1)}, u32[]{:S(2)}, u32[]{:S(2)}) collective-permute-start(bf16[128,1024]{1,0:T(8,128)(2,1)S(1)} %get-tuple-element.388), channel_id=1, source_target_pairs={{0,3},{1,2},{2,1},{3,0},{4,7},{5,6},{6,5},{7,4},{8,11},{9,10},{10,... | collective-permute-start | bytes 786440 | tf_op jit(solution)/shard_map/ppermute | solution.py:221
  393.1 32.9 %collective-permute-start.56 = (bf16[256,2048]{1,0:T(8,128)(2,1)}, bf16[256,2048]{1,0:T(8,128)(2,1)S(1)}, u32[]{:S(2)}, u32[]{:S(2)}) collective-permute-start(bf16[256,2048]{1,0:T(8,128)(2,1)} %copy-done.15), channel_id=1, source_target_pairs={{8,16},{16,8},{9,17},{17,9},{10,18},{18,10},{11,19},{19,11},{12,20... | collective-permute-start | bytes 3145736 | tf_op jit(solution)/shard_map/ppermute | solution.py:401
  393.8 34.7 %collective-permute-start.55 = (bf16[128,4096]{1,0:T(8,128)(2,1)S(1)}, bf16[128,4096]{1,0:T(8,128)(2,1)}, u32[]{:S(2)}, u32[]{:S(2)}) collective-permute-start(bf16[128,4096]{1,0:T(8,128)(2,1)S(1)} %pad_maximum_fusion.2.refs_0_), channel_id=1, source_target_pairs={{0,8},{24,16},{1,9},{25,17},{2,10},{26,18},{3,11},{27,19},{4,12},{... | collective-permute-start | bytes 3145736 | tf_op jit(solution)/shard_map/ppermute | solution.py:395
  401.1 30.3 %collective-permute-start.57 = (bf16[256,2048]{1,0:T(8,128)(2,1)S(1)}, bf16[256,2048]{1,0:T(8,128)(2,1)}, u32[]{:S(2)}, u32[]{:S(2)}) collective-permute-start(bf16[256,2048]{1,0:T(8,128)(2,1)S(1)} %get-tuple-element.348.refs_5_), channel_id=1, source_target_pairs={{8,0},{16,24},{9,1},{17,25},{10,2},{18,26},{11,3},{19,27},{12,4},{... | collective-permute-start | bytes 3145736 | tf_op jit(solution)/shard_map/ppermute | solution.py:397
  431.4 163.2 %reduce-scatter.7.cloned.1.call-start = ((), (), s32[]{:S(2)}) async-start(), calls=%async_computation.7 | async-start | bytes 11280384 | tf_op jit(solution)/shard_map/reduce_scatter | solution.py:285
  434.8 28.6 %collective-permute-start.58 = (bf16[128,4096]{1,0:T(8,128)(2,1)}, bf16[128,4096]{1,0:T(8,128)(2,1)S(1)}, u32[]{:S(2)}, u32[]{:S(2)}) collective-permute-start(bf16[128,4096]{1,0:T(8,128)(2,1)} %pad_maximum_fusion.3.refs_0_), channel_id=1, source_target_pairs={{0,8},{24,16},{1,9},{25,17},{2,10},{26,18},{3,11},{27,19},{4,12},{... | collective-permute-start | bytes 3145736 | tf_op jit(solution)/shard_map/ppermute | solution.py:395
  442.0 27.0 %collective-permute-start.60 = (bf16[256,2048]{1,0:T(8,128)(2,1)S(1)}, bf16[256,2048]{1,0:T(8,128)(2,1)}, u32[]{:S(2)}, u32[]{:S(2)}) collective-permute-start(bf16[256,2048]{1,0:T(8,128)(2,1)S(1)} %tick.21.refs_7_), channel_id=1, source_target_pairs={{8,0},{16,24},{9,1},{17,25},{10,2},{18,26},{11,3},{19,27},{12,4},{... | collective-permute-start | bytes 3145736 | tf_op jit(solution)/shard_map/ppermute | solution.py:397
  514.0 163.1 %reduce-scatter.11.cloned.1.call-start = ((), (), s32[]{:S(2)}) async-start(), calls=%async_computation.9 | async-start | bytes 9437184 | tf_op jit(solution)/shard_map/reduce_scatter | solution.py:285
  568.3 26.0 %collective-permute-start.68 = (bf16[256,2048]{1,0:T(8,128)(2,1)}, bf16[256,2048]{1,0:T(8,128)(2,1)S(1)}, u32[]{:S(2)}, u32[]{:S(2)}) collective-permute-start(bf16[256,2048]{1,0:T(8,128)(2,1)} %reduce-scatter.9.cloned.1.call-done.refs_0_), channel_id=1, source_target_pairs={{0,8},{24,16},{1,9},{25,17},{2,10},{26,18},{3,11},{27,19},{4,12},{... | collective-permute-start | bytes 3145736 | tf_op jit(solution)/shard_map/ppermute | solution.py:395
  (146 other events, 1744.8 us)
Sparse Core Ops, SparseCore 0:
  10.6 70.9 all-gather.2
  83.5 76.9 all-gather.4
  282.8 89.3 reduce-scatter.4
  431.5 70.8 reduce-scatter.8
  514.2 75.4 reduce-scatter.6
  598.6 69.7 reduce-scatter.10

commit v4 on v3

--- a/solution.py
+++ b/solution.py
@@ -114,13 +114,15 @@
     )(member_order(), mid_all, grad_pre)
 
 
-def attn_gradient(normed_in, grad_projected, extra):
+def attn_gradient(normed_in, grad_query, grad_pair, extra):
     peers = lax.axis_size("fsdp")
     rows, width = normed_in.shape
-    step, cols, more = width // peers, grad_projected.shape[1], extra.shape[1]
-
-    def body(normed_ref, grad_ref, extra_ref, out_ref):
-        out_ref[0, :step] = product_tn(normed_ref[...], grad_ref[...]).astype(LOW)
+    query_cols, pair_cols = grad_query.shape[1], grad_pair.shape[1]
+    step, cols, more = width // peers, query_cols + pair_cols, extra.shape[1]
+
+    def body(normed_ref, query_ref, pair_ref, extra_ref, out_ref):
+        out_ref[0, :step, :query_cols] = product_tn(normed_ref[...], query_ref[...]).astype(LOW)
+        out_ref[0, :step, query_cols:] = product_tn(normed_ref[...], pair_ref[...]).astype(LOW)
         out_ref[0, step:] = extra_ref[0]
 
     return pl.pallas_call(
@@ -128,7 +130,8 @@
         grid=(peers,),
         in_specs=[
             pl.BlockSpec((rows, step), lambda k: (0, k)),
-            pl.BlockSpec((rows, cols), lambda k: (0, 0)),
+            pl.BlockSpec((rows, query_cols), lambda k: (0, 0)),
+            pl.BlockSpec((rows, pair_cols), lambda k: (0, 0)),
             pl.BlockSpec((1, more, cols), lambda k: (k, 0, 0)),
         ],
         out_specs=pl.BlockSpec((1, step + more, cols), lambda k: (k, 0, 0)),
@@ -136,7 +139,7 @@
         compiler_params=ROOMY,
         cost_estimate=QUICK,
         name="attn_gradient",
-    )(normed_in, grad_projected, extra)
+    )(normed_in, grad_query, grad_pair, extra)
 
 
 def finish(ends, pairs, across, parts=1):
@@ -776,7 +779,6 @@
         attn_all,
         LOW,
     )
-    grad_projected = jnp.concatenate([grad_query_low, grad_pair_low], axis=1)
     pair_sum = jnp.sum(grad_pair_low.astype(FULL), axis=0)
     vector_terms = [
         query_sum,
@@ -792,14 +794,14 @@
         + [pair_sum[HD:].reshape(peers, HD // peers)],
         axis=1,
     )
-    used, extra_cols = by_member.shape[1], grad_projected.shape[1]
+    used, extra_cols = by_member.shape[1], attn_all.shape[1]
     by_member = jnp.pad(by_member, ((0, 0), (0, extra_cols - used)))
     grad_fc_bias = jnp.pad(grad_fc_bias, (0, extra_cols - ff_share))
     is_own = jnp.arange(peers)[:, None] == lax.axis_index("fsdp")
     fc_bias_rows = jnp.where(is_own, grad_fc_bias[None], 0.0)
     extra = jnp.stack([by_member, fc_bias_rows], axis=1).astype(LOW)
     extra = jnp.pad(extra, ((0, 0), (0, 14), (0, 0)))
-    attn_term = attn_gradient(normed_in, grad_projected, extra)
+    attn_term = attn_gradient(normed_in, grad_query_low, grad_pair_low, extra)
     attn_rows = attn_term.shape[1]
     attn_term = attn_term.reshape(peers * attn_rows, extra_cols)
     attn_share = scatter_rows(attn_term)

time: 698 us -> 702 us (level)
  local copies, waits for them, and re-layouts: 69.3 us -> 79.5 us
    unnamed x217 -> x181, local copies, waits for them, and re-layouts: 16.5 us -> 20.7 us
  transfers between devices with their start and end apart: 86 -> 86, of which waited for: 37 -> 35; matrix products, arithmetic and copies ran while one was open for 15% -> 16% of each run, Pallas kernels for 25% -> 25%
where the time goes in v4:
time: 702 us; the launch traced here: 691 us
  waiting for transfers between devices  224 us (32%)
  Pallas kernels  211 us (30%)
  starting transfers between devices  116 us (17%)
  local copies, waits for them, and re-layouts  79.5 us (11%)
  other arithmetic  31.6 us (5%)
  between operations  16.2 us (2%)
  matrix products  13.3 us (2%)
    ppermute x42, waiting for transfers between devices, swap(): return lax.ppermute(array, 'fsdp', [(i, i ^ bits) for i in range(8)])  79.7 us
    pallas_call x9, Pallas kernels, matmul(): pl.pallas_call(body, grid=(cols // step_cols, rows // step_rows), in_spec...  72 us
    ppermute x4, waiting for transfers between devices, move(): from_end = from_middle = lax.ppermute(outgoing, 'ctx', inward + outward)  40.5 us
    ppermute x7, starting transfers between devices, move(): from_end = lax.ppermute(incoming, 'ctx', inward)  38.5 us
    ppermute x42, starting transfers between devices, swap(): return lax.ppermute(array, 'fsdp', [(i, i ^ bits) for i in range(8)])  30.1 us
    pallas_call x2, Pallas kernels, feed_forward(): pl.pallas_call(body, grid=(rows // step_rows,), in_specs=[by_row, pl.Bloc...  30 us
    ppermute x7, waiting for transfers between devices, move(): from_middle = lax.ppermute(outgoing, 'ctx', outward)  29.2 us
    ppermute x7, waiting for transfers between devices, move(): from_end = lax.ppermute(incoming, 'ctx', inward)  28.5 us
  transfers between devices with their start and end apart: 86, of which 35 were waited for; matrix products, arithmetic and copies ran while one was open for 16% of the time, Pallas kernels for 25%

profile of v4, /device:TPU:0, one launch (start us, length us, event | category | flops | bytes accessed | tf_op | source)
XLA Modules:
  0.0 691.2 jit_solution(13927470905008152066)
XLA Ops:
  50.2 25.6 %collective-permute-done.10 = bf16[8,64,1024]{2,1,0:T(8,128)(2,1)} collective-permute-done((bf16[8,64,1024]{2,1,0:T(8,128)(2,1)S(1)}, bf16[8,64,1024]{2,1,0:T(8,128)(2,1)}, u32[]{:S(2)}, u32[]{:S(2)}) %collective-permute-start.10) | collective-permute-done | bytes 1048608 | tf_op jit(solution)/shard_map/ppermute | solution.py:329
  75.8 7.8 %all-gather.3.cloned.1.call-done.right_ref.refs_1_ = bf16[2048,2304]{1,0:T(8,128)(2,1)} async-done(((bf16[256,2304]{1,0:T(8,128)(2,1)}), bf16[2048,2304]{1,0:T(8,128)(2,1)}) %all-gather.3.cloned.1.call-update) | async-done | bytes 9437200 | tf_op jit(solution)/shard_map/all_gather | solution.py:277
  92.0 7.4 %fusion.query_ref = bf16[256,2304]{1,0:T(8,128)(2,1)S(1)} fusion(bf16[256,2048]{1,0:T(8,128)(2,1)S(1)} %get-tuple-element.415.normed_ref, bf16[2048,2304]{1,0:T(8,128)(2,1)} %all-gather.3.cloned.1.call-done.right_ref.refs_1_, f32[2304]{0:T(1024)S(1)} %pad_maximum_fusion.6), kind=kOutput, calls=%fused_computation.2 | convolution fusion | flops 2417098752 | bytes 11674624 | tf_op jit(solution)/shard_map/dot_general | solution.py:26
  117.7 6.5 collective-permute-done.14
  136.4 15.6 %attend.1 = (bf16[256,2048]{1,0:T(8,128)(2,1)}, f32[16,1,256]{2,1,0:T(1,128)}) custom-call(bf16[256,2304]{1,0:T(8,128)(2,1)} %copy-done.24, bf16[1024,128]{1,0:T(8,128)(2,1)} %get-tuple-element.422.key_ref, bf16[128,1024]{1,0:T(8,128)(2,1)} %copy.40.value_t_ref, f32[1024,256]{1,0:T(8,128)} %fusion.12.mask_ref), custom_call_target="tpu_custom_call" | custom-call | tf_op jit(solution)/shard_map/attend/pallas_call | solution.py:447
  190.7 11.9 %collective-permute-done.24 = bf16[256,2048]{1,0:T(8,128)(2,1)} collective-permute-done((bf16[256,2048]{1,0:T(8,128)(2,1)S(1)}, bf16[256,2048]{1,0:T(8,128)(2,1)}, u32[]{:S(2)}, u32[]{:S(2)}) %collective-permute-start.24) | collective-permute-done | bytes 1048608 | tf_op jit(solution)/shard_map/ppermute | solution.py:224
  226.3 15.0 %feed_forward.2 = (bf16[2048,1024]{1,0:T(8,128)(2,1)}, bf16[2048,1024]{1,0:T(8,128)(2,1)}) custom-call(bf16[2048,2048]{1,0:T(8,128)(2,1)} %constant_dynamic-update-slice_fusion.22.refs_0_.mid_ref, bf16[2048,1024]{1,0:T(8,128)(2,1)} %bitcast.30.refs_1_.right_ref, f32[1,1024]{1,0:T(1,128)} %bitcast.154, ...), custom_call_target="tpu_custom_call" | custom-call | tf_op jit(solution)/shard_map/feed_forward/pallas_call | solution.py:199
  256.7 15.0 %feed_forward.3 = (bf16[2048,1024]{1,0:T(8,128)(2,1)}, bf16[2048,1024]{1,0:T(8,128)(2,1)}) custom-call(bf16[2048,2048]{1,0:T(8,128)(2,1)} %constant_dynamic-update-slice_fusion.22.refs_0_.mid_ref, bf16[2048,1024]{1,0:T(8,128)(2,1)} %bitcast.30.refs_1_.right_ref, f32[1,1024]{1,0:T(1,128)} %bitcast.155, ...), custom_call_target="tpu_custom_call", output_to_operand_aliasing={{0}: (5, {}), {1}: (6, {})} | custom-call | tf_op jit(solution)/shard_map/feed_forward/pallas_call | solution.py:199
  274.2 13.4 %matmul_nt.3 = bf16[2048,2048]{1,0:T(8,128)(2,1)} custom-call(bf16[2048,1024]{1,0:T(8,128)(2,1)} %get-tuple-element.253.left_ref.grad_ref, bf16[2048,1024]{1,0:T(8,128)(2,1)} %bitcast.30.refs_1_.right_ref), custom_call_target="tpu_custom_call" | custom-call | tf_op jit(solution)/shard_map/matmul_nt/pallas_call | solution.py:75
  293.9 16.3 %fc_gradient.1 = bf16[8,256,1024]{2,1,0:T(8,128)(2,1)} custom-call(s32[8]{0:T(128)} %stack.32.order_ref, bf16[2048,2048]{1,0:T(8,128)(2,1)} %constant_dynamic-update-slice_fusion.22.refs_0_.mid_ref, bf16[2048,1024]{1,0:T(8,128)(2,1)} %get-tuple-element.253.left_ref.grad_ref), custom_call_target="tpu_custom_call" | custom-call | tf_op jit(solution)/shard_map/fc_gradient/pallas_call | solution.py:99
  310.3 6.6 matmul_tn.7.refs_4_.refs_0_
  348.3 6.6 collective-permute-done.44
  365.5 11.2 %collective-permute-done.49 = bf16[128,1024]{1,0:T(8,128)(2,1)S(1)} collective-permute-done((bf16[128,1024]{1,0:T(8,128)(2,1)S(1)}, bf16[128,1024]{1,0:T(8,128)(2,1)S(1)}, u32[]{:S(2)}, u32[]{:S(2)}) %collective-permute-start.49) | collective-permute-done | bytes 262176 | tf_op jit(solution)/shard_map/ppermute | solution.py:224
  377.5 8.0 %collective-permute-done.46.refs_1_.refs_2_ = bf16[256,2048]{1,0:T(8,128)(2,1)S(1)} collective-permute-done((bf16[256,2048]{1,0:T(8,128)(2,1)S(1)}, bf16[256,2048]{1,0:T(8,128)(2,1)S(1)}, u32[]{:S(2)}, u32[]{:S(2)}) %collective-permute-start.46) | collective-permute-done | bytes 1048608 | tf_op jit(solution)/shard_map/ppermute | solution.py:395
  388.6 7.0 %collective-permute-done.53 = bf16[128,1024]{1,0:T(8,128)(2,1)S(1)} collective-permute-done((bf16[128,1024]{1,0:T(8,128)(2,1)S(1)}, bf16[128,1024]{1,0:T(8,128)(2,1)S(1)}, u32[]{:S(2)}, u32[]{:S(2)}) %collective-permute-start.53) | collective-permute-done | bytes 262176 | tf_op jit(solution)/shard_map/ppermute | solution.py:224
  399.3 6.7 collective-permute-start.55
  416.6 6.6 matmul_tn.9
  423.2 6.8 matmul_nt.4.grad_ref
  448.3 17.4 %attend_back.1 = (bf16[256,2048]{1,0:T(8,128)(2,1)}, f32[1024,128]{1,0:T(8,128)}, f32[1024,128]{1,0:T(8,128)}) custom-call(bf16[256,2304]{1,0:T(8,128)(2,1)} %copy-done.24, bf16[256,2048]{1,0:T(8,128)(2,1)} %matmul_nt.4.grad_ref, bf16[256,2048]{1,0:T(8,128)(2,1)} %get-tuple-element.208.left_ref.out_ref, f32[16,1,256]{2,1,0:T(1,128)} %get-tuple-element.300.total_ref, ...), custom_call_target="tpu_custom_call" | custom-call | tf_op jit(solution)/shard_map/attend_back/pallas_call | solution.py:503
  473.7 7.1 %matmul_nt.5.grad_ref = f32[256,2048]{1,0:T(8,128)} custom-call(bf16[256,2048]{1,0:T(8,128)(2,1)} %get-tuple-element.314.left_ref.query_ref, bf16[2048,2304]{1,0:T(8,128)(2,1)} %all-gather.3.cloned.1.call-done.right_ref.refs_1_), custom_call_target="tpu_custom_call" | custom-call | tf_op jit(solution)/shard_map/matmul_nt/pallas_call | solution.py:75
  488.5 9.6 %collective-permute-done.62 = bf16[256,256]{1,0:T(8,128)(2,1)S(1)} collective-permute-done((bf16[256,256]{1,0:T(8,128)(2,1)S(1)}, bf16[256,256]{1,0:T(8,128)(2,1)S(1)}, u32[]{:S(2)}, u32[]{:S(2)}) %collective-permute-start.62) | collective-permute-done | bytes 131104 | tf_op jit(solution)/shard_map/ppermute | solution.py:761
  506.6 9.3 %attn_gradient.1 = bf16[8,272,2304]{2,1,0:T(8,128)(2,1)} custom-call(bf16[256,2048]{1,0:T(8,128)(2,1)} %copy-done.27, bf16[256,2048]{1,0:T(8,128)(2,1)} %get-tuple-element.314.left_ref.query_ref, bf16[256,256]{1,0:T(8,128)(2,1)} %copy-done.28, bf16[8,16,2304]{2,1,0:T(8,128)(2,1)} %fusion.13.extra_ref), custom_call_target="tpu_custom_call" | custom-call | tf_op jit(solution)/shard_map/attn_gradient/pallas_call | solution.py:128
  520.1 20.2 %collective-permute-done.64.refs_1_.refs_0_ = bf16[128,4096]{1,0:T(8,128)(2,1)S(1)} collective-permute-done((bf16[128,4096]{1,0:T(8,128)(2,1)}, bf16[128,4096]{1,0:T(8,128)(2,1)S(1)}, u32[]{:S(2)}, u32[]{:S(2)}) %collective-permute-start.64) | collective-permute-done | bytes 1048608 | tf_op jit(solution)/shard_map/ppermute | solution.py:395
  548.4 13.6 %matmul_nn.1 = bf16[2048,2048]{1,0:T(8,128)(2,1)} custom-call(bf16[2048,1024]{1,0:T(8,128)(2,1)} %get-tuple-element.339.left_ref, bf16[1024,2048]{1,0:T(8,128)(2,1)} %right_ref.1), custom_call_target="tpu_custom_call" | custom-call | tf_op jit(solution)/shard_map/matmul_nn/pallas_call | solution.py:75
  572.2 7.1 %collective-permute-start.68 = (bf16[256,2048]{1,0:T(8,128)(2,1)}, bf16[256,2048]{1,0:T(8,128)(2,1)S(1)}, u32[]{:S(2)}, u32[]{:S(2)}) collective-permute-start(bf16[256,2048]{1,0:T(8,128)(2,1)} %reduce-scatter.9.cloned.1.call-done.refs_0_), channel_id=1, source_target_pairs={{0,8},{24,16},{1,9},{25,17},{2,10},{26,18},{3,11},{27,19},{4,12},{... | collective-permute-start | bytes 3145736 | tf_op jit(solution)/shard_map/ppermute | solution.py:398
  580.6 7.8 %finish.2 = f32[1024,2048]{1,0:T(8,128)} custom-call(s32[1]{0:T(128)} %bitcast.33.at_end_ref.ends_ref, s32[8]{0:T(128)} %stack.32.order_ref, bf16[256,2048]{1,0:T(8,128)(2,1)} %copy-done.7, bf16[256,2048]{1,0:T(8,128)(2,1)} %copy-done.11, bf16[256,2048]{1,0:T(8,128)(2,1)} %copy-done.3, bf16[256,2048]{1,0:T(8,128)(2,1)} %copy-done.12, ...), custom_call_target="tpu_custom_call" | custom-call | tf_op jit(solution)/shard_map/finish/pallas_call | solution.py:167
  588.7 10.4 %collective-permute-done.68.refs_1_ = bf16[256,2048]{1,0:T(8,128)(2,1)S(1)} collective-permute-done((bf16[256,2048]{1,0:T(8,128)(2,1)}, bf16[256,2048]{1,0:T(8,128)(2,1)S(1)}, u32[]{:S(2)}, u32[]{:S(2)}) %collective-permute-start.68) | collective-permute-done | bytes 1048608 | tf_op jit(solution)/shard_map/ppermute | solution.py:398
  611.2 8.5 %collective-permute-done.71.refs_1_ = bf16[144,2304]{1,0:T(8,128)(2,1)S(1)} collective-permute-done((bf16[144,2304]{1,0:T(8,128)(2,1)S(1)}, bf16[144,2304]{1,0:T(8,128)(2,1)S(1)}, u32[]{:S(2)}, u32[]{:S(2)}) %collective-permute-start.71) | collective-permute-done | bytes 663584 | tf_op jit(solution)/shard_map/ppermute | solution.py:398
  620.2 6.6 collective-permute-done.73.refs_6_
  636.2 7.3 %collective-permute-done.74.refs_1_ = bf16[128,2304]{1,0:T(8,128)(2,1)S(1)} collective-permute-done((bf16[128,2304]{1,0:T(8,128)(2,1)S(1)}, bf16[128,2304]{1,0:T(8,128)(2,1)S(1)}, u32[]{:S(2)}, u32[]{:S(2)}) %collective-permute-start.74) | collective-permute-done | bytes 589856 | tf_op jit(solution)/shard_map/ppermute | solution.py:398
  652.9 7.9 %finish.3 = f32[256,8192]{1,0:T(8,128)} custom-call(s32[1]{0:T(128)} %bitcast.33.at_end_ref.ends_ref, s32[8]{0:T(128)} %stack.32.order_ref, bf16[128,4096]{1,0:T(8,128)(2,1)} %copy-done.8, bf16[128,4096]{1,0:T(8,128)(2,1)} %get-tuple-element.370.refs_1_, bf16[128,4096]{1,0:T(8,128)(2,1)} %copy-done.4, bf16[128,4096]{1,0:T(8,128)(2,1)} %get-tuple-element.372.refs_3_, ...), custom_call_target="tpu_custom_call" | custom-call | tf_op jit(solution)/shard_map/finish/pallas_call | solution.py:167
  667.3 10.0 %collective-permute-done.79 = bf16[128,2304]{1,0:T(8,128)(2,1)S(1)} collective-permute-done((bf16[128,2304]{1,0:T(8,128)(2,1)S(1)}, bf16[128,2304]{1,0:T(8,128)(2,1)S(1)}, u32[]{:S(2)}, u32[]{:S(2)}) %collective-permute-start.79) | collective-permute-done | bytes 589856 | tf_op jit(solution)/shard_map/ppermute | solution.py:400
  (491 shorter events, 338.1 us)
Async XLA Ops:
  7.2 76.4 %all-gather.3.cloned.1.call-start = ((), (), s32[]{:S(2)}) async-start(), calls=%async_computation.4 | async-start | bytes 10616832 | tf_op jit(solution)/shard_map/all_gather | solution.py:277
  9.7 216.7 %all-gather.5.cloned.1.call-start = ((), (), s32[]{:S(2)}) async-start(), calls=%async_computation.5 | async-start | bytes 9437184 | tf_op jit(solution)/shard_map/all_gather | solution.py:277
  48.6 27.1 %collective-permute-start.10 = (bf16[8,64,1024]{2,1,0:T(8,128)(2,1)S(1)}, bf16[8,64,1024]{2,1,0:T(8,128)(2,1)}, u32[]{:S(2)}, u32[]{:S(2)}) collective-permute-start(bf16[8,64,1024]{2,1,0:T(8,128)(2,1)S(1)} %bitcast_dynamic-update-slice_fusion.4), channel_id=1, source_target_pairs={{0,8},{8,16},{16,24},{24,0},{1,9},{9,17},{17,25},{25,1},{2,10},{10... | collective-permute-start | bytes 3145736 | tf_op jit(solution)/shard_map/ppermute | solution.py:329
  83.6 314.1 %reduce-scatter.5.cloned.1.call-start = ((), (), s32[]{:S(2)}) async-start(), calls=%async_computation.6 | async-start | bytes 9437184 | tf_op jit(solution)/shard_map/reduce_scatter | solution.py:288
  87.3 36.9 %collective-permute-start.14 = (bf16[256,2048]{1,0:T(8,128)(2,1)}, bf16[256,2048]{1,0:T(8,128)(2,1)}, u32[]{:S(2)}, u32[]{:S(2)}) collective-permute-start(bf16[256,2048]{1,0:T(8,128)(2,1)} %own_ref), channel_id=1, source_target_pairs={{0,2},{1,3},{2,0},{3,1},{4,6},{5,7},{6,4},{7,5},{8,10},{9,11},{10,... | collective-permute-start | bytes 3145736 | tf_op jit(solution)/shard_map/ppermute | solution.py:224
  88.8 36.6 %collective-permute-start.15 = (bf16[256,2048]{1,0:T(8,128)(2,1)}, bf16[256,2048]{1,0:T(8,128)(2,1)}, u32[]{:S(2)}, u32[]{:S(2)}) collective-permute-start(bf16[256,2048]{1,0:T(8,128)(2,1)} %own_ref), channel_id=1, source_target_pairs={{0,4},{1,5},{2,6},{3,7},{4,0},{5,1},{6,2},{7,3},{8,12},{9,13},{10,... | collective-permute-start | bytes 3145736 | tf_op jit(solution)/shard_map/ppermute | solution.py:224
  104.2 28.3 %collective-permute-start.16 = (bf16[256,2048]{1,0:T(8,128)(2,1)}, bf16[256,2048]{1,0:T(8,128)(2,1)S(1)}, u32[]{:S(2)}, u32[]{:S(2)}) collective-permute-start(bf16[256,2048]{1,0:T(8,128)(2,1)} %own_ref), channel_id=1, source_target_pairs={{0,1},{1,0},{2,3},{3,2},{4,5},{5,4},{6,7},{7,6},{8,9},{9,8},{10,11... | collective-permute-start | bytes 3145736 | tf_op jit(solution)/shard_map/ppermute | solution.py:224
  125.4 31.7 %collective-permute-start.17 = (bf16[256,2048]{1,0:T(8,128)(2,1)}, bf16[256,2048]{1,0:T(8,128)(2,1)}, u32[]{:S(2)}, u32[]{:S(2)}) collective-permute-start(bf16[256,2048]{1,0:T(8,128)(2,1)} %collective-permute-done.14), channel_id=1, source_target_pairs={{0,1},{1,0},{2,3},{3,2},{4,5},{5,4},{6,7},{7,6},{8,9},{9,8},{10,11... | collective-permute-start | bytes 3145736 | tf_op jit(solution)/shard_map/ppermute | solution.py:224
  127.3 32.1 %collective-permute-start.18 = (bf16[256,2048]{1,0:T(8,128)(2,1)}, bf16[256,2048]{1,0:T(8,128)(2,1)}, u32[]{:S(2)}, u32[]{:S(2)}) collective-permute-start(bf16[256,2048]{1,0:T(8,128)(2,1)} %collective-permute-done.15), channel_id=1, source_target_pairs={{0,1},{1,0},{2,3},{3,2},{4,5},{5,4},{6,7},{7,6},{8,9},{9,8},{10,11... | collective-permute-start | bytes 3145736 | tf_op jit(solution)/shard_map/ppermute | solution.py:224
  129.7 26.9 %collective-permute-start.19 = (bf16[128,2048]{1,0:T(8,128)(2,1)}, bf16[128,2048]{1,0:T(8,128)(2,1)}, u32[]{:S(2)}, u32[]{:S(2)}) collective-permute-start(bf16[128,2048]{1,0:T(8,128)(2,1)} %slice.218), channel_id=1, source_target_pairs={{0,4},{1,5},{2,6},{3,7},{4,0},{5,1},{6,2},{7,3},{8,12},{9,13},{10,... | collective-permute-start | bytes 1572872 | tf_op jit(solution)/shard_map/ppermute | solution.py:224
  130.4 26.2 %collective-permute-start.20 = (bf16[128,2048]{1,0:T(8,128)(2,1)}, bf16[128,2048]{1,0:T(8,128)(2,1)}, u32[]{:S(2)}, u32[]{:S(2)}) collective-permute-start(bf16[128,2048]{1,0:T(8,128)(2,1)} %slice.219), channel_id=1, source_target_pairs={{0,2},{1,3},{2,0},{3,1},{4,6},{5,7},{6,4},{7,5},{8,10},{9,11},{10,... | collective-permute-start | bytes 1572872 | tf_op jit(solution)/shard_map/ppermute | solution.py:224
  132.5 43.8 %collective-permute-start.23 = (bf16[8,64,1024]{2,1,0:T(8,128)(2,1)}, bf16[8,64,1024]{2,1,0:T(8,128)(2,1)S(1)}, u32[]{:S(2)}, u32[]{:S(2)}) collective-permute-start(bf16[8,64,1024]{2,1,0:T(8,128)(2,1)} %collective-permute-done.10), channel_id=1, source_target_pairs={{0,8},{8,16},{16,24},{24,0},{1,9},{9,17},{17,25},{25,1},{2,10},{10... | collective-permute-start | bytes 3145736 | tf_op jit(solution)/shard_map/ppermute | solution.py:329
  177.3 25.2 %collective-permute-start.24 = (bf16[256,2048]{1,0:T(8,128)(2,1)S(1)}, bf16[256,2048]{1,0:T(8,128)(2,1)}, u32[]{:S(2)}, u32[]{:S(2)}) collective-permute-start(bf16[256,2048]{1,0:T(8,128)(2,1)S(1)} %get-tuple-element.216.own_ref), channel_id=1, source_target_pairs={{0,2},{1,3},{2,0},{3,1},{4,6},{5,7},{6,4},{7,5},{8,10},{9,11},{10,... | collective-permute-start | bytes 3145736 | tf_op jit(solution)/shard_map/ppermute | solution.py:224
  178.3 24.9 %collective-permute-start.25 = (bf16[256,2048]{1,0:T(8,128)(2,1)S(1)}, bf16[256,2048]{1,0:T(8,128)(2,1)S(1)}, u32[]{:S(2)}, u32[]{:S(2)}) collective-permute-start(bf16[256,2048]{1,0:T(8,128)(2,1)S(1)} %get-tuple-element.216.own_ref), channel_id=1, source_target_pairs={{0,4},{1,5},{2,6},{3,7},{4,0},{5,1},{6,2},{7,3},{8,12},{9,13},{10,... | collective-permute-start | bytes 3145736 | tf_op jit(solution)/shard_map/ppermute | solution.py:224
  179.6 27.7 %collective-permute-start.26 = (bf16[256,2048]{1,0:T(8,128)(2,1)S(1)}, bf16[256,2048]{1,0:T(8,128)(2,1)}, u32[]{:S(2)}, u32[]{:S(2)}) collective-permute-start(bf16[256,2048]{1,0:T(8,128)(2,1)S(1)} %get-tuple-element.216.own_ref), channel_id=1, source_target_pairs={{0,1},{1,0},{2,3},{3,2},{4,5},{5,4},{6,7},{7,6},{8,9},{9,8},{10,11... | collective-permute-start | bytes 3145736 | tf_op jit(solution)/shard_map/ppermute | solution.py:224
  180.2 33.5 %collective-permute-start.33 = (bf16[8,64,1024]{2,1,0:T(8,128)(2,1)}, bf16[8,64,1024]{2,1,0:T(8,128)(2,1)S(1)}, u32[]{:S(2)}, u32[]{:S(2)}) collective-permute-start(bf16[8,64,1024]{2,1,0:T(8,128)(2,1)} %copy-done.32), channel_id=1, source_target_pairs={{0,8},{8,16},{16,24},{24,0},{1,9},{9,17},{17,25},{25,1},{2,10},{10... | collective-permute-start | bytes 3145736 | tf_op jit(solution)/shard_map/ppermute | solution.py:329
  247.2 26.8 %collective-permute-start.34 = (bf16[256,2048]{1,0:T(8,128)(2,1)}, bf16[256,2048]{1,0:T(8,128)(2,1)S(1)}, u32[]{:S(2)}, u32[]{:S(2)}) collective-permute-start(bf16[256,2048]{1,0:T(8,128)(2,1)} %matmul_tn.5.refs_0_), channel_id=1, source_target_pairs={{0,8},{24,16},{1,9},{25,17},{2,10},{26,18},{3,11},{27,19},{4,12},{... | collective-permute-start | bytes 3145736 | tf_op jit(solution)/shard_map/ppermute | solution.py:398
  287.6 283.7 %reduce-scatter.9.cloned.1.call-start = ((), (), s32[]{:S(2)}) async-start(), calls=%async_computation.8 | async-start | bytes 9437184 | tf_op jit(solution)/shard_map/reduce_scatter | solution.py:288
  288.8 28.1 %collective-permute-start.35 = (bf16[256,2048]{1,0:T(8,128)(2,1)S(1)}, bf16[256,2048]{1,0:T(8,128)(2,1)S(1)}, u32[]{:S(2)}, u32[]{:S(2)}) collective-permute-start(bf16[256,2048]{1,0:T(8,128)(2,1)S(1)} %copy-done.10), channel_id=1, source_target_pairs={{0,8},{24,16},{1,9},{25,17},{2,10},{26,18},{3,11},{27,19},{4,12},{... | collective-permute-start | bytes 3145736 | tf_op jit(solution)/shard_map/ppermute | solution.py:398
  318.7 24.6 %collective-permute-start.37 = (bf16[256,2048]{1,0:T(8,128)(2,1)S(1)}, bf16[256,2048]{1,0:T(8,128)(2,1)S(1)}, u32[]{:S(2)}, u32[]{:S(2)}) collective-permute-start(bf16[256,2048]{1,0:T(8,128)(2,1)S(1)} %get-tuple-element.344.refs_1_), channel_id=1, source_target_pairs={{0,8},{24,16},{8,0},{16,24},{1,9},{25,17},{9,1},{17,25},{2,10},{26... | collective-permute-start | bytes 3145736 | tf_op jit(solution)/shard_map/ppermute | solution.py:395
  323.0 25.1 %collective-permute-start.41 = (bf16[128,1024]{1,0:T(8,128)(2,1)S(1)}, bf16[128,1024]{1,0:T(8,128)(2,1)S(1)}, u32[]{:S(2)}, u32[]{:S(2)}) collective-permute-start(bf16[128,1024]{1,0:T(8,128)(2,1)S(1)} %get-tuple-element.396), channel_id=1, source_target_pairs={{0,3},{1,2},{2,1},{3,0},{4,7},{5,6},{6,5},{7,4},{8,11},{9,10},{10,... | collective-permute-start | bytes 786440 | tf_op jit(solution)/shard_map/ppermute | solution.py:224
  360.3 25.1 %collective-permute-start.46 = (bf16[256,2048]{1,0:T(8,128)(2,1)S(1)}, bf16[256,2048]{1,0:T(8,128)(2,1)S(1)}, u32[]{:S(2)}, u32[]{:S(2)}) collective-permute-start(bf16[256,2048]{1,0:T(8,128)(2,1)S(1)} %get-tuple-element.346.refs_3_), channel_id=1, source_target_pairs={{0,8},{24,16},{8,0},{16,24},{1,9},{25,17},{9,1},{17,25},{2,10},{26... | collective-permute-start | bytes 3145736 | tf_op jit(solution)/shard_map/ppermute | solution.py:395
  397.7 34.0 %collective-permute-start.56 = (bf16[256,2048]{1,0:T(8,128)(2,1)}, bf16[256,2048]{1,0:T(8,128)(2,1)}, u32[]{:S(2)}, u32[]{:S(2)}) collective-permute-start(bf16[256,2048]{1,0:T(8,128)(2,1)} %copy-done.15), channel_id=1, source_target_pairs={{8,16},{16,8},{9,17},{17,9},{10,18},{18,10},{11,19},{19,11},{12,20... | collective-permute-start | bytes 3145736 | tf_op jit(solution)/shard_map/ppermute | solution.py:404
  399.3 33.9 %collective-permute-start.55 = (bf16[128,4096]{1,0:T(8,128)(2,1)S(1)}, bf16[128,4096]{1,0:T(8,128)(2,1)}, u32[]{:S(2)}, u32[]{:S(2)}) collective-permute-start(bf16[128,4096]{1,0:T(8,128)(2,1)S(1)} %pad_maximum_fusion.1.refs_0_), channel_id=1, source_target_pairs={{0,8},{24,16},{1,9},{25,17},{2,10},{26,18},{3,11},{27,19},{4,12},{... | collective-permute-start | bytes 3145736 | tf_op jit(solution)/shard_map/ppermute | solution.py:398
  406.0 29.9 %collective-permute-start.57 = (bf16[256,2048]{1,0:T(8,128)(2,1)S(1)}, bf16[256,2048]{1,0:T(8,128)(2,1)}, u32[]{:S(2)}, u32[]{:S(2)}) collective-permute-start(bf16[256,2048]{1,0:T(8,128)(2,1)S(1)} %get-tuple-element.348.refs_5_), channel_id=1, source_target_pairs={{8,0},{16,24},{9,1},{17,25},{10,2},{18,26},{11,3},{19,27},{12,4},{... | collective-permute-start | bytes 3145736 | tf_op jit(solution)/shard_map/ppermute | solution.py:400
  436.0 163.3 %reduce-scatter.7.cloned.1.call-start = ((), (), s32[]{:S(2)}) async-start(), calls=%async_computation.7 | async-start | bytes 11280384 | tf_op jit(solution)/shard_map/reduce_scatter | solution.py:288
  439.5 29.2 %collective-permute-start.58 = (bf16[128,4096]{1,0:T(8,128)(2,1)}, bf16[128,4096]{1,0:T(8,128)(2,1)S(1)}, u32[]{:S(2)}, u32[]{:S(2)}) collective-permute-start(bf16[128,4096]{1,0:T(8,128)(2,1)} %pad_maximum_fusion.2.refs_0_), channel_id=1, source_target_pairs={{0,8},{24,16},{1,9},{25,17},{2,10},{26,18},{3,11},{27,19},{4,12},{... | collective-permute-start | bytes 3145736 | tf_op jit(solution)/shard_map/ppermute | solution.py:398
  446.7 27.0 %collective-permute-start.60 = (bf16[256,2048]{1,0:T(8,128)(2,1)S(1)}, bf16[256,2048]{1,0:T(8,128)(2,1)}, u32[]{:S(2)}, u32[]{:S(2)}) collective-permute-start(bf16[256,2048]{1,0:T(8,128)(2,1)S(1)} %tick.21.refs_7_), channel_id=1, source_target_pairs={{8,0},{16,24},{9,1},{17,25},{10,2},{18,26},{11,3},{19,27},{12,4},{... | collective-permute-start | bytes 3145736 | tf_op jit(solution)/shard_map/ppermute | solution.py:400
  516.0 165.5 %reduce-scatter.11.cloned.1.call-start = ((), (), s32[]{:S(2)}) async-start(), calls=%async_computation.9 | async-start | bytes 9437184 | tf_op jit(solution)/shard_map/reduce_scatter | solution.py:288
  516.0 24.3 %collective-permute-start.64 = (bf16[128,4096]{1,0:T(8,128)(2,1)}, bf16[128,4096]{1,0:T(8,128)(2,1)S(1)}, u32[]{:S(2)}, u32[]{:S(2)}) collective-permute-start(bf16[128,4096]{1,0:T(8,128)(2,1)} %get-tuple-element.370.refs_1_), channel_id=1, source_target_pairs={{0,8},{24,16},{8,0},{16,24},{1,9},{25,17},{9,1},{17,25},{2,10},{26... | collective-permute-start | bytes 3145736 | tf_op jit(solution)/shard_map/ppermute | solution.py:395
  543.5 24.5 %collective-permute-start.66 = (bf16[128,4096]{1,0:T(8,128)(2,1)}, bf16[128,4096]{1,0:T(8,128)(2,1)S(1)}, u32[]{:S(2)}, u32[]{:S(2)}) collective-permute-start(bf16[128,4096]{1,0:T(8,128)(2,1)} %get-tuple-element.372.refs_3_), channel_id=1, source_target_pairs={{0,8},{24,16},{8,0},{16,24},{1,9},{25,17},{9,1},{17,25},{2,10},{26... | collective-permute-start | bytes 3145736 | tf_op jit(solution)/shard_map/ppermute | solution.py:395
  572.2 26.9 %collective-permute-start.68 = (bf16[256,2048]{1,0:T(8,128)(2,1)}, bf16[256,2048]{1,0:T(8,128)(2,1)S(1)}, u32[]{:S(2)}, u32[]{:S(2)}) collective-permute-start(bf16[256,2048]{1,0:T(8,128)(2,1)} %reduce-scatter.9.cloned.1.call-done.refs_0_), channel_id=1, source_target_pairs={{0,8},{24,16},{1,9},{25,17},{2,10},{26,18},{3,11},{27,19},{4,12},{... | collective-permute-start | bytes 3145736 | tf_op jit(solution)/shard_map/ppermute | solution.py:398
  (128 other events, 1659.3 us)
Sparse Core Ops, SparseCore 0:
  10.5 73.0 all-gather.2
  85.5 76.9 all-gather.4
  287.8 89.2 reduce-scatter.4
  436.2 70.8 reduce-scatter.8
  516.1 75.5 reduce-scatter.6
  603.4 69.0 reduce-scatter.10
